TPU v7x, 128 devices: a whole 4x4x4 slice. The times are simulated.
128 devices in a mesh: section: 2 (over y_hi), wide: 16 (over x, y_lo, core), tp: 4 (over z).
Axes of the slice: x: 4, y: 4 (y_hi: 2, y_lo: 2; y = y_hi * 2 + y_lo), z: 4, core: 2. Of those that a mesh axis runs over, the one named last changes fastest.
Arguments:
- block_input: bfloat16 [2, 2048, 2048], P(None, ('wide', 'tp')), may hold values from -6 to 6
- out_grad: bfloat16 [2, 2048, 2048], P(None, ('wide', 'tp')), may hold values from -6 to 6
- seg_ids: int32 [2, 2048], replicated, may hold values from 0 to 9, as said below
- attn_gain: bfloat16 [2, 2048], P('section', 'wide'), may hold values from 0.5 to 1.5
- w_query: bfloat16 [2, 2048, 2048], P('section', 'wide', 'tp'), may hold values from -0.125 to 0.125
- w_key: bfloat16 [2, 2048, 256], P('section', 'wide', 'tp'), may hold values from -0.125 to 0.125
- w_value: bfloat16 [2, 2048, 256], P('section', 'wide', 'tp'), may hold values from -0.125 to 0.125
- w_out: bfloat16 [2, 2048, 2048], P('section', 'tp', 'wide'), may hold values from -2 to 2
- ffn_gain: bfloat16 [2, 2048], P('section', 'wide'), may hold values from 0.5 to 1.5
- w_gate: bfloat16 [2, 2048, 5632], P('section', 'wide', 'tp'), may hold values from -0.125 to 0.125
- w_up: bfloat16 [2, 2048, 5632], P('section', 'wide', 'tp'), may hold values from -0.125 to 0.125
- w_down: bfloat16 [2, 5632, 2048], P('section', 'tp', 'wide'), may hold values from -0.078125 to 0.078125
Outputs:
- block_output: bfloat16 [2, 2, 2048, 2048], P('section', None, ('wide', 'tp'))
- input_grad: float32 [2, 2, 2048, 2048], P('section', None, ('wide', 'tp'))
- grad_attn_gain: float32 [2, 2048], P('section', ('wide', 'tp'))
- grad_query: float32 [2, 2048, 2048], P('section', 'wide', 'tp')
- grad_key: float32 [2, 2048, 256], P('section', 'wide', 'tp')
- grad_value: float32 [2, 2048, 256], P('section', 'wide', 'tp')
- grad_out: float32 [2, 2048, 2048], P('section', 'tp', 'wide')
- grad_ffn_gain: float32 [2, 2048], P('section', ('wide', 'tp'))
- grad_gate: float32 [2, 2048, 5632], P('section', 'wide', 'tp')
- grad_up: float32 [2, 2048, 5632], P('section', 'wide', 'tp')
- grad_down: float32 [2, 5632, 2048], P('section', 'tp', 'wide')
Inputs may be any that keep to these rules, and one draw needn't show every extreme that they name: `seg_ids`: in every micro-batch the document numbers start at 0, never fall along the sequence and rise by one at each new document; every document holds 102 to 2048 positions; in one micro-batch the whole sequence is a single document, and in another one there are ten documents.
All inputs are finite; a program needn't handle non-finite values.
Results may differ from a plain program's by a relative error of at most 0.035.
Values may be sent and summed in bfloat16 or wider, within the bound.
No kernel may reach another device: no remote copies, remote signals or barrier semaphores. Data moves between devices by JAX's collectives and lax.ppermute only.
A program may use at most 256 MiB of HBM per device.

v0:
```python
import math

import jax
import jax.numpy as jnp
from jax import lax
from jax.sharding import PartitionSpec as P

HD = 64


epsilon = 1e-05
masked_score = -1e30


def joined_along(blocks, dim):
    blocks = jnp.moveaxis(blocks, 0, dim)
    shape = blocks.shape
    return blocks.reshape(*shape[:dim], shape[dim] * shape[dim + 1], *shape[dim + 2 :])


def copy_for_each(array, axis):
    peers = lax.axis_size(axis)
    return lax.all_to_all(
        jnp.broadcast_to(array[None], (peers, *array.shape)), axis, 0, 0, tiled=True
    )


def gathered_copies(array, axis, dim):
    return joined_along(copy_for_each(array, axis), dim)


def in_blocks(array, dim, peers):
    before, after = (array.shape[:dim], array.shape[dim + 1 :])
    return jnp.moveaxis(array.reshape(*before, peers, -1, *after), dim, 0)


def summed_on_arrival(array, axis, dim):
    peers = lax.axis_size(axis)
    blocks = lax.all_to_all(in_blocks(array, dim, peers), axis, 0, 0, tiled=True)
    return jnp.sum(blocks.astype(jnp.float32), axis=0)


def turned_gather(arrays, axis, dims):
    turned = [jnp.moveaxis(a, dim, 0) for a, dim in zip(arrays, dims)]
    widths = [t[0].size for t in turned]
    both = jnp.concatenate([t.reshape(-1, w) for t, w in zip(turned, widths)], axis=1)
    whole = lax.all_gather(both, axis, axis=0, tiled=True)
    blocks = jnp.split(whole, [sum(widths[:k]) for k in range(1, len(widths))], axis=1)
    return tuple(
        (
            jnp.moveaxis(b.reshape(-1, *t.shape[1:]), 0, dim)
            for b, t, dim in zip(blocks, turned, dims)
        )
    )


def passed_along(array, axis, by):
    peers = lax.axis_size(axis)
    pairs = [(i, i + by) for i in range(peers) if 0 <= i + by < peers]
    return lax.ppermute(array, axis, pairs)


def side_by_side(arrays, axis, dim, along):
    both = jnp.concatenate(arrays, axis=along)
    whole, at, finished = (lax.psum_scatter(both, axis, scatter_dimension=dim, tiled=True), 0, [])
    for a in arrays:
        finished.append(lax.slice_in_dim(whole, at, at + a.shape[along], axis=along))
        at += a.shape[along]
    return tuple(finished)


def sent_and_summed(array, axis, dim):
    blocks = in_blocks(array, dim, lax.axis_size(axis))
    arrived = lax.all_to_all(blocks, axis, split_axis=0, concat_axis=0, tiled=True)
    return arrived.sum(axis=0)


def rotate(values):
    half_width = values.shape[-1] // 2
    return jnp.concatenate([-values[..., half_width:], values[..., :half_width]], axis=-1)


def rotary(values, cosine, sine_table):
    return values * cosine + rotate(values) * sine_table


def normalize(residual, gain_vector):
    return (
        residual
        * lax.rsqrt(jnp.mean(residual * residual, axis=-1, keepdims=True) + epsilon)
        * gain_vector
    )


def swish_gate(gate_values, up_values):
    return gate_values / (1.0 + jnp.exp(-gate_values)) * up_values


def plain_dot(former, latter):
    return jnp.dot(former, latter, preferred_element_type=jnp.float32)


def dot_against(former, latter):
    return lax.dot_general(
        former, latter, (((1,), (1,)), ((), ())), preferred_element_type=jnp.float32
    )


def dot_leading(former, latter):
    return lax.dot_general(
        former, latter, (((0,), (0,)), ((), ())), preferred_element_type=jnp.float32
    )


def seq_gather(local_rows):
    return gathered_copies(local_rows, "tp", 0)


def seq_reduce(partial_rows):
    return summed_on_arrival(partial_rows.astype(jnp.bfloat16), "tp", 0)


def attention_scores(query_heads, keys_all, allowed):
    score_scale = 1.0 / math.sqrt(HD)
    scores = (
        jnp.einsum("qgjd,kgd->gjqk", query_heads, keys_all, preferred_element_type=jnp.float32)
        * score_scale
    )
    return jnp.where(allowed, scores, masked_score)


def forward_layer(residual, weights, allowed, tables):
    (
        gain_attn,
        query_weight,
        key_weight,
        value_weight,
        out_weight,
        gain_ffn,
        gate_weight,
        up_weight,
        down_weight,
    ) = weights
    cosine, sine_table = tables
    normed = normalize(residual, gain_attn.astype(jnp.float32)).astype(jnp.bfloat16)
    rows_attn = seq_gather(normed)
    row_count = rows_attn.shape[0]
    head_count = query_weight.shape[1] // HD
    key_heads = key_weight.shape[1] // HD
    group_size = head_count // key_heads
    key_width = key_heads * HD
    query_pre = plain_dot(rows_attn, query_weight).reshape(row_count, head_count, HD)
    key_pre = plain_dot(rows_attn, key_weight).reshape(row_count, key_heads, HD)
    value_pre = plain_dot(rows_attn, value_weight)
    query_rot = rotary(query_pre, cosine, sine_table).astype(jnp.bfloat16)
    key_rot = rotary(key_pre, cosine, sine_table).astype(jnp.bfloat16).reshape(row_count, key_width)
    pair_local = jnp.concatenate([key_rot, value_pre.astype(jnp.bfloat16)], axis=1)
    pair_all = gathered_copies(pair_local, "wide", 0)
    keys_all = pair_all[:, :key_width].reshape(-1, key_heads, HD)
    values_all = pair_all[:, key_width:].reshape(-1, key_heads, HD)
    query_heads = query_rot.reshape(row_count, key_heads, group_size, HD)
    scores = attention_scores(query_heads, keys_all, allowed)
    row_max = jnp.max(scores, axis=-1, keepdims=True)
    raised = jnp.exp(scores - row_max)
    totals = jnp.sum(raised, axis=-1, keepdims=True)
    softmax_probs = (raised / totals).astype(jnp.bfloat16)
    log_total = row_max + jnp.log(totals)
    context = jnp.einsum(
        "gjqk,kgd->qgjd", softmax_probs, values_all, preferred_element_type=jnp.float32
    )
    context = context.reshape(row_count, head_count * HD).astype(jnp.bfloat16)
    middle = residual + seq_reduce(plain_dot(context, out_weight))
    normed_ffn = normalize(middle, gain_ffn.astype(jnp.float32)).astype(jnp.bfloat16)
    rows_ffn = seq_gather(normed_ffn)
    gate_values = plain_dot(rows_ffn, gate_weight)
    up_values = plain_dot(rows_ffn, up_weight)
    hidden = swish_gate(gate_values, up_values).astype(jnp.bfloat16)
    result = middle + seq_reduce(plain_dot(hidden, down_weight))
    kept_state = (
        residual,
        middle,
        rows_attn,
        query_heads,
        keys_all,
        values_all,
        log_total,
        context,
        rows_ffn,
        gate_values,
        up_values,
        hidden,
    )
    return (result, kept_state)


def backward_layer(grad_residual, kept_state, weights, allowed, tables):
    (
        gain_attn,
        query_weight,
        key_weight,
        value_weight,
        out_weight,
        gain_ffn,
        gate_weight,
        up_weight,
        down_weight,
    ) = weights
    cosine, sine_table = tables
    (
        residual,
        middle,
        rows_attn,
        query_heads,
        keys_all,
        values_all,
        log_total,
        context,
        rows_ffn,
        gate_values,
        up_values,
        hidden,
    ) = kept_state
    score_scale = 1.0 / math.sqrt(HD)
    row_count = rows_attn.shape[0]
    head_count = query_weight.shape[1] // HD
    key_heads = key_weight.shape[1] // HD
    key_width = key_heads * HD
    grad_ffn_rows = seq_gather(grad_residual.astype(jnp.bfloat16))
    grad_down = dot_leading(hidden, grad_ffn_rows)
    grad_hidden = dot_against(grad_ffn_rows, down_weight)
    _, pull_swish = jax.vjp(swish_gate, gate_values, up_values)
    grad_gate_full, grad_up_full = pull_swish(grad_hidden)
    grad_gate_low = grad_gate_full.astype(jnp.bfloat16)
    grad_up_low = grad_up_full.astype(jnp.bfloat16)
    grad_gate = dot_leading(rows_ffn, grad_gate_low)
    grad_up = dot_leading(rows_ffn, grad_up_low)
    grad_normed_ffn = seq_reduce(
        dot_against(grad_gate_low, gate_weight) + dot_against(grad_up_low, up_weight)
    )
    _, pull_second = jax.vjp(normalize, middle, gain_ffn.astype(jnp.float32))
    grad_middle_norm, grad_gain_ffn = pull_second(grad_normed_ffn)
    grad_middle = grad_residual + grad_middle_norm
    grad_attn_rows = seq_gather(grad_middle.astype(jnp.bfloat16))
    grad_out = dot_leading(context, grad_attn_rows)
    grad_context = (
        dot_against(grad_attn_rows, out_weight).astype(jnp.bfloat16).reshape(query_heads.shape)
    )
    scores = attention_scores(query_heads, keys_all, allowed)
    softmax_probs = jnp.exp(scores - log_total)
    probs_low = softmax_probs.astype(jnp.bfloat16)
    grad_probs = jnp.einsum(
        "qgjd,kgd->gjqk", grad_context, values_all, preferred_element_type=jnp.float32
    )
    row_delta = jnp.sum(softmax_probs * grad_probs, axis=-1, keepdims=True)
    grad_scores = (softmax_probs * (grad_probs - row_delta)).astype(jnp.bfloat16)
    grad_query = (
        jnp.einsum("gjqk,kgd->qgjd", grad_scores, keys_all, preferred_element_type=jnp.float32)
        * score_scale
    )
    grad_keys = (
        jnp.einsum("gjqk,qgjd->kgd", grad_scores, query_heads, preferred_element_type=jnp.float32)
        * score_scale
    )
    grad_values = jnp.einsum(
        "gjqk,qgjd->kgd", probs_low, grad_context, preferred_element_type=jnp.float32
    )
    seq_total = keys_all.shape[0]
    grad_pair = jnp.concatenate(
        [grad_keys.reshape(seq_total, key_width), grad_values.reshape(seq_total, key_width)], axis=1
    )
    grad_pair_own = summed_on_arrival(grad_pair.astype(jnp.bfloat16), "wide", 0)
    grad_key_rot = grad_pair_own[:, :key_width].reshape(row_count, key_heads, HD)
    grad_value_low = grad_pair_own[:, key_width:].astype(jnp.bfloat16)
    grad_query_rot = grad_query.reshape(row_count, head_count, HD)
    _, pull_query = jax.vjp(lambda argument: rotary(argument, cosine, sine_table), grad_query_rot)
    grad_query_low = (
        pull_query(grad_query_rot)[0].reshape(row_count, head_count * HD).astype(jnp.bfloat16)
    )
    _, pull_key = jax.vjp(lambda argument: rotary(argument, cosine, sine_table), grad_key_rot)
    grad_key_low = pull_key(grad_key_rot)[0].reshape(row_count, key_width).astype(jnp.bfloat16)
    grad_query_weight = dot_leading(rows_attn, grad_query_low)
    grad_key_weight = dot_leading(rows_attn, grad_key_low)
    grad_value_weight = dot_leading(rows_attn, grad_value_low)
    grad_rows = (
        dot_against(grad_query_low, query_weight)
        + dot_against(grad_key_low, key_weight)
        + dot_against(grad_value_low, value_weight)
    )
    grad_normed = seq_reduce(grad_rows)
    _, pull_first = jax.vjp(normalize, residual, gain_attn.astype(jnp.float32))
    grad_residual_norm, grad_gain_attn = pull_first(grad_normed)
    grad_input = grad_middle + grad_residual_norm
    matrices = (
        grad_query_weight,
        grad_key_weight,
        grad_value_weight,
        grad_out,
        grad_gate,
        grad_up,
        grad_down,
    )
    return (grad_input, matrices, (grad_gain_attn, grad_gain_ffn))


def body(
    block_input,
    out_grad,
    seg_ids,
    attn_gain,
    w_query,
    w_key,
    w_value,
    w_out,
    ffn_gain,
    w_gate,
    w_up,
    w_down,
):
    section_index = lax.axis_index("section")
    micro_count = block_input.shape[0]
    local_rows = block_input.shape[1]
    model_width = block_input.shape[2]
    wide_rows = local_rows * lax.axis_size("tp")
    seq_total = seg_ids.shape[1]
    wide_start = lax.axis_index("wide") * wide_rows
    weights = turned_gather(
        (
            attn_gain[0],
            w_query[0],
            w_key[0],
            w_value[0],
            w_out[0],
            ffn_gain[0],
            w_gate[0],
            w_up[0],
            w_down[0],
        ),
        "wide",
        (0, 0, 0, 0, 1, 0, 0, 0, 1),
    )
    query_index = wide_start + jnp.arange(wide_rows, dtype=jnp.int32)
    key_index = jnp.arange(seq_total, dtype=jnp.int32)
    frequency = 10000.0 ** (-jnp.arange(0, HD, 2, dtype=jnp.float32) / HD)
    angles = query_index.astype(jnp.float32)[:, None] * frequency[None, :]
    angles = jnp.concatenate([angles, angles], axis=1)[:, None, :]
    tables = (jnp.cos(angles), jnp.sin(angles))
    causal = query_index[:, None] >= key_index[None, :]

    def allowed_for(batch_index):
        seg_row = lax.dynamic_index_in_dim(seg_ids, batch_index, 0, keepdims=False)
        seg_query = lax.dynamic_slice_in_dim(seg_row, wide_start, wide_rows)
        return causal & (seg_query[:, None] == seg_row[None, :])

    def forward_tick(received, tick_index):
        batch_index = jnp.clip(tick_index - section_index, 0, micro_count - 1)
        fresh_rows = lax.dynamic_index_in_dim(block_input, batch_index, 0, keepdims=False)
        residual = jnp.where(section_index == 0, fresh_rows, received).astype(jnp.float32)
        result, kept_state = forward_layer(residual, weights, allowed_for(batch_index), tables)
        result_low = result.astype(jnp.bfloat16)
        sent_rows = passed_along(result_low, "section", 1)
        return (sent_rows, (result_low, kept_state))

    start_value = jnp.zeros((local_rows, model_width), jnp.bfloat16)
    _, (outputs_all, kept_all) = lax.scan(forward_tick, start_value, jnp.arange(micro_count + 1))
    block_output = lax.dynamic_slice_in_dim(outputs_all, section_index, micro_count, 0)[None]
    back_weights = turned_gather(
        (
            attn_gain[0],
            w_query[0],
            w_key[0],
            w_value[0],
            w_out[0],
            ffn_gain[0],
            w_gate[0],
            w_up[0],
            w_down[0],
        ),
        "wide",
        (0, 0, 0, 0, 1, 0, 0, 0, 1),
    )
    matrix_zero = tuple(
        (
            jnp.zeros(gathered.shape, jnp.float32)
            for gathered in back_weights[1:5] + back_weights[6:9]
        )
    )
    gain_zero = (
        jnp.zeros(back_weights[0].shape, jnp.float32),
        jnp.zeros(back_weights[5].shape, jnp.float32),
    )

    def backward_tick(carry_state, tick_index):
        received, matrix_sums, gain_sums = carry_state
        raw_index = tick_index - 1 + section_index
        is_valid = (raw_index >= 0) & (raw_index < micro_count)
        batch_index = jnp.clip(raw_index, 0, micro_count - 1)
        given_grad = lax.dynamic_index_in_dim(out_grad, batch_index, 0, keepdims=False)
        grad_residual = jnp.where(section_index == 1, given_grad, received).astype(jnp.float32)
        kept_state = jax.tree.map(
            lambda stacked: lax.dynamic_index_in_dim(
                stacked, batch_index + section_index, 0, keepdims=False
            ),
            kept_all,
        )
        grad_input, matrices, gains = backward_layer(
            grad_residual, kept_state, back_weights, allowed_for(batch_index), tables
        )
        sent_rows = passed_along(grad_input.astype(jnp.bfloat16), "section", -1)
        matrices = tuple((jnp.where(is_valid, matrix, 0.0) for matrix in matrices))
        gains = tuple((jnp.where(is_valid, gain_term, 0.0) for gain_term in gains))
        matrix_sums = tuple((running + addend for running, addend in zip(matrix_sums, matrices)))
        gain_sums = tuple((running + addend for running, addend in zip(gain_sums, gains)))
        return ((sent_rows, matrix_sums, gain_sums), grad_input)

    (_, matrix_sums, gain_sums), grads_all = lax.scan(
        backward_tick, (start_value, matrix_zero, gain_zero), jnp.arange(micro_count + 1)
    )
    input_grad = lax.dynamic_slice_in_dim(grads_all, 1 - section_index, micro_count, 0)[None]
    matrix_parts = (
        *tuple(
            (
                part.astype(jnp.float32)
                for part in side_by_side(
                    (
                        matrix_sums[0].astype(jnp.bfloat16),
                        matrix_sums[1].astype(jnp.bfloat16),
                        matrix_sums[2].astype(jnp.bfloat16),
                    ),
                    "wide",
                    0,
                    1,
                )
            )
        ),
        lax.psum_scatter(
            matrix_sums[3].astype(jnp.bfloat16), "wide", scatter_dimension=1, tiled=True
        ).astype(jnp.float32),
        *tuple(
            (
                part.astype(jnp.float32)
                for part in side_by_side(
                    (matrix_sums[4].astype(jnp.bfloat16), matrix_sums[5].astype(jnp.bfloat16)),
                    "wide",
                    0,
                    1,
                )
            )
        ),
        lax.psum_scatter(
            matrix_sums[6].astype(jnp.bfloat16), "wide", scatter_dimension=1, tiled=True
        ).astype(jnp.float32),
    )
    gain_parts = (
        sent_and_summed(gain_sums[0], ("wide", "tp"), 0),
        sent_and_summed(gain_sums[1], ("wide", "tp"), 0),
    )
    return (
        block_output,
        input_grad,
        gain_parts[0][None],
        matrix_parts[0][None],
        matrix_parts[1][None],
        matrix_parts[2][None],
        matrix_parts[3][None],
        gain_parts[1][None],
        matrix_parts[4][None],
        matrix_parts[5][None],
        matrix_parts[6][None],
    )


def solution(mesh):
    placed = (
        P(None, ("wide", "tp"), None),
        P(None, ("wide", "tp"), None),
        P(),
        P("section", "wide"),
        P("section", "wide", "tp"),
        P("section", "wide", "tp"),
        P("section", "wide", "tp"),
        P("section", "tp", "wide"),
        P("section", "wide"),
        P("section", "wide", "tp"),
        P("section", "wide", "tp"),
        P("section", "tp", "wide"),
    )
    return jax.shard_map(
        body,
        mesh=mesh,
        in_specs=placed,
        out_specs=(
            P("section", None, ("wide", "tp"), None),
            P("section", None, ("wide", "tp"), None),
            P("section", ("wide", "tp")),
            P("section", "wide", "tp"),
            P("section", "wide", "tp"),
            P("section", "wide", "tp"),
            P("section", "tp", "wide"),
            P("section", ("wide", "tp")),
            P("section", "wide", "tp"),
            P("section", "wide", "tp"),
            P("section", "tp", "wide"),
        ),
        check_vma=False,
    )
```

profile of v0, /device:TPU:1, one launch (start us, length us, event | category | flops | bytes accessed | tf_op | source)
XLA Modules:
  0.0 1286.9 jit_solution(1500535717642667746)
XLA Ops:
  18.2 120.9 %all-gather.2.cloned.1.call-done = bf16[2048,5378]{1,0:T(8,128)(2,1)} async-done(((bf16[128,5378]{1,0:T(8,128)(2,1)}), bf16[2048,5378]{1,0:T(8,128)(2,1)}) %all-gather.2.cloned.1.call-update) | async-done | bytes 22028304 | tf_op jit(solution)/shard_map/all_gather | solution.py:47
  151.1 18.7 %slice_bitcast_fusion.1 = (bf16[1408,2048]{0,1:T(8,128)(2,1)}, bf16[2048,1408]{1,0:T(8,128)(2,1)}, bf16[2048,1408]{1,0:T(8,128)(2,1)}) fusion(bf16[2048,5378]{1,0:T(8,128)(2,1)} %all-gather.2.cloned.1.call-done), kind=kLoop, calls=%fused_computation.203 | loop fusion | bytes 34603008 | tf_op jit(solution)/shard_map/transpose | solution.py:51
  169.8 8.2 copy.105
  185.6 307.0 %while.74 = (s32[]{:T(128)}, bf16[32,2048]{1,0:T(8,128)(2,1)S(1)}, bf16[3,32,2048]{2,1,0:T(8,128)(2,1)}, f32[3,32,2048]{2,1,0:T(8,128)}, f32[3,32,2048]{2,1,0:T(...) while((s32[]{:T(128)}, bf16[32,2048]{1,0:T(8,128)(2,1)S(1)}, ...), condition=%wide.region_7.8_spmd.clone, body=%wide.region_0.7_spmd.clone.sunk | while | flops 3385859072 | bytes 97947824 | solution.py:364
  305.8 11.0 all-to-all-start.1
  409.3 11.0 all-to-all-start.1
  494.1 445.0 %while.75 = (s32[]{:T(128)}, bf16[32,2048]{1,0:T(8,128)(2,1)S(1)}, f32[2048,512]{1,0:T(8,128)}, f32[2048,64]{0,1:T(8,128)}, f32[2048,64]{0,1:T(8,128)}, /*index=...) while((s32[]{:T(128)}, bf16[32,2048]{1,0:T(8,128)(2,1)S(1)}, ...), condition=%wide.region_19.20_spmd.clone, body=%wide.region_8.19_spmd.clone.sunk | while | flops 7054761472 | bytes 304281312 | solution.py:415
  593.0 11.3 all-to-all-start.8
  680.9 10.4 select_add_fusion.18
  691.3 10.4 select_add_fusion.16
  707.2 10.6 select_add_fusion.17
  739.7 8.7 all-to-all-start.8
  827.8 10.4 select_add_fusion.18
  838.2 10.4 select_add_fusion.16
  854.2 10.6 select_add_fusion.17
  886.6 8.8 all-to-all-start.8
  949.4 7.8 convert_element_type.343
  957.2 8.3 copy.121
  970.5 7.3 convert_element_type.341
  977.9 7.9 pad_maximum_fusion.2
  987.1 8.8 all-to-all-start.10
  1018.6 51.5 %reduce-scatter.9.cloned.1.call-done = bf16[128,640]{1,0:T(8,128)(2,1)} async-done(((bf16[2048,640]{1,0:T(8,128)(2,1)}), bf16[128,640]{1,0:T(8,128)(2,1)}) %reduce-scatter.9.cloned.1.call-update) | async-done | bytes 163856 | tf_op jit(solution)/shard_map/reduce_scatter | solution.py:65
  1074.1 73.9 %reduce-scatter.15.cloned.1.call-done = bf16[128,1408]{1,0:T(8,128)(2,1)} async-done(((bf16[2048,1408]{1,0:T(8,128)(2,1)}), bf16[128,1408]{1,0:T(8,128)(2,1)}) %reduce-scatter.15.cloned.1.call-update) | async-done | bytes 360464
  1150.1 127.6 %reduce-scatter.11.cloned.1.call-done = bf16[128,2816]{1,0:T(8,128)(2,1)} async-done(((bf16[2048,2816]{1,0:T(8,128)(2,1)}), bf16[128,2816]{1,0:T(8,128)(2,1)}) %reduce-scatter.11.cloned.1.call-update) | async-done | bytes 720912 | tf_op jit(solution)/shard_map/reduce_scatter | solution.py:65
  (601 shorter events, 697.5 us)
Async XLA Ops:
  7.2 132.0 %all-gather.2.cloned.1.call-start = ((), (), s32[]{:S(2)}) async-start(), calls=%async_computation.16 | async-start | bytes 23953408 | tf_op jit(solution)/shard_map/all_gather | solution.py:47
  16.6 1000.2 %reduce-scatter.13.cloned.1.call-start = ((), (), s32[]{:S(2)}) async-start(), calls=%async_computation.19 | async-start | bytes 2228224
  191.1 13.2 %all-to-all-start = ((bf16[4,32,2048]{2,1,0:T(8,128)(2,1)}), bf16[4,32,2048]{2,1,0:T(8,128)(2,1)S(1)}, u32[]{:S(2)}, u32[]{:S(2)}) async-start(bf16[4,32,2048]{2,1,0:T(8,128)(2,1)} %broadcast_in_dim.474), calls=%async_computation | async-start | bytes 1048576 | tf_op jit(solution)/shard_map/while/body/eval_jaxpr/all_to_all | solution.py:23
  208.8 15.9 %all-to-all-start.1 = ((bf16[16,128,128]{1,2,0:T(8,128)(2,1)}), bf16[16,128,128]{1,2,0:T(8,128)(2,1)S(1)}, u32[]{:S(2)}, u32[]{:S(2)}) async-start(bf16[16,128,128]{1,2,0:T(8,128)(2,1)} %broadcast_in_dim.475), calls=%async_computation.1 | async-start | bytes 1048576 | tf_op jit(solution)/shard_map/while/body/eval_jaxpr/all_to_all | solution.py:23
  305.8 20.6 %all-to-all-start.1 = ((bf16[16,128,128]{1,2,0:T(8,128)(2,1)}), bf16[16,128,128]{1,2,0:T(8,128)(2,1)S(1)}, u32[]{:S(2)}, u32[]{:S(2)}) async-start(bf16[16,128,128]{1,2,0:T(8,128)(2,1)} %broadcast_in_dim.475), calls=%async_computation.1 | async-start | bytes 1048576 | tf_op jit(solution)/shard_map/while/body/eval_jaxpr/all_to_all | solution.py:23
  409.3 20.6 %all-to-all-start.1 = ((bf16[16,128,128]{1,2,0:T(8,128)(2,1)}), bf16[16,128,128]{1,2,0:T(8,128)(2,1)S(1)}, u32[]{:S(2)}, u32[]{:S(2)}) async-start(bf16[16,128,128]{1,2,0:T(8,128)(2,1)} %broadcast_in_dim.475), calls=%async_computation.1 | async-start | bytes 1048576 | tf_op jit(solution)/shard_map/while/body/eval_jaxpr/all_to_all | solution.py:23
  512.2 17.6 %all-to-all-start.5 = ((bf16[4,32,2048]{2,1,0:T(8,128)(2,1)}), bf16[4,32,2048]{2,1,0:T(8,128)(2,1)}, u32[]{:S(2)}, u32[]{:S(2)}) async-start(bf16[4,32,2048]{2,1,0:T(8,128)(2,1)} %broadcast_in_dim.484), calls=%async_computation.5 | async-start | bytes 1048576 | tf_op jit(solution)/shard_map/while/body/eval_jaxpr/all_to_all | solution.py:23
  540.3 18.2 %all-to-all-start.6 = ((bf16[4,32,2048]{2,1,0:T(8,128)(2,1)}), bf16[4,32,2048]{2,1,0:T(8,128)(2,1)S(1)}, u32[]{:S(2)}, u32[]{:S(2)}) async-start(bf16[4,32,2048]{2,1,0:T(8,128)(2,1)} %bitcast.654), calls=%async_computation.6 | async-start | bytes 1048576 | tf_op jit(solution)/shard_map/while/body/eval_jaxpr/all_to_all | solution.py:39
  593.0 21.7 %all-to-all-start.8 = ((bf16[16,128,128]{1,2,0:T(8,128)(2,1)}), bf16[16,128,128]{1,2,0:T(8,128)(2,1)S(1)}, u32[]{:S(2)}, u32[]{:S(2)}) async-start(bf16[16,128,128]{1,2,0:T(8,128)(2,1)} %pad_maximum_fusion.8), calls=%async_computation.8 | async-start | bytes 1048576 | tf_op jit(solution)/shard_map/while/body/eval_jaxpr/all_to_all | solution.py:39
  620.3 13.0 %all-to-all-start.9 = ((bf16[4,32,2048]{2,1,0:T(8,128)(2,1)}), bf16[4,32,2048]{2,1,0:T(8,128)(2,1)S(1)}, u32[]{:S(2)}, u32[]{:S(2)}) async-start(bf16[4,32,2048]{2,1,0:T(8,128)(2,1)} %bitcast.661), calls=%async_computation.9 | async-start | bytes 1048576 | tf_op jit(solution)/shard_map/while/body/eval_jaxpr/all_to_all | solution.py:39
  648.6 17.6 %all-to-all-start.5 = ((bf16[4,32,2048]{2,1,0:T(8,128)(2,1)}), bf16[4,32,2048]{2,1,0:T(8,128)(2,1)}, u32[]{:S(2)}, u32[]{:S(2)}) async-start(bf16[4,32,2048]{2,1,0:T(8,128)(2,1)} %broadcast_in_dim.484), calls=%async_computation.5 | async-start | bytes 1048576 | tf_op jit(solution)/shard_map/while/body/eval_jaxpr/all_to_all | solution.py:23
  676.7 25.0 %all-to-all-start.6 = ((bf16[4,32,2048]{2,1,0:T(8,128)(2,1)}), bf16[4,32,2048]{2,1,0:T(8,128)(2,1)S(1)}, u32[]{:S(2)}, u32[]{:S(2)}) async-start(bf16[4,32,2048]{2,1,0:T(8,128)(2,1)} %bitcast.654), calls=%async_computation.6 | async-start | bytes 1048576 | tf_op jit(solution)/shard_map/while/body/eval_jaxpr/all_to_all | solution.py:39
  703.0 14.8 %all-to-all-start.7 = ((bf16[4,32,2048]{2,1,0:T(8,128)(2,1)}), bf16[4,32,2048]{2,1,0:T(8,128)(2,1)S(1)}, u32[]{:S(2)}, u32[]{:S(2)}) async-start(bf16[4,32,2048]{2,1,0:T(8,128)(2,1)} %broadcast_in_dim.485), calls=%async_computation.7 | async-start | bytes 1048576 | tf_op jit(solution)/shard_map/while/body/eval_jaxpr/all_to_all | solution.py:23
  739.7 21.8 %all-to-all-start.8 = ((bf16[16,128,128]{1,2,0:T(8,128)(2,1)}), bf16[16,128,128]{1,2,0:T(8,128)(2,1)S(1)}, u32[]{:S(2)}, u32[]{:S(2)}) async-start(bf16[16,128,128]{1,2,0:T(8,128)(2,1)} %pad_maximum_fusion.8), calls=%async_computation.8 | async-start | bytes 1048576 | tf_op jit(solution)/shard_map/while/body/eval_jaxpr/all_to_all | solution.py:39
  767.1 13.8 %all-to-all-start.9 = ((bf16[4,32,2048]{2,1,0:T(8,128)(2,1)}), bf16[4,32,2048]{2,1,0:T(8,128)(2,1)S(1)}, u32[]{:S(2)}, u32[]{:S(2)}) async-start(bf16[4,32,2048]{2,1,0:T(8,128)(2,1)} %bitcast.661), calls=%async_computation.9 | async-start | bytes 1048576 | tf_op jit(solution)/shard_map/while/body/eval_jaxpr/all_to_all | solution.py:39
  795.6 17.6 %all-to-all-start.5 = ((bf16[4,32,2048]{2,1,0:T(8,128)(2,1)}), bf16[4,32,2048]{2,1,0:T(8,128)(2,1)}, u32[]{:S(2)}, u32[]{:S(2)}) async-start(bf16[4,32,2048]{2,1,0:T(8,128)(2,1)} %broadcast_in_dim.484), calls=%async_computation.5 | async-start | bytes 1048576 | tf_op jit(solution)/shard_map/while/body/eval_jaxpr/all_to_all | solution.py:23
  823.6 25.0 %all-to-all-start.6 = ((bf16[4,32,2048]{2,1,0:T(8,128)(2,1)}), bf16[4,32,2048]{2,1,0:T(8,128)(2,1)S(1)}, u32[]{:S(2)}, u32[]{:S(2)}) async-start(bf16[4,32,2048]{2,1,0:T(8,128)(2,1)} %bitcast.654), calls=%async_computation.6 | async-start | bytes 1048576 | tf_op jit(solution)/shard_map/while/body/eval_jaxpr/all_to_all | solution.py:39
  849.9 14.8 %all-to-all-start.7 = ((bf16[4,32,2048]{2,1,0:T(8,128)(2,1)}), bf16[4,32,2048]{2,1,0:T(8,128)(2,1)S(1)}, u32[]{:S(2)}, u32[]{:S(2)}) async-start(bf16[4,32,2048]{2,1,0:T(8,128)(2,1)} %broadcast_in_dim.485), calls=%async_computation.7 | async-start | bytes 1048576 | tf_op jit(solution)/shard_map/while/body/eval_jaxpr/all_to_all | solution.py:23
  886.6 21.9 %all-to-all-start.8 = ((bf16[16,128,128]{1,2,0:T(8,128)(2,1)}), bf16[16,128,128]{1,2,0:T(8,128)(2,1)S(1)}, u32[]{:S(2)}, u32[]{:S(2)}) async-start(bf16[16,128,128]{1,2,0:T(8,128)(2,1)} %pad_maximum_fusion.8), calls=%async_computation.8 | async-start | bytes 1048576 | tf_op jit(solution)/shard_map/while/body/eval_jaxpr/all_to_all | solution.py:39
  914.1 13.8 %all-to-all-start.9 = ((bf16[4,32,2048]{2,1,0:T(8,128)(2,1)}), bf16[4,32,2048]{2,1,0:T(8,128)(2,1)S(1)}, u32[]{:S(2)}, u32[]{:S(2)}) async-start(bf16[4,32,2048]{2,1,0:T(8,128)(2,1)} %bitcast.661), calls=%async_computation.9 | async-start | bytes 1048576 | tf_op jit(solution)/shard_map/while/body/eval_jaxpr/all_to_all | solution.py:39
  944.3 125.8 %reduce-scatter.9.cloned.1.call-start = ((), (), s32[]{:S(2)}) async-start(), calls=%async_computation.17 | async-start | bytes 2785280 | tf_op jit(solution)/shard_map/reduce_scatter | solution.py:65
  949.3 198.6 %reduce-scatter.15.cloned.1.call-start = ((), (), s32[]{:S(2)}) async-start(), calls=%async_computation.20 | async-start | bytes 6127616
  965.5 312.2 %reduce-scatter.11.cloned.1.call-start = ((), (), s32[]{:S(2)}) async-start(), calls=%async_computation.18 | async-start | bytes 12255232 | tf_op jit(solution)/shard_map/reduce_scatter | solution.py:65
  987.1 16.6 %all-to-all-start.10 = ((f32[64,1,32]{2,1,0:T(1,128)}), f32[64,1,32]{2,1,0:T(1,128)S(1)}, u32[]{:S(2)}, u32[]{:S(2)}) async-start(f32[64,1,32]{2,1,0:T(1,128)} %bitcast.16), calls=%async_computation.10 | async-start | bytes 65536 | tf_op jit(solution)/shard_map/all_to_all | solution.py:74
  (95 other events, 878.5 us)
Sparse Core Ops, SparseCore 0:
  16.8 122.3 all-gather.1
  944.4 60.0 reduce-scatter.12
  1006.9 63.1 reduce-scatter.8
  1072.4 75.5 reduce-scatter.14
  1150.2 127.4 reduce-scatter.10
where the time goes:
time: 1300 us; the launch traced here: 1290 us
  waiting for transfers between devices  499 us (38%)
  matrix products  305 us (23%)
  starting transfers between devices  186 us (14%)
  local copies, waits for them, and re-layouts  132 us (10%)
  other arithmetic  130 us (10%)
  loops' own time  20.3 us (2%)
  between operations  14.5 us (1%)
    reduce_scatter x2, waiting for transfers between devices, side_by_side(): lax.psum_scatter(both, axis, scatter_dimension=dim, tiled=True)  179 us
    dot_general x21, matrix products, dot_leading(): lax.dot_general(former, latter, (((0,), (0,)), ((), ())), preferred_eleme...  124 us
    all_gather x1, waiting for transfers between devices, turned_gather(): whole = lax.all_gather(both, axis, axis=0, tiled=True)  121 us
    all_to_all x15, starting transfers between devices, summed_on_arrival(): lax.all_to_all(in_blocks(array, dim, peers), axis, 0, 0, tiled=True)  77.3 us
    all_to_all x15, starting transfers between devices, copy_for_each(): lax.all_to_all(jnp.broadcast_to(array[None], (peers, *array.shape)), axis...  74.9 us
    unnamed x7, waiting for transfers between devices  74 us
    dot_general x21, matrix products, plain_dot(): return jnp.dot(former, latter, preferred_element_type=jnp.float32)  52.8 us
    dot_general x21, matrix products, dot_against(): lax.dot_general(former, latter, (((1,), (1,)), ((), ())), preferred_eleme...  50.2 us
  transfers between devices with their start and end apart: 43, of which 30 were waited for; matrix products, arithmetic and copies ran while one was open for 21% of the time, Pallas kernels for 0%

commit v1 on v0

v1 whole, which is shorter than its diff:
```python
import functools

import jax
import jax.numpy as jnp
from jax import lax
from jax.experimental import pallas as pl
from jax.experimental.pallas import tpu as pltpu
from jax.sharding import Mesh, PartitionSpec as P

HD = 64
EPS = 1e-05
MASKED = -1e30
KEYS_STEP = 512
AXES = ("section", "x", "ylo", "core", "tp")
BF16 = jnp.bfloat16
F32 = jnp.float32


def nn(a, b):
    return jnp.dot(a, b, preferred_element_type=F32)


def nt(a, b):
    return lax.dot_general(a, b, (((1,), (1,)), ((), ())), preferred_element_type=F32)


def tn(a, b):
    return lax.dot_general(a, b, (((0,), (0,)), ((), ())), preferred_element_type=F32)


def from_z(rows, by):
    return lax.ppermute(rows, "tp", [((i + by) % 4, i) for i in range(4)])


def swap_core(v):
    return lax.ppermute(v, "core", [(0, 1), (1, 0)])


def swap_ylo(v):
    return lax.ppermute(v, "ylo", [(0, 1), (1, 0)])


def swap_section(v):
    return lax.ppermute(v, "section", [(0, 1), (1, 0)])


def swap_across(v):
    return lax.ppermute(v, ("section", "ylo"), [(0, 3), (3, 0), (1, 2), (2, 1)])


def pick(first, a, b):
    return jnp.where(first, a, b)


def in_order(first, own, other, dim=0):
    return jnp.where(
        first,
        jnp.concatenate([own, other], axis=dim),
        jnp.concatenate([other, own], axis=dim),
    )


def gather_rows(rows):
    near = jnp.concatenate([rows] + [from_z(rows, k) for k in (1, 2, 3)], axis=0)
    return jnp.concatenate([near, swap_core(near)], axis=0)


def reduce_rows(partial):
    half = partial.shape[0] // 2
    step = half // 4
    mine = partial[:half] + swap_core(partial[half:].astype(BF16)).astype(F32)
    low = mine.astype(BF16)
    total = mine[:step]
    for k in (1, 2, 3):
        total = total + from_z(low[k * step : (k + 1) * step], -k).astype(F32)
    return total


def gather_kv(pair):
    copies = jnp.broadcast_to(pair[None], (8, *pair.shape))
    whole = lax.all_to_all(copies, ("x", "ylo"), 0, 0, tiled=True)
    return whole.reshape(-1, pair.shape[1])


def reduce_kv(partial):
    blocks = partial.reshape(8, -1, partial.shape[1])
    arrived = lax.all_to_all(blocks, ("x", "ylo"), 0, 0, tiled=True)
    return jnp.sum(arrived.astype(F32), axis=0)


def attend_kernel(q_ref, kv_ref, bias_ref, o_ref, lse_ref, s_ref):
    rows, width = q_ref.shape
    heads = width // HD
    keys = kv_ref.shape[0]
    steps = keys // KEYS_STEP
    tops = [jnp.full((1, rows), MASKED, F32) for _ in range(heads)]
    for t in range(steps):
        at = pl.ds(t * KEYS_STEP, KEYS_STEP)
        k = kv_ref[at, :HD]
        bias = bias_ref[at, :]
        for h in range(heads):
            s = nt(k, q_ref[:, h * HD : (h + 1) * HD]) + bias
            s_ref[h, at, :] = s
            tops[h] = jnp.maximum(tops[h], jnp.max(s, axis=0, keepdims=True))
    sums = [jnp.zeros((1, rows), F32) for _ in range(heads)]
    outs = [jnp.zeros((HD, rows), F32) for _ in range(heads)]
    for t in range(steps):
        at = pl.ds(t * KEYS_STEP, KEYS_STEP)
        v_t = kv_ref[at, :].T[HD:, :]
        for h in range(heads):
            e = jnp.exp(s_ref[h, at, :] - tops[h])
            sums[h] = sums[h] + jnp.sum(e, axis=0, keepdims=True)
            outs[h] = outs[h] + nn(v_t, e.astype(BF16))
    flat = jnp.concatenate([outs[h] / sums[h] for h in range(heads)], axis=0)
    o_ref[...] = flat.T.astype(BF16)
    lse_ref[...] = jnp.concatenate(
        [tops[h] + jnp.log(sums[h]) for h in range(heads)], axis=0
    )


def attend(q, kv, bias):
    rows, width = q.shape
    heads, keys = width // HD, kv.shape[0]
    work = heads * rows * keys
    return pl.pallas_call(
        attend_kernel,
        out_shape=(
            jax.ShapeDtypeStruct((rows, width), BF16),
            jax.ShapeDtypeStruct((heads, rows), F32),
        ),
        in_specs=[pl.BlockSpec(memory_space=pltpu.VMEM)] * 3,
        out_specs=(pl.BlockSpec(memory_space=pltpu.VMEM),) * 2,
        scratch_shapes=[pltpu.VMEM((heads, keys, rows), F32)],
        compiler_params=pltpu.CompilerParams(vmem_limit_bytes=40 * 1024 * 1024),
        cost_estimate=pl.CostEstimate(
            flops=4 * work * HD, bytes_accessed=4 * keys * rows, transcendentals=work
        ),
        name="attend",
    )(q, kv, bias)


def attend_back_kernel(q_ref, kv_ref, bias_ref, o_ref, do_ref, lse_ref, dq_ref, dkv_ref):
    rows, width = q_ref.shape
    heads = width // HD
    keys = kv_ref.shape[0]
    steps = keys // KEYS_STEP
    both = (do_ref[...].astype(F32) * o_ref[...].astype(F32)).T
    deltas = [
        jnp.sum(both[h * HD : (h + 1) * HD, :], axis=0, keepdims=True) for h in range(heads)
    ]
    dq_t = [jnp.zeros((HD, rows), F32) for _ in range(heads)]
    for t in range(steps):
        at = pl.ds(t * KEYS_STEP, KEYS_STEP)
        k = kv_ref[at, :HD]
        v = kv_ref[at, HD:]
        k_t = kv_ref[at, :].T[:HD, :]
        bias = bias_ref[at, :]
        dk = jnp.zeros((KEYS_STEP, HD), F32)
        dv = jnp.zeros((KEYS_STEP, HD), F32)
        for h in range(heads):
            q_h = q_ref[:, h * HD : (h + 1) * HD]
            do_h = do_ref[:, h * HD : (h + 1) * HD]
            p = jnp.exp(nt(k, q_h) + bias - lse_ref[h : h + 1, :])
            dp = nt(v, do_h)
            ds = (p * (dp - deltas[h])).astype(BF16)
            dv = dv + nn(p.astype(BF16), do_h)
            dk = dk + nn(ds, q_h)
            dq_t[h] = dq_t[h] + nn(k_t, ds)
        dkv_ref[at, :] = jnp.concatenate([dk, dv], axis=1).astype(BF16)
    dq_ref[...] = jnp.concatenate(dq_t, axis=0).T * (HD**-0.5)


def attend_back(q, kv, bias, o, do, lse):
    rows, width = q.shape
    heads, keys = width // HD, kv.shape[0]
    work = heads * rows * keys
    return pl.pallas_call(
        attend_back_kernel,
        out_shape=(
            jax.ShapeDtypeStruct((rows, width), F32),
            jax.ShapeDtypeStruct((keys, 2 * HD), BF16),
        ),
        in_specs=[pl.BlockSpec(memory_space=pltpu.VMEM)] * 6,
        out_specs=(pl.BlockSpec(memory_space=pltpu.VMEM),) * 2,
        compiler_params=pltpu.CompilerParams(vmem_limit_bytes=40 * 1024 * 1024),
        cost_estimate=pl.CostEstimate(
            flops=10 * work * HD, bytes_accessed=4 * keys * rows, transcendentals=work
        ),
        name="attend_back",
    )(q, kv, bias, o, do, lse)


def gather_weight(shard, place):
    near = swap_ylo(shard)
    far = swap_across(shard)
    far_near = swap_ylo(far)
    first = place["ylo"] == 0
    own = in_order(first, shard, near)
    other = in_order(first, far_near, far)
    early = place["section"] == 0
    pairs = (pick(early, own, other), pick(early, other, own))
    return [lax.all_gather(p, "x", axis=0, tiled=True) for p in pairs]


def reduce_weight_x(grad):
    return lax.psum_scatter(grad, "x", scatter_dimension=0, tiled=True)


def reduce_weight_y(parts, place):
    early = place["section"] == 0
    own = pick(early, parts[0], parts[1])
    other = pick(early, parts[1], parts[0])
    first = place["ylo"] == 0
    n = own.shape[0] // 2
    own_keep, own_send = pick(first, own[:n], own[n:]), pick(first, own[n:], own[:n])
    far_send, far_keep = pick(first, other[:n], other[n:]), pick(first, other[n:], other[:n])
    far = far_keep.astype(F32) + swap_ylo(far_send).astype(F32)
    crossed = swap_across(far.astype(BF16))
    near = swap_ylo(own_send)
    return own_keep.astype(F32) + near.astype(F32) + crossed.astype(F32)


def rms(rows):
    return lax.rsqrt(jnp.mean(rows * rows, axis=-1, keepdims=True) + EPS)


def rotate(v):
    lane = lax.broadcasted_iota(jnp.int32, v.shape, 1) % HD
    return jnp.where(lane < HD // 2, -jnp.roll(v, -HD // 2, 1), jnp.roll(v, HD // 2, 1))


def rotate_back(w):
    lane = lax.broadcasted_iota(jnp.int32, w.shape, 1) % HD
    return jnp.where(lane < HD // 2, jnp.roll(w, -HD // 2, 1), -jnp.roll(w, HD // 2, 1))


def norm_back(grad, n, r, gain):
    scaled = grad * gain
    return r * (scaled - n * jnp.mean(scaled * n, axis=-1, keepdims=True))


def halves(w, first):
    n = w.shape[1] // 2
    return pick(first, w[:, :n], w[:, n:]), pick(first, w[:, n:], w[:, :n])


def body(
    block_input,
    out_grad,
    seg_ids,
    attn_gain,
    w_query,
    w_key,
    w_value,
    w_out,
    ffn_gain,
    w_gate,
    w_up,
    w_down,
):
    place = {name: lax.axis_index(name) for name in AXES}
    section, core, tp = place["section"], place["core"], place["tp"]
    even = core == 0

    q_own, q_send = halves(w_query[0], even)
    kv_own = pick(even, w_key[0], w_value[0])
    kv_send = pick(even, w_value[0], w_key[0])
    out_own, out_send = halves(w_out[0].T, even)
    gate_own, gate_send = halves(w_gate[0], even)
    up_own, up_send = halves(w_up[0], even)
    down_own, down_send = halves(w_down[0].T, even)

    def chip_rows(own, send):
        return in_order(even, jnp.concatenate(own, 1), swap_core(jnp.concatenate(send, 1)))

    w_qkv2 = gather_weight(chip_rows([q_own, kv_own], [q_send, kv_send]), place)
    w_out2 = gather_weight(chip_rows([out_own], [out_send]), place)
    w_gu2 = gather_weight(chip_rows([gate_own, up_own], [gate_send, up_send]), place)
    w_dn2 = gather_weight(chip_rows([down_own], [down_send]), place)

    gains = jnp.concatenate([attn_gain, ffn_gain], axis=0)
    gains = lax.all_gather(gains, ("section", "x", "ylo", "core"), axis=0, tiled=False)
    gains = gains.reshape(2, 16, 2, -1).transpose(0, 2, 1, 3).reshape(2, 2, -1).astype(F32)

    micro_rows = block_input.shape[1]
    group = 8 * micro_rows
    block = place["x"] * 2 + place["ylo"]
    seg_row = lax.dynamic_index_in_dim(seg_ids, section, 0, keepdims=False)
    turn = (jnp.arange(4) + tp) % 4
    inner = turn[:, None] * micro_rows + jnp.arange(micro_rows)[None, :]
    inner = inner.reshape(-1)
    cores = jnp.arange(2)
    q_pos = ((cores + core) % 2)[:, None] * (4 * micro_rows) + inner[None, :]
    q_pos = q_pos.reshape(-1) + block * group
    k_pos = cores[:, None] * (4 * micro_rows) + inner[None, :]
    k_pos = (jnp.arange(8) * group)[:, None] + k_pos.reshape(-1)[None, :]
    k_pos = k_pos.reshape(-1)
    q_seg, k_seg = seg_row[q_pos], seg_row[k_pos]
    seen = (k_pos[:, None] <= q_pos[None, :]) & (k_seg[:, None] == q_seg[None, :])
    bias = jnp.where(seen, 0.0, MASKED).astype(F32)

    frequency = 10000.0 ** (-jnp.arange(0, HD, 2, dtype=F32) / HD)
    angles = q_pos.astype(F32)[:, None] * frequency[None, :]
    cos, sin = jnp.cos(angles), jnp.sin(angles)
    cos, sin = (jnp.concatenate([t] * 10, axis=1) for t in (cos, sin))
    plain = (lax.broadcasted_iota(jnp.int32, cos.shape, 1) >= 4 * HD) & (core == 1)
    cos, sin = jnp.where(plain, 1.0, cos), jnp.where(plain, 0.0, sin)
    q_width = 4 * HD
    scale = jnp.where(jnp.arange(cos.shape[1]) < q_width, HD**-0.5, 1.0)

    def forward(x, layer):
        gain_a, gain_f = gains[layer, 0], gains[layer, 1]
        r1 = rms(x)
        a = gather_rows((x * r1 * gain_a).astype(BF16))
        qkv = nn(a, w_qkv2[layer])
        qkv = (qkv * cos + rotate(qkv) * sin).astype(BF16)
        q = qkv[:, :q_width] * jnp.asarray(HD**-0.5, BF16)
        kv = qkv[:, q_width:]
        n = kv.shape[0] // 2
        kv = pick(even, kv, jnp.concatenate([kv[n:], kv[:n]], axis=0))
        kv = gather_kv(in_order(even, kv, swap_core(kv), 1))
        ctx, lse = attend(q, kv, bias)
        mid = x + reduce_rows(nt(ctx, w_out2[layer]))
        r2 = rms(mid)
        b = gather_rows((mid * r2 * gain_f).astype(BF16))
        gu = nn(b, w_gu2[layer])
        units = gu.shape[1] // 2
        gate, up = gu[:, :units], gu[:, units:]
        hidden = (gate / (1.0 + jnp.exp(-gate)) * up).astype(BF16)
        y = mid + reduce_rows(nt(hidden, w_dn2[layer]))
        return y, (x, r1, a, q, kv, ctx, lse, mid, r2, b, gate, up, hidden)

    def backward(dy, kept, layer):
        x, r1, a, q, kv, ctx, lse, mid, r2, b, gate, up, hidden = kept
        gain_a, gain_f = gains[layer, 0], gains[layer, 1]
        dff = gather_rows(dy.astype(BF16))
        g_dn = tn(dff, hidden).astype(BF16)
        dhidden = nn(dff, w_dn2[layer])
        sig = 1.0 / (1.0 + jnp.exp(-gate))
        dgate = dhidden * up * (sig * (1.0 + gate * (1.0 - sig)))
        dup = dhidden * (gate * sig)
        dgu = jnp.concatenate([dgate, dup], axis=1).astype(BF16)
        g_gu = tn(b, dgu).astype(BF16)
        db = reduce_rows(nt(dgu, w_gu2[layer]))
        n2 = mid * r2
        gg_f = jnp.sum(db * n2, axis=0)
        dmid = dy + norm_back(db, n2, r2, gain_f)
        dattn = gather_rows(dmid.astype(BF16))
        g_out = tn(dattn, ctx).astype(BF16)
        do = nn(dattn, w_out2[layer]).astype(BF16)
        dq, dkv = attend_back(q, kv, bias, ctx, do, lse)
        dkv = reduce_kv(dkv)
        n = dkv.shape[0] // 2
        dkv_own = pick(even, dkv[:, :HD], dkv[:, HD:])
        dkv_send = pick(even, dkv[:, HD:], dkv[:, :HD])
        dkv = dkv_own + swap_core(dkv_send.astype(BF16)).astype(F32)
        dkv = pick(even, dkv, jnp.concatenate([dkv[n:], dkv[:n]], axis=0))
        dqkv = jnp.concatenate([dq, dkv], axis=1)
        dqkv = (dqkv * cos + rotate_back(dqkv * sin)).astype(BF16)
        g_qkv = tn(a, dqkv).astype(BF16)
        da = reduce_rows(nt(dqkv, w_qkv2[layer]))
        n1 = x * r1
        gg_a = jnp.sum(da * n1, axis=0)
        dx = dmid + norm_back(da, n1, r1, gain_a)
        return dx, (g_qkv, g_out, g_gu, g_dn), (gg_a, gg_f)

    x0 = lax.dynamic_index_in_dim(block_input, section, 0, keepdims=False).astype(F32)
    y0, kept0 = forward(x0, 0)
    y0_low = y0.astype(BF16)
    y1, kept1 = forward(y0_low.astype(F32), 1)
    y1_low = y1.astype(BF16)
    dy1 = lax.dynamic_index_in_dim(out_grad, section, 0, keepdims=False).astype(F32)
    dx1, mats1, gg1 = backward(dy1, kept1, 1)
    parts1 = [reduce_weight_x(g) for g in mats1]
    dx0, mats0, gg0 = backward(dx1.astype(BF16).astype(F32), kept0, 0)
    parts0 = [reduce_weight_x(g) for g in mats0]

    early = section == 0

    def both_micros(layer0, layer1, dtype):
        own = pick(early, layer0, layer1)
        other = swap_section(pick(early, layer1, layer0).astype(BF16)).astype(dtype)
        return in_order(early, own.astype(dtype)[None], other[None])[None]

    block_output = both_micros(y0_low, y1_low, BF16)
    input_grad = both_micros(dx0, dx1, F32)

    def finish(parts):
        chip = reduce_weight_y(parts, place)
        n = chip.shape[0] // 2
        own, send = pick(even, chip[:n], chip[n:]), pick(even, chip[n:], chip[:n])
        other = swap_core(send.astype(BF16)).astype(F32)
        return own, other

    def across(own, other):
        return in_order(even, own, other, 1)

    g_qkv, g_out, g_gu, g_dn = [finish(p) for p in zip(parts0, parts1)]
    w = q_width
    grad_query = across(g_qkv[0][:, :w], g_qkv[1][:, :w])
    grad_key = pick(even, g_qkv[0][:, w:], g_qkv[1][:, w:])
    grad_value = pick(even, g_qkv[1][:, w:], g_qkv[0][:, w:])
    grad_out = across(*g_out).T
    u = g_gu[0].shape[1] // 2
    grad_gate = across(g_gu[0][:, :u], g_gu[1][:, :u])
    grad_up = across(g_gu[0][:, u:], g_gu[1][:, u:])
    grad_down = across(*g_dn).T

    own = pick(early, jnp.stack(gg0), jnp.stack(gg1))
    other = pick(early, jnp.stack(gg1), jnp.stack(gg0))
    own = own + swap_section(other)
    blocks = own.reshape(2, 64, -1).transpose(1, 0, 2)
    gain_sums = jnp.sum(
        lax.all_to_all(blocks, ("x", "ylo", "core", "tp"), 0, 0, tiled=True), axis=0
    )
    return (
        block_output,
        input_grad,
        gain_sums[0][None],
        grad_query[None],
        grad_key[None],
        grad_value[None],
        grad_out[None],
        gain_sums[1][None],
        grad_gate[None],
        grad_up[None],
        grad_down[None],
    )


def solution(mesh):
    fine = Mesh(mesh.devices.reshape(2, 4, 2, 2, 4), AXES)
    wide = ("x", "ylo", "core")
    rows = P(None, (*wide, "tp"), None)
    into = P("section", wide, "tp")
    out_of = P("section", "tp", wide)
    grown = P("section", None, (*wide, "tp"), None)
    gain_grad = P("section", (*wide, "tp"))
    return jax.shard_map(
        body,
        mesh=fine,
        in_specs=(
            rows, rows, P(), P("section", wide), into, into, into, out_of,
            P("section", wide), into, into, out_of,
        ),
        out_specs=(
            grown, grown, gain_grad, into, into, into, out_of, gain_grad, into, into, out_of,
        ),
        check_vma=False,
    )
```

time: 1300 us -> 827 us (0.64)
  matrix products: 305 us -> 59.3 us
  other arithmetic: 130 us -> 43 us
  waiting for transfers between devices: 499 us -> 414 us
  local copies, waits for them, and re-layouts: 132 us -> 63.9 us
  blocking collectives: 0 us -> 52.1 us
  starting transfers between devices: 186 us -> 148 us
  loops' own time: 20.3 us -> 0 us
  Pallas kernels: 0 us -> 19.3 us
    dot_general x84 -> x24, matrix products: 305 us -> 59.3 us  [the longest x8 23.9 us: tn(): lax.dot_general(a, b, (((0,), (0,)), ((), ())), preferred_element_type=F32)]
    ppermute x6 -> x103, waiting for transfers between devices: 21.5 us -> 222 us  [the longest x16 85.5 us: swap_ylo(): return lax.ppermute(v, 'ylo', [(0, 1), (1, 0)])]
    all_to_all x32 -> x4, starting transfers between devices: 166 us -> 17.9 us  [the longest x1 7.36 us: body(): lax.all_to_all(blocks, ('x', 'ylo', 'core', 'tp'), 0, 0, tiled=True)]
    all_gather x1 -> x8, waiting for transfers between devices: 121 us -> 8.33 us  [gather_weight(): return [lax.all_gather(p, 'x', axis=0, tiled=True) for p in pairs]]
    ppermute x6 -> x103, starting transfers between devices: 20.3 us -> 130 us  [the longest x48 57.6 us: from_z(): return lax.ppermute(rows, 'tp', [((i + by) % 4, i) for i in range(4)])]
    unnamed x7 -> x16, waiting for transfers between devices: 74 us -> 0.26 us
    all_to_all x32 -> x4, waiting for transfers between devices: 103 us -> 36 us  [the longest x2 17.9 us: gather_kv(): whole = lax.all_to_all(copies, ('x', 'ylo'), 0, 0, tiled=True)]
    all_gather x0 -> x1, blocking collectives: none -> 39.9 us  [body(): lax.all_gather(gains, ('section', 'x', 'ylo', 'core'), axis=0, tiled=False)]
  transfers between devices with their start and end apart: 43 -> 123, of which waited for: 30 -> 77; matrix products, arithmetic and copies ran while one was open for 21% -> 16% of each run, Pallas kernels for 0% -> 2%
where the time goes in v1:
time: 827 us; the launch traced here: 817 us
  waiting for transfers between devices  414 us (50%)
  starting transfers between devices  148 us (18%)
  local copies, waits for them, and re-layouts  63.9 us (8%)
  matrix products  59.3 us (7%)
  blocking collectives  52.1 us (6%)
  other arithmetic  43 us (5%)
  Pallas kernels  19.3 us (2%)
  between operations  16.6 us (2%)
    reduce_scatter x8, waiting for transfers between devices, reduce_weight_x(): return lax.psum_scatter(grad, 'x', scatter_dimension=0, tiled=True)  148 us
    ppermute x16, waiting for transfers between devices, swap_ylo(): return lax.ppermute(v, 'ylo', [(0, 1), (1, 0)])  85.5 us
    ppermute x48, waiting for transfers between devices, from_z(): return lax.ppermute(rows, 'tp', [((i + by) % 4, i) for i in range(4)])  72.1 us
    ppermute x48, starting transfers between devices, from_z(): return lax.ppermute(rows, 'tp', [((i + by) % 4, i) for i in range(4)])  57.6 us
    ppermute x28, starting transfers between devices, swap_core(): return lax.ppermute(v, 'core', [(0, 1), (1, 0)])  44 us
    ppermute x8, waiting for transfers between devices, swap_across(): return lax.ppermute(v, ('section', 'ylo'), [(0, 3), (3, 0), (1, 2), (2, 1)])  40 us
    all_gather x1, blocking collectives, body(): lax.all_gather(gains, ('section', 'x', 'ylo', 'core'), axis=0, tiled=False)  39.9 us
    unnamed x237, local copies, waits for them, and re-layouts  36.2 us
  transfers between devices with their start and end apart: 123, of which 77 were waited for; matrix products, arithmetic and copies ran while one was open for 16% of the time, Pallas kernels for 2%

profile of v1, /device:TPU:1, one launch (start us, length us, event | category | flops | bytes accessed | tf_op | source)
XLA Modules:
  0.0 816.8 jit_solution(11291171527962871675)
XLA Ops:
  31.5 18.6 %collective-permute-done.11 = bf16[256,256]{0,1:T(8,128)(2,1)S(1)} collective-permute-done((bf16[256,256]{0,1:T(8,128)(2,1)S(1)}, bf16[256,256]{0,1:T(8,128)(2,1)S(1)}, u32[]{:S(2)}, u32[]{:S(2)}) %collective-permute-start.11) | collective-permute-done | bytes 131104 | tf_op jit(solution)/shard_map/ppermute | solution.py:48
  56.4 13.8 %collective-permute-done.22 = bf16[256,1408]{0,1:T(8,128)(2,1)S(1)} collective-permute-done((bf16[256,1408]{0,1:T(8,128)(2,1)S(1)}, bf16[256,1408]{0,1:T(8,128)(2,1)S(1)}, u32[]{:S(2)}, u32[]{:S(2)}) %collective-permute-start.22) | collective-permute-done | bytes 720928 | tf_op jit(solution)/shard_map/ppermute | solution.py:40
  70.2 15.4 %collective-permute-done.24 = bf16[256,1408]{0,1:T(8,128)(2,1)S(1)} collective-permute-done((bf16[256,1408]{0,1:T(8,128)(2,1)S(1)}, bf16[256,1408]{0,1:T(8,128)(2,1)S(1)}, u32[]{:S(2)}, u32[]{:S(2)}) %collective-permute-start.24) | collective-permute-done | bytes 720928 | tf_op jit(solution)/shard_map/ppermute | solution.py:40
  92.3 39.9 %all-gather.1 = bf16[32,2,128]{2,1,0:T(2,128)(2,1)S(1)} all-gather(bf16[1,2,128]{2,1,0:T(2,128)(2,1)S(1)} %maximum_bitcast_fusion), channel_id=2, replica_groups=mesh['section'=2,'x'=4,'ylo'=2,'core'=2,'tp'=4] {'section','x','ylo','co..., dimensions={0}, use_global_device_ids=true | all-gather | bytes 16896 | tf_op jit(solution)/shard_map/all_gather | solution.py:282
  132.6 11.0 %collective-permute-done.27 = bf16[256,704]{0,1:T(8,128)(2,1)S(1)} collective-permute-done((bf16[256,704]{0,1:T(8,128)(2,1)S(1)}, bf16[256,704]{0,1:T(8,128)(2,1)S(1)}, u32[]{:S(2)}, u32[]{:S(2)}) %collective-permute-start.27) | collective-permute-done | bytes 360480 | tf_op jit(solution)/shard_map/ppermute | solution.py:48
  144.2 8.5 %collective-permute-done.28 = bf16[256,704]{0,1:T(8,128)(2,1)S(1)} collective-permute-done((bf16[256,704]{0,1:T(8,128)(2,1)S(1)}, bf16[256,704]{0,1:T(8,128)(2,1)S(1)}, u32[]{:S(2)}, u32[]{:S(2)}) %collective-permute-start.28) | collective-permute-done | bytes 360480 | tf_op jit(solution)/shard_map/ppermute | solution.py:40
  175.1 11.8 %gather_fusion = s32[2048]{0:T(1024)S(1)} fusion(s32[2048]{0:T(1024)S(1)} %bitcast.146, s32[2048]{0:T(1024)S(1)} %broadcast_clamp_fusion), kind=kCustom, calls=%fused_computation | custom fusion | bytes 24576 | tf_op jit(solution)/shard_map/gather | solution.py:298
  192.0 8.7 %all-to-all-done = bf16[8,256,128]{2,1,0:T(8,128)(2,1)S(1)} async-done(((bf16[8,256,128]{2,1,0:T(8,128)(2,1)}), bf16[8,256,128]{2,1,0:T(8,128)(2,1)S(1)}, u32[]{:S(2)}, u32[]{:S(2)}) %all-to-all-start) | async-done | bytes 524320 | tf_op jit(solution)/shard_map/all_to_all | solution.py:81
  294.7 9.2 %all-to-all-done.1 = bf16[8,256,128]{2,1,0:T(8,128)(2,1)S(1)} async-done(((bf16[8,256,128]{2,1,0:T(8,128)(2,1)}), bf16[8,256,128]{2,1,0:T(8,128)(2,1)S(1)}, u32[]{:S(2)}, u32[]{:S(2)}) %all-to-all-start.1) | async-done | bytes 524320 | tf_op jit(solution)/shard_map/all_to_all | solution.py:81
  343.8 5.9 fusion.125
  349.7 8.3 %all-gather.25.cloned.1.call-done = bf16[2048,704]{0,1:T(8,128)(2,1)} async-done(((bf16[512,704]{0,1:T(8,128)(2,1)}), bf16[2048,704]{0,1:T(8,128)(2,1)}) %all-gather.25.cloned.1.call-update) | async-done | bytes 2883600 | tf_op jit(solution)/shard_map/all_gather | solution.py:202
  391.5 5.7 attend_back.2
  397.2 12.2 %all_to_all.25 = bf16[8,256,128]{2,1,0:T(8,128)(2,1)S(1)} all-to-all(bf16[8,256,128]{2,1,0:T(8,128)(2,1)S(1)} %bitcast.144), channel_id=1, replica_groups=mesh['section'=2,'x'=4,'ylo'=2,'core'=2,'tp'=4] {'x','ylo'}, dimensions={0} | all-to-all | bytes 1048576 | tf_op jit(solution)/shard_map/all_to_all | solution.py:87
  485.7 6.4 attend_back.3
  498.7 12.2 %all-to-all-done.3 = bf16[8,256,128]{2,1,0:T(8,128)(2,1)S(1)} async-done(((bf16[8,256,128]{2,1,0:T(8,128)(2,1)}), bf16[8,256,128]{2,1,0:T(8,128)(2,1)S(1)}, u32[]{:S(2)}, u32[]{:S(2)}) %all-to-all-start.3) | async-done | bytes 524320 | tf_op jit(solution)/shard_map/all_to_all | solution.py:87
  525.2 5.6 convolution_convert_fusion
  556.9 7.4 all-to-all-start.4
  566.4 6.0 all-to-all-done.4
  604.7 38.1 %reduce-scatter.21.cloned.1.call-done = bf16[512,704]{0,1:T(8,128)(2,1)} async-done(((bf16[2048,704]{0,1:T(8,128)(2,1)}), bf16[512,704]{0,1:T(8,128)(2,1)}) %reduce-scatter.21.cloned.1.call-update) | async-done | bytes 720912 | tf_op jit(solution)/shard_map/reduce_scatter | solution.py:206
  646.5 7.1 collective-permute-done.100
  656.3 48.1 %reduce-scatter.19.cloned.1.call-done = bf16[512,1408]{0,1:T(8,128)(2,1)} async-done(((bf16[2048,1408]{0,1:T(8,128)(2,1)}), bf16[512,1408]{0,1:T(8,128)(2,1)}) %reduce-scatter.19.cloned.1.call-update) | async-done | bytes 1441808 | tf_op jit(solution)/shard_map/reduce_scatter | solution.py:206
  704.4 61.7 %reduce-scatter.17.cloned.1.call-done = bf16[512,1408]{0,1:T(8,128)(2,1)} async-done(((bf16[2048,1408]{0,1:T(8,128)(2,1)}), bf16[512,1408]{0,1:T(8,128)(2,1)}) %reduce-scatter.17.cloned.1.call-update) | async-done | bytes 1441808 | tf_op jit(solution)/shard_map/reduce_scatter | solution.py:206
  770.3 15.0 %collective-permute-done.96 = bf16[256,1408]{0,1:T(8,128)(2,1)S(1)} collective-permute-done((bf16[256,1408]{0,1:T(8,128)(2,1)S(1)}, bf16[256,1408]{0,1:T(8,128)(2,1)S(1)}, u32[]{:S(2)}, u32[]{:S(2)}) %collective-permute-start.96) | collective-permute-done | bytes 720928 | tf_op jit(solution)/shard_map/ppermute | solution.py:40
  793.1 7.6 collective-permute-done.95
  (700 shorter events, 416.1 us)
Async XLA Ops:
  7.2 162.4 %all-gather.11.cloned.1.call-start = ((), (), s32[]{:S(2)}) async-start(), calls=%async_computation.13 | async-start | bytes 1638400 | tf_op jit(solution)/shard_map/all_gather | solution.py:202
  24.4 180.0 %all-gather.13.cloned.1.call-start = ((), (), s32[]{:S(2)}) async-start(), calls=%async_computation.14 | async-start | bytes 1310720 | tf_op jit(solution)/shard_map/all_gather | solution.py:202
  28.6 26.4 %collective-permute-start.23 = (bf16[256,1408]{0,1:T(8,128)(2,1)S(1)}, bf16[256,1408]{0,1:T(8,128)(2,1)S(1)}, u32[]{:S(2)}, u32[]{:S(2)}) collective-permute-start(bf16[256,1408]{0,1:T(8,128)(2,1)S(1)} %maximum_select_fusion.2), channel_id=1, source_target_pairs={{0,72},{72,0},{8,64},{64,8},{1,73},{73,1},{9,65},{65,9},{2,74},{74... | collective-permute-start | bytes 2162696 | tf_op jit(solution)/shard_map/ppermute | solution.py:48
  54.8 185.9 %all-gather.15.cloned.1.call-start = ((), (), s32[]{:S(2)}) async-start(), calls=%async_computation.15 | async-start | bytes 7208960 | tf_op jit(solution)/shard_map/all_gather | solution.py:202
  55.0 30.7 %collective-permute-start.24 = (bf16[256,1408]{0,1:T(8,128)(2,1)S(1)}, bf16[256,1408]{0,1:T(8,128)(2,1)S(1)}, u32[]{:S(2)}, u32[]{:S(2)}) collective-permute-start(bf16[256,1408]{0,1:T(8,128)(2,1)S(1)} %collective-permute-done.23), channel_id=1, source_target_pairs={{0,8},{8,0},{1,9},{9,1},{2,10},{10,2},{3,11},{11,3},{4,12},{12,4},... | collective-permute-start | bytes 2162696 | tf_op jit(solution)/shard_map/ppermute | solution.py:40
  87.8 160.0 %all-gather.17.cloned.1.call-start = ((), (), s32[]{:S(2)}) async-start(), calls=%async_computation.16 | async-start | bytes 3604480 | tf_op jit(solution)/shard_map/all_gather | solution.py:202
  88.8 43.4 %collective-permute-start.25 = (bf16[128,704]{0,1:T(8,128)(2,1)S(1)}, bf16[128,704]{0,1:T(8,128)(2,1)S(1)}, u32[]{:S(2)}, u32[]{:S(2)}) collective-permute-start(bf16[128,704]{0,1:T(8,128)(2,1)S(1)} %get-tuple-element.196), channel_id=1, source_target_pairs={{0,4},{4,0},{1,5},{5,1},{2,6},{6,2},{3,7},{7,3},{8,12},{12,8},{9,1... | collective-permute-start | bytes 540680 | tf_op jit(solution)/shard_map/ppermute | solution.py:36
  154.3 124.1 %all-gather.19.cloned.1.call-start = ((), (), s32[]{:S(2)}) async-start(), calls=%async_computation.17 | async-start | bytes 1638400 | tf_op jit(solution)/shard_map/all_gather | solution.py:202
  191.4 116.1 %all-gather.21.cloned.1.call-start = ((), (), s32[]{:S(2)}) async-start(), calls=%async_computation.18 | async-start | bytes 1310720 | tf_op jit(solution)/shard_map/all_gather | solution.py:202
  209.2 134.5 %all-gather.23.cloned.1.call-start = ((), (), s32[]{:S(2)}) async-start(), calls=%async_computation.19 | async-start | bytes 7208960 | tf_op jit(solution)/shard_map/all_gather | solution.py:202
  288.6 69.4 %all-gather.25.cloned.1.call-start = ((), (), s32[]{:S(2)}) async-start(), calls=%async_computation.20 | async-start | bytes 3604480 | tf_op jit(solution)/shard_map/all_gather | solution.py:202
  290.3 22.1 %collective-permute-start.53 = (bf16[32,2048]{1,0:T(8,128)(2,1)}, bf16[32,2048]{1,0:T(8,128)(2,1)}, u32[]{:S(2)}, u32[]{:S(2)}) collective-permute-start(bf16[32,2048]{1,0:T(8,128)(2,1)} %get-tuple-element.101), channel_id=1, source_target_pairs={{3,0},{0,1},{1,2},{2,3},{7,4},{4,5},{5,6},{6,7},{11,8},{8,9},{9,10... | collective-permute-start | bytes 393224 | tf_op jit(solution)/shard_map/ppermute | solution.py:32
  290.5 21.9 %collective-permute-start.52 = (bf16[32,2048]{1,0:T(8,128)(2,1)}, bf16[32,2048]{1,0:T(8,128)(2,1)}, u32[]{:S(2)}, u32[]{:S(2)}) collective-permute-start(bf16[32,2048]{1,0:T(8,128)(2,1)} %get-tuple-element.101), channel_id=1, source_target_pairs={{2,0},{3,1},{0,2},{1,3},{6,4},{7,5},{4,6},{5,7},{10,8},{11,9},{8,1... | collective-permute-start | bytes 393224 | tf_op jit(solution)/shard_map/ppermute | solution.py:32
  314.3 258.7 %reduce-scatter.15.cloned.1.call-start = ((), (), s32[]{:S(2)}) async-start(), calls=%async_computation.24 | async-start | bytes 1310720 | tf_op jit(solution)/shard_map/reduce_scatter | solution.py:206
  460.9 112.2 %reduce-scatter.13.cloned.1.call-start = ((), (), s32[]{:S(2)}) async-start(), calls=%async_computation.23 | async-start | bytes 1310720 | tf_op jit(solution)/shard_map/reduce_scatter | solution.py:206
  495.6 91.9 %reduce-scatter.11.cloned.1.call-start = ((), (), s32[]{:S(2)}) async-start(), calls=%async_computation.22 | async-start | bytes 1638400 | tf_op jit(solution)/shard_map/reduce_scatter | solution.py:206
  498.6 88.9 %reduce-scatter.9.cloned.1.call-start = ((), (), s32[]{:S(2)}) async-start(), calls=%async_computation.21 | async-start | bytes 1638400 | tf_op jit(solution)/shard_map/reduce_scatter | solution.py:206
  516.5 88.2 %reduce-scatter.23.cloned.1.call-start = ((), (), s32[]{:S(2)}) async-start(), calls=%async_computation.28 | async-start | bytes 3604480 | tf_op jit(solution)/shard_map/reduce_scatter | solution.py:206
  520.3 122.4 %reduce-scatter.21.cloned.1.call-start = ((), (), s32[]{:S(2)}) async-start(), calls=%async_computation.27 | async-start | bytes 3604480 | tf_op jit(solution)/shard_map/reduce_scatter | solution.py:206
  524.1 180.3 %reduce-scatter.19.cloned.1.call-start = ((), (), s32[]{:S(2)}) async-start(), calls=%async_computation.26 | async-start | bytes 7208960 | tf_op jit(solution)/shard_map/reduce_scatter | solution.py:206
  530.9 235.2 %reduce-scatter.17.cloned.1.call-start = ((), (), s32[]{:S(2)}) async-start(), calls=%async_computation.25 | async-start | bytes 7208960 | tf_op jit(solution)/shard_map/reduce_scatter | solution.py:206
  646.1 123.3 %collective-permute-start.99 = (bf16[256,704]{0,1:T(8,128)(2,1)S(1)}, bf16[256,704]{0,1:T(8,128)(2,1)S(1)}, u32[]{:S(2)}, u32[]{:S(2)}) collective-permute-start(bf16[256,704]{0,1:T(8,128)(2,1)S(1)} %broadcast_select_fusion.11), channel_id=1, source_target_pairs={{0,8},{8,0},{1,9},{9,1},{2,10},{10,2},{3,11},{11,3},{4,12},{12,4},... | collective-permute-start | bytes 1081352 | tf_op jit(solution)/shard_map/ppermute | solution.py:40
  653.8 115.7 %collective-permute-start.101 = (bf16[256,704]{0,1:T(8,128)(2,1)S(1)}, bf16[256,704]{0,1:T(8,128)(2,1)S(1)}, u32[]{:S(2)}, u32[]{:S(2)}) collective-permute-start(bf16[256,704]{0,1:T(8,128)(2,1)S(1)} %add_convert_fusion.1), channel_id=1, source_target_pairs={{0,72},{72,0},{8,64},{64,8},{1,73},{73,1},{9,65},{65,9},{2,74},{74... | collective-permute-start | bytes 1081352 | tf_op jit(solution)/shard_map/ppermute | solution.py:48
  769.7 31.0 %collective-permute-start.95 = (bf16[256,1408]{0,1:T(8,128)(2,1)S(1)}, bf16[256,1408]{0,1:T(8,128)(2,1)S(1)}, u32[]{:S(2)}, u32[]{:S(2)}) collective-permute-start(bf16[256,1408]{0,1:T(8,128)(2,1)S(1)} %broadcast_select_fusion.5), channel_id=1, source_target_pairs={{0,8},{8,0},{1,9},{9,1},{2,10},{10,2},{3,11},{11,3},{4,12},{12,4},... | collective-permute-start | bytes 2162696 | tf_op jit(solution)/shard_map/ppermute | solution.py:40
  (201 other events, 1753.8 us)
Sparse Core Ops, SparseCore 0:
  24.5 26.9 all-gather.10
  54.9 26.6 all-gather.12
  87.9 65.8 all-gather.14
  155.9 37.9 all-gather.16
  195.4 25.5 all-gather.18
  223.1 24.7 all-gather.20
  249.6 68.1 all-gather.22
  320.0 37.9 all-gather.24
  461.0 21.5 reduce-scatter.14
  484.9 27.6 reduce-scatter.12
  515.0 23.5 reduce-scatter.10
  540.8 24.1 reduce-scatter.8
  567.4 37.1 reduce-scatter.22
  606.9 35.8 reduce-scatter.20
  645.0 59.3 reduce-scatter.18
  706.6 59.3 reduce-scatter.16

commit v2 on v1

v2 whole, which is shorter than its diff:
```python
import functools
import math

import jax
import jax.numpy as jnp
from jax import lax
from jax.experimental import pallas as pl
from jax.experimental.pallas import tpu as pltpu
from jax.sharding import Mesh, PartitionSpec as P

HD = 64
GAIN_ROWS = 16
EPS = 1e-05
MASKED = -1e30
KEYS_STEP = 512
AXES = ("section", "x", "ylo", "core", "tp")
SECTION, X, YLO, CORE, TP = range(5)
BF16 = jnp.bfloat16
F32 = jnp.float32
VMEM = pl.BlockSpec(memory_space=pltpu.VMEM)
SMEM = pl.BlockSpec(memory_space=pltpu.SMEM)
HBM = pl.BlockSpec(memory_space=pltpu.HBM)
DMA = pltpu.SemaphoreType.DMA


def nn(a, b):
    return jnp.dot(a, b, preferred_element_type=F32)


def nt(a, b):
    return lax.dot_general(a, b, (((1,), (1,)), ((), ())), preferred_element_type=F32)


def tn(a, b):
    return lax.dot_general(a, b, (((0,), (0,)), ((), ())), preferred_element_type=F32)


def shape(dims, dtype=BF16):
    return jax.ShapeDtypeStruct(tuple(dims), dtype)


SHORT = pl.CostEstimate(flops=1, bytes_accessed=1, transcendentals=0)


def call(kernel, outs, args, scratch=(), room=8, spec=VMEM, out_spec=VMEM):
    specs = []
    for a in args:
        own = SMEM if not isinstance(a, list) and a.dtype == jnp.int32 else spec
        specs += [HBM] * len(a) if isinstance(a, list) else [own]
    args = [v for a in args for v in (a if isinstance(a, list) else [a])]
    held = [m for m in scratch if isinstance(m, pltpu.VMEM((8, 128), F32).__class__)]
    room = room * 2**20 + sum(
        math.prod(m.shape) * jnp.dtype(m.dtype).itemsize for m in held if m.dtype in (BF16, F32)
    )
    return pl.pallas_call(
        kernel,
        out_shape=tuple(outs),
        in_specs=specs,
        out_specs=(out_spec,) * len(outs),
        scratch_shapes=list(scratch),
        compiler_params=pltpu.CompilerParams(vmem_limit_bytes=room),
        cost_estimate=SHORT,
        name=getattr(kernel, "func", kernel).__name__,
    )(*args)


def from_z(rows, by):
    return lax.ppermute(rows, "tp", [((i + by) % 4, i) for i in range(4)])


def from_x(v, by):
    return lax.ppermute(v, "x", [((i + by) % 4, i) for i in range(4)])


def swap_core(v):
    return lax.ppermute(v, "core", [(0, 1), (1, 0)])


def swap_ylo(v):
    return lax.ppermute(v, "ylo", [(0, 1), (1, 0)])


def swap_section(v):
    return lax.ppermute(v, "section", [(0, 1), (1, 0)])


def swap_across(v):
    return lax.ppermute(v, ("section", "ylo"), [(0, 3), (3, 0), (1, 2), (2, 1)])


def after(value, *others):
    return lax.optimization_barrier((value, *others))[0]


def y_exchange(v):
    return swap_ylo(v), swap_across(v), swap_section(v)


def gather_rows(rows):
    pieces = [rows] + [from_z(rows, k) for k in (1, 2, 3)]
    return pieces + [swap_core(p) for p in pieces]


def gather_kv(half):
    copies = jnp.broadcast_to(half[None], (8, *half.shape))
    own = lax.all_to_all(copies, ("x", "ylo"), 0, 0, tiled=True).reshape(-1, half.shape[1])
    return own, swap_core(own)


def reduce_rows(send, mine):
    own, *pieces = split(mine, swap_core(send))
    return [own] + [from_z(p, -k) for k, p in zip((1, 2, 3), pieces)]


def gather_x(block):
    return lax.all_gather(block, "x", axis=0, tiled=True)


def reduce_x(grad):
    return lax.psum_scatter(grad, "x", scatter_dimension=0, tiled=True)


def pack_attn_kernel(place, q_ref, k_ref, v_ref, o_ref, ga_ref, gf_ref, own_ref, send_ref):
    n, rows = q_ref.shape[1] // 2, q_ref.shape[0]
    m = n + 2 * HD
    kv = jnp.concatenate([k_ref[...], v_ref[...]], axis=1)
    o = o_ref[...].T
    odd = place[CORE] == 1
    row = lax.broadcasted_iota(jnp.int32, (GAIN_ROWS, ga_ref.shape[1]), 0)
    ga, gf = (jnp.broadcast_to(g[...].astype(F32), row.shape) for g in (ga_ref, gf_ref))
    gains = jnp.where(row == 0, ga, jnp.where(row == 1, gf, 0.0)).astype(BF16)
    rest = jnp.zeros((GAIN_ROWS, own_ref.shape[1] - gains.shape[1]), BF16)
    for ref, high in ((own_ref, odd), (send_ref, jnp.logical_not(odd))):
        ref[:rows, :n] = jnp.where(high, q_ref[:, n:], q_ref[:, :n])
        ref[:rows, n:m] = kv
        ref[:rows, m:] = jnp.where(high, o[:, n:], o[:, :n])
        ref[rows:, :] = jnp.concatenate([gains, rest], axis=1)


def pack_ffn_kernel(place, d_ref, g_ref, u_ref, own_ref, send_ref):
    odd = place[CORE] == 1
    d = d_ref[...].T
    n = d.shape[1] // 2
    spare = jnp.zeros((own_ref.shape[0], own_ref.shape[1] - 3 * n), BF16)
    low, high = (
        jnp.concatenate([w[:, at] for w in (g_ref[...], u_ref[...], d)] + [spare], axis=1)
        for at in (slice(0, n), slice(n, 2 * n))
    )
    own_ref[...] = jnp.where(odd, high, low)
    send_ref[...] = jnp.where(odd, low, high)


def chip_rows_kernel(place, own_ref, other_ref, out_ref):
    n = own_ref.shape[0]
    core = place[CORE]
    out_ref[pl.ds(pl.multiple_of(core * n, n), n), :] = own_ref[...]
    out_ref[pl.ds(pl.multiple_of((1 - core) * n, n), n), :] = other_ref[...]


def chip_rows(place, own, other):
    n, c = own.shape
    return call(chip_rows_kernel, [shape((2 * n, c))], [place, own, other])[0]


def chip_attn_kernel(place, own_ref, other_ref, out_ref):
    n = own_ref.shape[0] - GAIN_ROWS
    core = place[CORE]
    odd = core == 1
    out_ref[pl.ds(pl.multiple_of(core * n, n), n), :] = own_ref[:n, :]
    out_ref[pl.ds(pl.multiple_of((1 - core) * n, n), n), :] = other_ref[:n, :]
    own, other = own_ref[n:, :n], other_ref[n:, :n]
    rest = jnp.zeros((GAIN_ROWS, out_ref.shape[1] - 2 * n), BF16)
    out_ref[2 * n :, :] = jnp.concatenate(
        [jnp.where(odd, other, own), jnp.where(odd, own, other), rest], axis=1
    )


def pairs_kernel(place, own_ref, near_ref, far_ref, straight_ref, p0_ref, p1_ref):
    n = own_ref.shape[0]
    here = pl.ds(pl.multiple_of(place[YLO] * n, n), n)
    there = pl.ds(pl.multiple_of((1 - place[YLO]) * n, n), n)

    def fill(mine, other):
        mine[here, :] = own_ref[...]
        mine[there, :] = near_ref[...]
        other[here, :] = straight_ref[...]
        other[there, :] = far_ref[...]

    @pl.when(place[SECTION] == 0)
    def _():
        fill(p0_ref, p1_ref)

    @pl.when(place[SECTION] == 1)
    def _():
        fill(p1_ref, p0_ref)


def pairs(place, own, others):
    n, c = own.shape
    out = shape((2 * n, c))
    return call(pairs_kernel, [out, out], [place, own, *others])


def fetch(pieces, whole, sems):
    n = pieces[0].shape[0]
    copies = [
        pltpu.make_async_copy(p, whole.at[pl.ds(i * n, n), :], sems.at[i])
        for i, p in enumerate(pieces)
    ]
    for c in copies:
        c.start()

    def wait():
        for c in copies:
            c.wait()

    return wait


def rms(rows):
    return lax.rsqrt(jnp.mean(rows * rows, axis=-1, keepdims=True) + EPS)


def turned(v, by):
    return pltpu.roll(v, by % v.shape[1], 1)


def low_half(v):
    return lax.broadcasted_iota(jnp.int32, v.shape, 1) % HD < HD // 2


def rope(v, cos, sin):
    half = HD // 2
    return v * cos + jnp.where(low_half(v), -turned(v, -half), turned(v, half)) * sin


def rope_back(u, cos, sin):
    half, w = HD // 2, u * sin
    return u * cos + jnp.where(low_half(w), turned(w, -half), -turned(w, half))


def halves_out(partial, send_ref, mine_ref):
    n = send_ref.shape[0]
    send_ref[...] = partial[n:].astype(BF16)
    mine_ref[...] = partial[:n]


def split_kernel(mine_ref, other_ref, own_ref, *piece_refs):
    n = own_ref.shape[0]
    own_ref[...] = mine_ref[:n, :] + other_ref[:n, :].astype(F32)
    for k, ref in enumerate(piece_refs, 1):
        at = slice(k * n, (k + 1) * n)
        ref[...] = (mine_ref[at, :] + other_ref[at, :].astype(F32)).astype(BF16)


def split(mine, other):
    n, d = mine.shape[0] // 4, mine.shape[1]
    return call(split_kernel, [shape((n, d), F32)] + [shape((n, d))] * 3, [mine, other])


def total_of(refs):
    return sum((r[...].astype(F32) for r in refs[1:]), refs[0][...])


def add_norm_kernel(a, b, c, d, x_ref, gain_ref, mid_ref, low_ref):
    mid = x_ref[...].astype(F32) + total_of((a, b, c, d))
    mid_ref[...] = mid
    low_ref[...] = (mid * rms(mid) * gain_ref[...]).astype(BF16)


def add_kernel(a, b, c, d, mid_ref, y_ref):
    y_ref[...] = (mid_ref[...] + total_of((a, b, c, d))).astype(BF16)


def norm_back_kernel(a, b, c, d, after_ref, x_ref, gain_ref, dx_ref, low_ref, gain_grad_ref):
    grad = total_of((a, b, c, d))
    x = x_ref[...].astype(F32)
    r = rms(x)
    n = x * r
    gain_grad_ref[...] = jnp.sum(grad * n, axis=0, keepdims=True)
    scaled = grad * gain_ref[...]
    dx = after_ref[...].astype(F32) + r * (
        scaled - n * jnp.mean(scaled * n, axis=-1, keepdims=True)
    )
    dx_ref[...] = dx
    low_ref[...] = dx.astype(BF16)


def qkv_kernel(place, *refs, parts):
    pieces, refs = refs[:8], refs[8:]
    weights, refs = refs[:parts], refs[parts:]
    cos_ref, sin_ref, x_ref, a_ref, q_ref, kv_ref, w_ref, wo_ref, ga_ref, gf_ref, *refs = refs
    gains_ref, x_sems, w_sems = refs
    rows_there = fetch(pieces, x_ref, x_sems)
    n = w_ref.shape[0] // 8
    step = n + GAIN_ROWS

    def copies(i, block):
        src, at = (weights[0], i * step) if parts == 1 else (weights[i // 2], i % 2 * step)
        rows = pl.ds(pl.multiple_of(block * n, n), n)
        cols, m = w_ref.shape[1], wo_ref.shape[1]
        sides = (
            (src.at[pl.ds(at, n), pl.ds(0, cols)], w_ref.at[rows, :]),
            (src.at[pl.ds(at, n), pl.ds(cols, m)], wo_ref.at[rows, :]),
            (src.at[pl.ds(at + n, GAIN_ROWS), pl.ds(0, n)], gains_ref.at[block]),
        )
        return [pltpu.make_async_copy(a, b, w_sems.at[i, j]) for j, (a, b) in enumerate(sides)]

    for i in range(8):
        block = i if parts == 1 else lax.rem(place[X] + i // 2, 4) * 2 + i % 2
        for c in copies(i, block):
            c.start()
    for i in range(8):
        for c in copies(i, i):
            c.wait()
    gains = jnp.concatenate([gains_ref[i] for i in range(8)], axis=1).astype(F32)
    ga_ref[...] = gains[0:1, :]
    gf_ref[...] = gains[1:2, :]
    rows_there()
    x = x_ref[...].astype(F32)
    a = (x * rms(x) * ga_ref[...]).astype(BF16)
    a_ref[...] = a
    out = rope(nn(a, w_ref[...]), cos_ref[...], sin_ref[...])
    width = q_ref.shape[1]
    q_ref[...] = (out[:, :width].astype(BF16).astype(F32) * HD**-0.5).astype(BF16)
    half = out.shape[0] // 2
    k, v = out[:, width : width + HD], out[:, width + HD :]
    keys = jnp.concatenate([k[:half], k[half:]], axis=1)
    values = jnp.concatenate([v[half:], v[:half]], axis=1)
    kv_ref[...] = jnp.where(place[CORE] == 1, values, keys).astype(BF16)


def key_step(ref, t):
    per = ref.shape[0] // KEYS_STEP
    return pl.ds(t % per * KEYS_STEP, KEYS_STEP), slice(t // per * HD, (t // per + 1) * HD)


def attend_kernel(place, q_ref, own_ref, other_ref, bias_ref, w_hbm, *refs):
    o_ref, lse_ref, k_ref, v_ref, send_ref, mine_ref, s_ref, w_ref, sem = refs
    load = pltpu.make_async_copy(w_hbm, w_ref, sem)
    load.start()
    odd = place[CORE] == 1
    k_ref[...] = jnp.where(odd, other_ref[...], own_ref[...])
    v_ref[...] = jnp.where(odd, own_ref[...], other_ref[...])
    rows, width = q_ref.shape
    heads = width // HD
    steps = 2 * k_ref.shape[0] // KEYS_STEP
    tops = [jnp.full((1, rows), MASKED, F32) for _ in range(heads)]
    for t in range(steps):
        at = pl.ds(t * KEYS_STEP, KEYS_STEP)
        part, cols = key_step(k_ref, t)
        k = k_ref[part, cols]
        bias = bias_ref[at, :]
        for h in range(heads):
            s = nt(k, q_ref[:, h * HD : (h + 1) * HD]) + bias
            s_ref[h, at, :] = s
            tops[h] = jnp.maximum(tops[h], jnp.max(s, axis=0, keepdims=True))
    sums = [jnp.zeros((1, rows), F32) for _ in range(heads)]
    outs = [jnp.zeros((HD, rows), F32) for _ in range(heads)]
    for t in range(steps):
        at = pl.ds(t * KEYS_STEP, KEYS_STEP)
        part, cols = key_step(v_ref, t)
        v_t = v_ref[part, :].T[cols, :]
        for h in range(heads):
            e = jnp.exp(s_ref[h, at, :] - tops[h])
            sums[h] = sums[h] + jnp.sum(e, axis=0, keepdims=True)
            outs[h] = outs[h] + nn(v_t, e.astype(BF16))
    flat = jnp.concatenate([outs[h] / sums[h] for h in range(heads)], axis=0)
    o_ref[...] = flat.T.astype(BF16)
    lse_ref[...] = jnp.concatenate([tops[h] + jnp.log(sums[h]) for h in range(heads)], axis=0)
    load.wait()
    halves_out(nt(o_ref[...], w_ref[...]), send_ref, mine_ref)


def ffn_kernel(*refs):
    pieces, w_hbm, refs = refs[:8], refs[8], refs[9:]
    b_ref, gu_ref, h_ref, send_ref, mine_ref, gu_w, down_w, b_sems, gu_sems, sem = refs
    rows_there = fetch(pieces, b_ref, b_sems)
    steps, n, c = 4, w_hbm.shape[0] // 4, gu_w.shape[1]

    def load(i):
        at = pl.ds(i * n, n)
        return pltpu.make_async_copy(w_hbm.at[at, pl.ds(0, c)], gu_w.at[at, :], gu_sems.at[i])

    for i in range(steps):
        load(i).start()
    down = pltpu.make_async_copy(w_hbm.at[:, pl.ds(c, down_w.shape[1])], down_w, sem)
    down.start()
    rows_there()
    for i in range(steps):
        load(i).wait()
        at = slice(i * n, (i + 1) * n)
        part = nn(b_ref[:, at], gu_w[at, :])
        gu_ref[...] = part if i == 0 else gu_ref[...] + part
    units = gu_ref.shape[1] // 2
    gate, up = gu_ref[:, :units], gu_ref[:, units:]
    h_ref[:, :units] = (gate / (1.0 + jnp.exp(-gate)) * up).astype(BF16)
    spare = h_ref.shape[1] - units
    h_ref[:, units:] = jnp.zeros((h_ref.shape[0], spare), BF16)
    down.wait()
    halves_out(nt(h_ref[...], down_w[...]), send_ref, mine_ref)


def ffn_back_kernel(*refs):
    pieces, w_hbm, act_hbm, refs = refs[:8], refs[8], refs[9], refs[10:]
    dff_ref, dgu_ref, send_ref, mine_ref, gu_w, down_w, gu_ref, r_sems, gu_sems = refs
    rows_there = fetch(pieces, dff_ref, r_sems)
    c = gu_w.shape[1]
    down = pltpu.make_async_copy(w_hbm.at[:, pl.ds(c, down_w.shape[1])], down_w, gu_sems.at[2])
    down.start()
    act = pltpu.make_async_copy(act_hbm, gu_ref, gu_sems.at[0])
    act.start()
    load = pltpu.make_async_copy(w_hbm.at[:, pl.ds(0, c)], gu_w, gu_sems.at[1])
    load.start()
    rows_there()
    down.wait()
    units = gu_ref.shape[1] // 2
    dh = nn(dff_ref[...], down_w[...])[:, :units]
    act.wait()
    gate, up = gu_ref[:, :units], gu_ref[:, units:]
    sig = 1.0 / (1.0 + jnp.exp(-gate))
    dgate = dh * up * (sig * (1.0 + gate * (1.0 - sig)))
    dgu_ref[...] = jnp.concatenate([dgate, dh * (gate * sig)], axis=1).astype(BF16)
    load.wait()
    halves_out(nt(dgu_ref[...], gu_w[...]), send_ref, mine_ref)


def attend_back_kernel(place, *refs):
    pieces, refs = refs[:8], refs[8:]
    w_hbm, q_ref, k_ref, v_ref, bias_ref, o_ref, lse_ref, cos_ref, sin_ref, *refs = refs
    dattn_ref, dq_ref, own_ref, send_ref, w_ref, do_ref, dk_ref, dv_ref, sem, r_sems = refs
    rows_there = fetch(pieces, dattn_ref, r_sems)
    load = pltpu.make_async_copy(w_hbm, w_ref, sem)
    load.start()
    rows, width = q_ref.shape
    heads = width // HD
    steps = 2 * k_ref.shape[0] // KEYS_STEP
    rows_there()
    load.wait()
    do = nn(dattn_ref[...], w_ref[...])
    do_ref[...] = do.astype(BF16)
    both = (do_ref[...].astype(F32) * o_ref[...].astype(F32)).T
    deltas = [
        jnp.sum(both[h * HD : (h + 1) * HD, :], axis=0, keepdims=True) for h in range(heads)
    ]
    dq_t = [jnp.zeros((HD, rows), F32) for _ in range(heads)]
    for t in range(steps):
        at = pl.ds(t * KEYS_STEP, KEYS_STEP)
        part, cols = key_step(k_ref, t)
        k = k_ref[part, cols]
        v = v_ref[part, cols]
        k_t = k_ref[part, :].T[cols, :]
        bias = bias_ref[at, :]
        dk = jnp.zeros((KEYS_STEP, HD), F32)
        dv = jnp.zeros((KEYS_STEP, HD), F32)
        for h in range(heads):
            q_h = q_ref[:, h * HD : (h + 1) * HD]
            do_h = do_ref[:, h * HD : (h + 1) * HD]
            p = jnp.exp(nt(k, q_h) + bias - lse_ref[h : h + 1, :])
            ds = (p * (nt(v, do_h) - deltas[h])).astype(BF16)
            dv = dv + nn(p.astype(BF16), do_h)
            dk = dk + nn(ds, q_h)
            dq_t[h] = dq_t[h] + nn(k_t, ds)
        dk_ref[part, cols] = dk
        dv_ref[part, cols] = dv
    dq = jnp.concatenate(dq_t, axis=0).T * HD**-0.5
    dq_ref[...] = rope_back(dq, cos_ref[:, :width], sin_ref[:, :width]).astype(BF16)
    odd = place[CORE] == 1
    own_ref[...] = jnp.where(odd, dv_ref[...], dk_ref[...])
    send_ref[...] = jnp.where(odd, dk_ref[...], dv_ref[...]).astype(BF16)


def kv_add_kernel(own_ref, other_ref, out_ref):
    out_ref[...] = (own_ref[...] + other_ref[...].astype(F32)).astype(BF16)


def qkv_back_kernel(place, w_hbm, x_hbm, dq_ref, kv_ref, cos_ref, sin_ref, *refs):
    dqkv_ref, send_ref, mine_ref, gain_grad_ref, w_ref, x_ref, sems = refs
    load = pltpu.make_async_copy(w_hbm, w_ref, sems.at[0])
    load.start()
    rows_there = pltpu.make_async_copy(x_hbm, x_ref, sems.at[1])
    rows_there.start()
    width, odd = dq_ref.shape[1], place[CORE] == 1
    both = sum((kv_ref[i].astype(F32) for i in range(1, 8)), kv_ref[0].astype(F32))
    first, second = both[:, :HD], both[:, HD:]
    dk = jnp.concatenate([first, second], axis=0)
    dv = jnp.concatenate([second, first], axis=0)
    spare = jnp.zeros_like(dk)
    dkv = jnp.where(
        odd, jnp.concatenate([spare, dv], axis=1), jnp.concatenate([dk, spare], axis=1)
    )
    dkv = rope_back(dkv, cos_ref[:, width:], sin_ref[:, width:])
    dqkv_ref[:, :width] = dq_ref[...]
    dqkv_ref[:, width:] = dkv.astype(BF16)
    load.wait()
    da = nt(dqkv_ref[...], w_ref[...])
    halves_out(da, send_ref, mine_ref)
    rows_there.wait()
    x = x_ref[...].astype(F32)
    gain_grad_ref[...] = jnp.sum(da * (x * rms(x)), axis=0, keepdims=True)


def ffn_product_kernel(b_ref, dgu_ref, dff_ref, h_ref, out_ref):
    n = dgu_ref.shape[1]
    out_ref[:, :n] = tn(b_ref[...], dgu_ref[...]).astype(BF16)
    out_ref[:, n:] = tn(dff_ref[...], h_ref[...]).astype(BF16)


def ffn_products(b, dgu, dff, hidden):
    rows, d = b.shape
    n, wide = 256, dgu.shape[1] + hidden.shape[1]
    left = pl.BlockSpec((rows, n), lambda i: (0, i))
    return pl.pallas_call(
        ffn_product_kernel,
        out_shape=shape((d, wide)),
        grid=(d // n,),
        in_specs=[
            left,
            pl.BlockSpec(dgu.shape, lambda i: (0, 0)),
            left,
            pl.BlockSpec(hidden.shape, lambda i: (0, 0)),
        ],
        out_specs=pl.BlockSpec((n, wide), lambda i: (i, 0)),
        compiler_params=pltpu.CompilerParams(vmem_limit_bytes=16 * 1024 * 1024),
        cost_estimate=SHORT,
        name="ffn_product_kernel",
    )(b, dgu, dff, hidden)


def attn_product_kernel(dattn, a, gg_a, gg_f, ctx, dqkv, out):
    m = ctx.shape[1]
    wide = m + dqkv.shape[1]
    out[:, :m] = tn(dattn[...], ctx[...]).astype(BF16)
    out[:, m:wide] = tn(a[...], dqkv[...]).astype(BF16)
    row = lax.broadcasted_iota(jnp.int32, (out.shape[1] - wide, a.shape[1]), 0)
    ga, gf = (jnp.broadcast_to(g[...], row.shape) for g in (gg_a, gg_f))
    out[:, wide:] = jnp.where(row == 0, ga, jnp.where(row == 1, gf, 0.0)).T.astype(BF16)


def attn_products(dattn, ctx, a, dqkv, gg_a, gg_f):
    rows, d = a.shape
    n, wide = 512, ctx.shape[1] + dqkv.shape[1] + 128
    by_columns = [pl.BlockSpec((v.shape[0], n), lambda i: (0, i)) for v in (dattn, a, gg_a, gg_f)]
    return pl.pallas_call(
        attn_product_kernel,
        out_shape=shape((d, wide)),
        grid=(d // n,),
        in_specs=by_columns + [pl.BlockSpec(v.shape, lambda i: (0, 0)) for v in (ctx, dqkv)],
        out_specs=pl.BlockSpec((n, wide), lambda i: (i, 0)),
        compiler_params=pltpu.CompilerParams(vmem_limit_bytes=16 * 1024 * 1024),
        cost_estimate=SHORT,
        name="attn_product_kernel",
    )(dattn, a, gg_a, gg_f, ctx, dqkv)


def y_split_kernel(place, r0_ref, r1_ref, keep_ref, near_ref, far_ref, straight_ref):
    n = keep_ref.shape[0]
    here = pl.ds(pl.multiple_of(place[YLO] * n, n), n)
    there = pl.ds(pl.multiple_of((1 - place[YLO]) * n, n), n)

    def fill(mine, other):
        keep_ref[...] = mine[here, :]
        near_ref[...] = mine[there, :]
        straight_ref[...] = other[here, :]
        far_ref[...] = other[there, :]

    @pl.when(place[SECTION] == 0)
    def _():
        fill(r0_ref, r1_ref)

    @pl.when(place[SECTION] == 1)
    def _():
        fill(r1_ref, r0_ref)


def by_core_kernel(place, *refs):
    *parts, own_ref, send_ref = refs
    n = own_ref.shape[0]
    here = pl.ds(pl.multiple_of(place[CORE] * n, n), n)
    there = pl.ds(pl.multiple_of((1 - place[CORE]) * n, n), n)
    own_ref[...] = sum(p[here, :].astype(F32) for p in parts)
    send_ref[...] = sum(p[there, :].astype(F32) for p in parts).astype(BF16)


def by_core(parts, place):
    n, c = parts[0].shape[0] // 2, parts[0].shape[1]
    own, send = call(by_core_kernel, [shape((n, c), F32), shape((n, c))], [place, *parts])
    return own, swap_core(send)


def reduce_y(r0, r1, place):
    n, c = r0.shape[0] // 2, r0.shape[1]
    keep, near, far, straight = call(y_split_kernel, [shape((n, c))] * 4, [place, r0, r1])
    return [keep, swap_ylo(near), swap_across(far), swap_section(straight)]


def ordered(odd, own, other):
    other = other.astype(F32)
    return jnp.concatenate(
        [jnp.where(odd, other, own), jnp.where(odd, own, other)], axis=1
    )


def attn_grads_kernel(place, own_ref, other_ref, o_ref, q_ref, k_ref, v_ref, *gain_refs):
    odd = place[CORE] == 1
    m = n = q_ref.shape[1] // 2
    own, other = own_ref[:, :m].T, other_ref[:, :m].astype(F32).T
    o_ref[:m, :] = jnp.where(odd, other, own)
    o_ref[m:, :] = jnp.where(odd, own, other)
    q_ref[...] = ordered(odd, own_ref[:, m : m + n], other_ref[:, m : m + n])
    both = own_ref[:, m + n :] + other_ref[:, m + n :].astype(F32)
    k_ref[...] = both[:, :HD]
    v_ref[...] = both[:, HD : 2 * HD]
    rows = gain_refs[0].shape[0]
    gain_refs[-1][...] = both[:, 2 * HD :]
    for k, ref in enumerate(gain_refs[:-1]):
        at = lax.rem(place[TP] + k, 4) * rows
        ref[...] = gain_refs[-1][pl.ds(pl.multiple_of(at, rows), rows), :]


def ffn_grads_kernel(place, own_ref, other_ref, gate_ref, up_ref, down_ref):
    odd = place[CORE] == 1
    n = gate_ref.shape[1] // 2
    gate_ref[...] = ordered(odd, own_ref[:, :n], other_ref[:, :n])
    up_ref[...] = ordered(odd, own_ref[:, n : 2 * n], other_ref[:, n : 2 * n])
    own, other = own_ref[:, 2 * n :].T[:n], other_ref[:, 2 * n :].astype(F32).T[:n]
    down_ref[:n, :] = jnp.where(odd, other, own)
    down_ref[n:, :] = jnp.where(odd, own, other)


def body(
    block_input,
    out_grad,
    seg_ids,
    attn_gain,
    w_query,
    w_key,
    w_value,
    w_out,
    ffn_gain,
    w_gate,
    w_up,
    w_down,
):
    at = {name: lax.axis_index(name) for name in AXES}
    section, core, tp = at["section"], at["core"], at["tp"]
    place = jnp.stack([at[name] for name in AXES]).astype(jnp.int32)
    d = block_input.shape[2]
    micro_rows = block_input.shape[1]
    group = 8 * micro_rows
    q_width = w_query.shape[2] // 2
    units = w_gate.shape[2] // 2
    own_rows = w_query.shape[1]

    padded = units + (-units) % 128
    attn_dims = (own_rows + GAIN_ROWS, 2 * q_width + 2 * HD)
    attn_own, attn_send = call(
        pack_attn_kernel,
        [shape(attn_dims)] * 2,
        [place, w_query[0], w_key[0], w_value[0], w_out[0], attn_gain, ffn_gain],
        spec=pl.BlockSpec(),
    )
    attn_shard = call(
        chip_attn_kernel,
        [shape((2 * own_rows + GAIN_ROWS, attn_dims[1]))],
        [place, attn_own, swap_core(attn_send)],
    )[0]
    attn_y = y_exchange(attn_shard)
    attn_pairs = pairs(place, attn_shard, attn_y)
    attn0 = [attn_pairs[0]] + [from_x(attn_pairs[0], k) for k in (1, 2, 3)]

    ffn_own, ffn_send = call(
        pack_ffn_kernel,
        [shape((own_rows, 2 * units + padded))] * 2,
        [place, w_down[0], after(w_gate, attn_y[0])[0], w_up[0]],
        room=12,
        spec=pl.BlockSpec(),
    )
    ffn_shard = chip_rows(place, ffn_own, swap_core(ffn_send))
    ffn_y = y_exchange(after(ffn_shard, attn_pairs[0]))

    block = at["x"] * 2 + at["ylo"]
    seg_row = lax.dynamic_index_in_dim(seg_ids, section, 0, keepdims=False)
    def arranged(row):
        v = row.reshape(8, 2, 4, micro_rows)
        return lax.dynamic_slice_in_dim(jnp.concatenate([v, v], axis=2), tp, 4, 2)

    def keys_of(row):
        return arranged(row).transpose(1, 0, 2, 3).reshape(-1)

    def queries_of(row):
        v = lax.dynamic_index_in_dim(arranged(row), block, 0, keepdims=False)
        return jnp.where(core == 0, v, v[::-1]).reshape(-1)

    places = jnp.arange(seg_row.shape[0], dtype=jnp.int32)
    k_pos, k_seg = keys_of(places), keys_of(seg_row)
    q_pos, q_seg = queries_of(places), queries_of(seg_row)
    seen = (k_pos[:, None] <= q_pos[None, :]) & (k_seg[:, None] == q_seg[None, :])
    bias = jnp.where(seen, 0.0, MASKED).astype(F32)

    frequency = 10000.0 ** (-jnp.arange(0, HD, 2, dtype=F32) / HD)
    angles = q_pos.astype(F32)[:, None] * frequency[None, :]
    wide = q_width + 2 * HD
    plain = lax.broadcasted_iota(jnp.int32, (group, wide), 1) >= q_width + HD
    cos, sin = (jnp.concatenate([t] * 12, axis=1) for t in (jnp.cos(angles), jnp.sin(angles)))
    cos, sin = jnp.where(plain, 1.0, cos), jnp.where(plain, 0.0, sin)

    rows_low, rows_f32 = shape((micro_rows, d)), shape((micro_rows, d), F32)
    all_low = shape((group, d))
    partials = [shape((group // 2, d)), shape((group // 2, d), F32)]
    heads, keys = q_width // HD, seg_row.shape[0]
    gain_row = shape((1, d), F32)

    def project(x, qkv_w):
        return call(
            functools.partial(qkv_kernel, parts=len(qkv_w)),
            [all_low, all_low, shape((group, q_width)), shape((group // 2, 2 * HD))]
            + [shape((d, wide)), shape((d, q_width)), gain_row, gain_row],
            [place, gather_rows(x) + qkv_w, cos, sin],
            [
                pltpu.VMEM((8, GAIN_ROWS, d // 8), BF16),
                DMA((8,)),
                DMA((8, 3)),
            ],
            room=14,
        )

    both_kv = shape((keys // 2, 2 * HD))

    def attention(q, kv, w_out):
        return call(
            attend_kernel,
            [shape((group, q_width)), shape((heads, group), F32), both_kv, both_kv, *partials],
            [place, q, *kv, bias, [w_out]],
            [
                pltpu.VMEM((heads, keys, group), F32),
                pltpu.VMEM((d, q_width), BF16),
                DMA,
            ],
            room=12,
        )

    def feed_forward(b, w_ffn):
        return call(
            ffn_kernel,
            [all_low, shape((group, 2 * units), F32), shape((group, padded)), *partials],
            [[*gather_rows(b), w_ffn]],
            [
                pltpu.VMEM((d, 2 * units), BF16),
                pltpu.VMEM((d, padded), BF16),
                DMA((8,)),
                DMA((4,)),
                DMA,
            ],
            room=12,
        )

    def backward(dy, kept, early=()):
        x, rows, qkv_w, a, q, k, v, ctx, lse, mid, b, gu, hidden, gain_a, gain_f, w_ffn, w_out = kept
        dff, dgu, send, mine = call(
            ffn_back_kernel,
            [all_low, shape((group, 2 * units)), *partials],
            [[*gather_rows(dy), w_ffn, gu]],
            [
                pltpu.VMEM((d, 2 * units), BF16),
                pltpu.VMEM((d, padded), BF16),
                pltpu.VMEM((group, 2 * units), F32),
                DMA((8,)),
                DMA((3,)),
            ],
            room=12,
        )
        g_ffn = ffn_products(b, dgu, dff, hidden)
        dmid, dattn, gg_f = call(
            norm_back_kernel,
            [rows_f32, rows_low, gain_row],
            [*reduce_rows(send, mine), dy, mid, gain_f],
        )
        dattn = after(dattn, g_ffn, *early)
        dattn, dq, dkv, dkv_send = call(
            attend_back_kernel,
            [all_low, shape((group, q_width)), shape((keys // 2, 2 * HD), F32), both_kv],
            [place, gather_rows(dattn) + [w_out], q, k, v, bias, ctx, lse, cos, sin],
            [
                pltpu.VMEM((d, q_width), BF16),
                pltpu.VMEM((group, q_width), BF16),
                pltpu.VMEM((keys // 2, 2 * HD), F32),
                pltpu.VMEM((keys // 2, 2 * HD), F32),
                DMA,
                DMA((8,)),
            ],
            room=18,
        )
        dkv = call(kv_add_kernel, [both_kv], [dkv, swap_core(dkv_send)])[0]
        arrived = lax.all_to_all(
            dkv.reshape(8, group // 2, 2 * HD), ("x", "ylo"), 0, 0, tiled=True
        )
        dqkv, send, mine, gg_a = call(
            qkv_back_kernel,
            [shape((group, wide)), *partials, gain_row],
            [place, [qkv_w, rows], dq, arrived, cos, sin],
            [pltpu.VMEM((d, wide), BF16), pltpu.VMEM((group, d), BF16), DMA((2,))],
            room=16,
        )
        g_attn = attn_products(dattn, ctx, a, dqkv, gg_a, gg_f)
        dx, dx_low, _ = call(
            norm_back_kernel,
            [rows_f32, rows_low, gain_row],
            [*reduce_rows(send, mine), dmid, x, gain_a],
        )
        return dx, after(dx_low, g_attn), g_attn, g_ffn

    x0 = lax.dynamic_index_in_dim(block_input, section, 0, keepdims=False)
    dy1 = lax.dynamic_index_in_dim(out_grad, section, 0, keepdims=False)

    rows0, a0, q0, kv0, w_qkv0, w_out0, ga0, gf0 = project(x0, attn0)
    ffn_pairs = pairs(place, ffn_shard, [after(v, a0) for v in ffn_y])
    w_ffn0 = gather_x(ffn_pairs[0])
    kv0 = gather_kv(kv0)
    ctx0, lse0, k0, v0, send, mine = attention(q0, kv0, w_out0)
    attn1 = gather_x(after(attn_pairs[1], ctx0))
    mid0, b = call(add_norm_kernel, [rows_f32, rows_low], [*reduce_rows(send, mine), x0, gf0])
    w_ffn1 = gather_x(after(ffn_pairs[1], b))
    b0, up0, hidden0, send, mine = feed_forward(b, w_ffn0)
    y0 = call(add_kernel, [rows_low], [*reduce_rows(send, mine), mid0])[0]
    kept0 = (x0, rows0, w_qkv0, a0, q0, k0, v0, ctx0, lse0, mid0, b0, up0, hidden0, ga0, gf0, w_ffn0, w_out0)
    rows1, a1, q1, kv1, w_qkv1, w_out1, ga1, gf1 = project(y0, [attn1])
    ctx1, lse1, k1, v1, send, mine = attention(q1, gather_kv(kv1), w_out1)
    mid1, b = call(add_norm_kernel, [rows_f32, rows_low], [*reduce_rows(send, mine), y0, gf1])
    b1, up1, hidden1, send, mine = feed_forward(b, w_ffn1)
    y1 = call(add_kernel, [rows_low], [*reduce_rows(send, mine), mid1])[0]
    kept1 = (y0, rows1, w_qkv1, a1, q1, k1, v1, ctx1, lse1, mid1, b1, up1, hidden1, ga1, gf1, w_ffn1, w_out1)

    dx1, dx1_low, g_attn1, g_ffn1 = backward(dy1, kept1)
    ffn1, r_attn1 = reduce_x(g_ffn1), reduce_x(g_attn1)
    dx0, dx0_low, g_attn0, g_ffn0 = backward(dx1_low, kept0, [ffn1])
    ffn_y = reduce_y(reduce_x(g_ffn0), ffn1, place)
    dx0 = after(dx0, r_attn1, *ffn_y)
    early = section == 0

    ffn_parts = by_core(ffn_y, place)
    attn_parts = by_core(reduce_y(reduce_x(g_attn0), r_attn1, place), place)

    def finish(kernel, dims, parts):
        return call(kernel, [shape(s, F32) for s in dims], [place, *parts], room=12)

    own = own_rows
    grad_out, grad_query, grad_key, grad_value, *gain_pieces, _ = finish(
        attn_grads_kernel,
        [(2 * q_width, own), (own, 2 * q_width), (own, HD), (own, HD)]
        + [(micro_rows, 128)] * 4
        + [(own, 128)],
        attn_parts,
    )
    grad_gate, grad_up, grad_down = finish(
        ffn_grads_kernel, [(own, 2 * units)] * 2 + [(2 * units, own)], ffn_parts
    )
    gain_sums = gain_pieces[0]
    for k in (1, 2, 3):
        gain_sums = gain_sums + from_z(gain_pieces[k], -k)
    gain_sums = gain_sums[:, :2].T

    def both_micros(layer0, layer1, dtype):
        mine = jnp.where(early, layer0, layer1).astype(dtype)
        other = jnp.where(early, layer1, layer0).astype(BF16)
        other = swap_section(other).astype(dtype)
        return jnp.stack([jnp.where(early, mine, other), jnp.where(early, other, mine)])[None]

    block_output = both_micros(y0, y1, BF16)
    input_grad = both_micros(dx0, dx1, F32)

    return (
        block_output,
        input_grad,
        gain_sums[0][None],
        grad_query[None],
        grad_key[None],
        grad_value[None],
        grad_out[None],
        gain_sums[1][None],
        grad_gate[None],
        grad_up[None],
        grad_down[None],
    )


def solution(mesh):
    fine = Mesh(mesh.devices.reshape(2, 4, 2, 2, 4), AXES)
    wide = ("x", "ylo", "core")
    rows = P(None, (*wide, "tp"), None)
    into = P("section", wide, "tp")
    out_of = P("section", "tp", wide)
    grown = P("section", None, (*wide, "tp"), None)
    gain_grad = P("section", (*wide, "tp"))
    return jax.shard_map(
        body,
        mesh=fine,
        in_specs=(
            rows, rows, P(), P("section", wide), into, into, into, out_of,
            P("section", wide), into, into, out_of,
        ),
        out_specs=(
            grown, grown, gain_grad, into, into, into, out_of, gain_grad, into, into, out_of,
        ),
        check_vma=False,
    )
```

time: 827 us -> 698 us (0.84)
  waiting for transfers between devices: 414 us -> 236 us
  Pallas kernels: 19.3 us -> 104 us
  local copies, waits for them, and re-layouts: 63.9 us -> 125 us
  matrix products: 59.3 us -> 0 us
  other arithmetic: 43 us -> 4.15 us
  starting transfers between devices: 148 us -> 163 us
  blocking collectives: 52.1 us -> 40.2 us
    reduce_scatter x8 -> x4, waiting for transfers between devices: 148 us -> 16.7 us  [reduce_x(): return lax.psum_scatter(grad, 'x', scatter_dimension=0, tiled=True)]
    unnamed x237 -> x336, local copies, waits for them, and re-layouts: 36.2 us -> 122 us
    pallas_call x4 -> x46, Pallas kernels: 19.3 us -> 104 us  [the longest x42 91 us: call(): pl.pallas_call(kernel, out_shape=tuple(outs), in_specs=specs, out_specs=(...]
    ppermute x16 -> x4, waiting for transfers between devices: 85.5 us -> 5.37 us  [swap_ylo(): return lax.ppermute(v, 'ylo', [(0, 1), (1, 0)])]
    dot_general x24 -> x0, matrix products: 59.3 us -> none  [the longest x8 23.9 us: tn(): lax.dot_general(a, b, (((0,), (0,)), ((), ())), preferred_element_type=F32)]
    all_gather x8 -> x3, waiting for transfers between devices: 8.33 us -> 63.3 us  [gather_x(): return lax.all_gather(block, 'x', axis=0, tiled=True)]
    ppermute x3 -> x6, waiting for transfers between devices: 2.56 us -> 48.3 us  [swap_section(): return lax.ppermute(v, 'section', [(0, 1), (1, 0)])]
    ppermute x8 -> x4, waiting for transfers between devices: 40 us -> 0.01 us  [swap_across(): return lax.ppermute(v, ('section', 'ylo'), [(0, 3), (3, 0), (1, 2), (2, 1)])]
  transfers between devices with their start and end apart: 123 -> 124, of which waited for: 77 -> 48; matrix products, arithmetic and copies ran while one was open for 16% -> 1% of each run, Pallas kernels for 2% -> 13%
where the time goes in v2:
time: 698 us; the launch traced here: 688 us
  waiting for transfers between devices  236 us (34%)
  starting transfers between devices  163 us (23%)
  local copies, waits for them, and re-layouts  125 us (18%)
  Pallas kernels  104 us (15%)
  blocking collectives  40.2 us (6%)
  between operations  15.5 us (2%)
    unnamed x336, local copies, waits for them, and re-layouts  122 us
    pallas_call x42, Pallas kernels, call(): pl.pallas_call(kernel, out_shape=tuple(outs), in_specs=specs, out_specs=(...  91 us
    ppermute x48, starting transfers between devices, swap_core(): return lax.ppermute(v, 'core', [(0, 1), (1, 0)])  73.4 us
    all_gather x3, waiting for transfers between devices, gather_x(): return lax.all_gather(block, 'x', axis=0, tiled=True)  63.3 us
    ppermute x51, starting transfers between devices, from_z(): return lax.ppermute(rows, 'tp', [((i + by) % 4, i) for i in range(4)])  61.7 us
    ppermute x6, waiting for transfers between devices, swap_section(): return lax.ppermute(v, 'section', [(0, 1), (1, 0)])  48.3 us
    ppermute x51, waiting for transfers between devices, from_z(): return lax.ppermute(rows, 'tp', [((i + by) % 4, i) for i in range(4)])  42.9 us
    ppermute x3, waiting for transfers between devices, from_x(): return lax.ppermute(v, 'x', [((i + by) % 4, i) for i in range(4)])  30.3 us
  transfers between devices with their start and end apart: 124, of which 48 were waited for; matrix products, arithmetic and copies ran while one was open for 1% of the time, Pallas kernels for 13%

profile of v2, /device:TPU:1, one launch (start us, length us, event | category | flops | bytes accessed | tf_op | source)
XLA Modules:
  0.0 687.7 jit_solution(9450098253170173644)
XLA Ops:
  20.0 5.4 collective-permute-done.8.near_ref
  58.8 16.5 %collective-permute-done.11.refs_9_ = bf16[544,640]{1,0:T(8,128)(2,1)} collective-permute-done((bf16[544,640]{1,0:T(8,128)(2,1)}, bf16[544,640]{1,0:T(8,128)(2,1)}, u32[]{:S(2)}, u32[]{:S(2)}) %collective-permute-start.11) | collective-permute-done | bytes 696352 | tf_op jit(solution)/shard_map/ppermute | solution.py:72
  80.2 13.9 %collective-permute-done.13.refs_11_ = bf16[544,640]{1,0:T(8,128)(2,1)S(1)} collective-permute-done((bf16[544,640]{1,0:T(8,128)(2,1)}, bf16[544,640]{1,0:T(8,128)(2,1)S(1)}, u32[]{:S(2)}, u32[]{:S(2)}) %collective-permute-start.13) | collective-permute-done | bytes 696352 | tf_op jit(solution)/shard_map/ppermute | solution.py:72
  97.1 5.1 qkv_kernel.2
  116.5 5.4 all-to-all-done
  127.9 4.7 attend_kernel.2
  165.9 33.9 %all-gather.4.cloned.1.call-done.refs_8_ = bf16[2048,2176]{1,0:T(8,128)(2,1)} async-done(((bf16[512,2176]{1,0:T(8,128)(2,1)}), bf16[2048,2176]{1,0:T(8,128)(2,1)}) %all-gather.4.cloned.1.call-update) | async-done | bytes 8912912 | tf_op jit(solution)/shard_map/all_gather | solution.py:116
  208.8 5.5 ffn_kernel.2
  250.3 13.7 %all_to_all.20 = bf16[8,128,128]{2,1,0:T(8,128)(2,1)S(1)} all-to-all(bf16[8,128,128]{2,1,0:T(8,128)(2,1)S(1)} %broadcast_in_dim.61), channel_id=1, replica_groups=mesh['section'=2,'x'=4,'ylo'=2,'core'=2,'tp'=4] {'x','ylo'}, dimensions={0} | all-to-all | bytes 524288 | tf_op jit(solution)/shard_map/all_to_all | solution.py:106
  266.9 4.7 attend_kernel.3
  279.1 6.6 collective-permute-done.43.b
  301.7 29.5 %all-gather.8.cloned.1.call-done.refs_8_ = bf16[2048,2176]{1,0:T(8,128)(2,1)} async-done(((bf16[512,2176]{1,0:T(8,128)(2,1)}), bf16[2048,2176]{1,0:T(8,128)(2,1)}) %all-gather.8.cloned.1.call-update) | async-done | bytes 8912912 | tf_op jit(solution)/shard_map/all_gather | solution.py:116
  340.2 5.6 ffn_kernel.3
  346.6 5.7 ffn_back_kernel.2
  391.6 9.0 %attend_back_kernel.2 = (bf16[256,2048]{1,0:T(8,128)(2,1)S(1)}, bf16[256,256]{1,0:T(8,128)(2,1)S(1)}, f32[1024,128]{1,0:T(8,128)S(1)}, bf16[1024,128]{1,0:T(8,128)(2,1)S(1)}) custom-call(s32[5]{0:T(128)S(1)} %stack.41.place, bf16[32,2048]{1,0:T(8,128)(2,1)S(1)} %get-tuple-element.229.refs_0_, bf16[32,2048]{1,0:T(8,128)(2,1)S(1)} %collective-permute-done.69.refs_1_, ...), custom_call_target="tpu_custom_call" | custom-call | flops 1 | bytes 1 | tf_op jit(solution)/shard_map/attend_back_kernel/pallas_call | solution.py:55
  402.3 14.1 %all_to_all.21.kv_ref = bf16[8,128,128]{2,1,0:T(8,128)(2,1)S(1)} all-to-all(bf16[8,128,128]{2,1,0:T(8,128)(2,1)S(1)} %bitcast.53), channel_id=1, replica_groups=mesh['section'=2,'x'=4,'ylo'=2,'core'=2,'tp'=4] {'x','ylo'}, dimensions={0} | all-to-all | bytes 524288 | tf_op jit(solution)/shard_map/all_to_all | solution.py:795
  458.8 6.4 ffn_back_kernel.3
  481.9 6.2 collective-permute-done.89.b
  511.5 9.0 %attend_back_kernel.3 = (bf16[256,2048]{1,0:T(8,128)(2,1)S(1)}, bf16[256,256]{1,0:T(8,128)(2,1)S(1)}, f32[1024,128]{1,0:T(8,128)S(1)}, bf16[1024,128]{1,0:T(8,128)(2,1)S(1)}) custom-call(s32[5]{0:T(128)S(1)} %stack.41.place, bf16[32,2048]{1,0:T(8,128)(2,1)S(1)} %copy-done.136, bf16[32,2048]{1,0:T(8,128)(2,1)S(1)} %collective-permute-done.92.refs_1_, ...), custom_call_target="tpu_custom_call" | custom-call | flops 1 | bytes 1 | tf_op jit(solution)/shard_map/attend_back_kernel/pallas_call | solution.py:55
  522.2 12.4 %all_to_all.22.kv_ref = bf16[8,128,128]{2,1,0:T(8,128)(2,1)S(1)} all-to-all(bf16[8,128,128]{2,1,0:T(8,128)(2,1)S(1)} %bitcast.54), channel_id=1, replica_groups=mesh['section'=2,'x'=4,'ylo'=2,'core'=2,'tp'=4] {'x','ylo'}, dimensions={0} | all-to-all | bytes 524288 | tf_op jit(solution)/shard_map/all_to_all | solution.py:795
  551.4 7.5 %reduce-scatter.9.cloned.1.call-done.r0_ref = bf16[512,2176]{1,0:T(8,128)(2,1)} async-done(((bf16[2048,2176]{1,0:T(8,128)(2,1)}), bf16[512,2176]{1,0:T(8,128)(2,1)}) %reduce-scatter.9.cloned.1.call-update) | async-done | bytes 2228240 | tf_op jit(solution)/shard_map/reduce_scatter | solution.py:120
  579.5 41.0 %collective-permute-done.57 = bf16[32,2048]{1,0:T(8,128)(2,1)S(1)} collective-permute-done((bf16[32,2048]{1,0:T(8,128)(2,1)S(1)}, bf16[32,2048]{1,0:T(8,128)(2,1)S(1)}, u32[]{:S(2)}, u32[]{:S(2)}) %collective-permute-start.57) | collective-permute-done | bytes 131104 | tf_op jit(solution)/shard_map/ppermute | solution.py:84
  630.3 9.2 %reduce-scatter.11.cloned.1.call-done.r0_ref = bf16[512,768]{1,0:T(8,128)(2,1)} async-done(((bf16[2048,768]{1,0:T(8,128)(2,1)}), bf16[512,768]{1,0:T(8,128)(2,1)}) %reduce-scatter.11.cloned.1.call-update) | async-done | bytes 786448 | tf_op jit(solution)/shard_map/reduce_scatter | solution.py:120
  655.9 7.4 %collective-permute-done.110.refs_3_ = bf16[256,768]{1,0:T(8,128)(2,1)S(1)} collective-permute-done((bf16[256,768]{1,0:T(8,128)(2,1)S(1)}, bf16[256,768]{1,0:T(8,128)(2,1)S(1)}, u32[]{:S(2)}, u32[]{:S(2)}) %collective-permute-start.110) | collective-permute-done | bytes 393248 | tf_op jit(solution)/shard_map/ppermute | solution.py:84
  (650 shorter events, 394.0 us)
Async XLA Ops:
  7.2 192.6 %all-gather.4.cloned.1.call-start = ((), (), s32[]{:S(2)}) async-start(), calls=%async_computation.8 | async-start | bytes 11141120 | tf_op jit(solution)/shard_map/all_gather | solution.py:116
  43.0 32.3 %collective-permute-start.11 = (bf16[544,640]{1,0:T(8,128)(2,1)}, bf16[544,640]{1,0:T(8,128)(2,1)}, u32[]{:S(2)}, u32[]{:S(2)}) collective-permute-start(bf16[544,640]{1,0:T(8,128)(2,1)} %get-tuple-element.162.refs_8_), channel_id=1, source_target_pairs={{16,0},{32,16},{48,32},{0,48},{17,1},{33,17},{49,33},{1,49},{18,2}... | collective-permute-start | bytes 2088968 | tf_op jit(solution)/shard_map/ppermute | solution.py:72
  51.3 54.0 %collective-permute-start.27 = (bf16[256,2176]{1,0:T(8,128)(2,1)}, bf16[256,2176]{1,0:T(8,128)(2,1)}, u32[]{:S(2)}, u32[]{:S(2)}) collective-permute-start(bf16[256,2176]{1,0:T(8,128)(2,1)} %chip_rows_kernel.1.own_ref), channel_id=1, source_target_pairs={{0,8},{8,0},{1,9},{9,1},{2,10},{10,2},{3,11},{11,3},{4,12},{12,4},... | collective-permute-start | bytes 3342344 | tf_op jit(solution)/shard_map/ppermute | solution.py:80
  52.6 52.7 %collective-permute-start.28 = (bf16[256,2176]{1,0:T(8,128)(2,1)}, bf16[256,2176]{1,0:T(8,128)(2,1)}, u32[]{:S(2)}, u32[]{:S(2)}) collective-permute-start(bf16[256,2176]{1,0:T(8,128)(2,1)} %chip_rows_kernel.1.own_ref), channel_id=1, source_target_pairs={{0,72},{72,0},{8,64},{64,8},{1,73},{73,1},{9,65},{65,9},{2,74},{74... | collective-permute-start | bytes 3342344 | tf_op jit(solution)/shard_map/ppermute | solution.py:88
  54.5 50.8 %collective-permute-start.29 = (bf16[256,2176]{1,0:T(8,128)(2,1)}, bf16[256,2176]{1,0:T(8,128)(2,1)}, u32[]{:S(2)}, u32[]{:S(2)}) collective-permute-start(bf16[256,2176]{1,0:T(8,128)(2,1)} %chip_rows_kernel.1.own_ref), channel_id=1, source_target_pairs={{0,64},{64,0},{1,65},{65,1},{2,66},{66,2},{3,67},{67,3},{4,68},{68... | collective-permute-start | bytes 3342344 | tf_op jit(solution)/shard_map/ppermute | solution.py:84
  116.1 124.1 %all-gather.6.cloned.1.call-start = ((), (), s32[]{:S(2)}) async-start(), calls=%async_computation.9 | async-start | bytes 3481600 | tf_op jit(solution)/shard_map/all_gather | solution.py:116
  136.5 194.7 %all-gather.8.cloned.1.call-start = ((), (), s32[]{:S(2)}) async-start(), calls=%async_computation.10 | async-start | bytes 11141120 | tf_op jit(solution)/shard_map/all_gather | solution.py:116
  149.5 342.1 %reduce-scatter.5.cloned.1.call-start = ((), (), s32[]{:S(2)}) async-start(), calls=%async_computation.11 | async-start | bytes 11141120 | tf_op jit(solution)/shard_map/reduce_scatter | solution.py:120
  295.7 50.8 %collective-permute-start.61 = (bf16[32,2048]{1,0:T(8,128)(2,1)S(1)}, bf16[32,2048]{1,0:T(8,128)(2,1)}, u32[]{:S(2)}, u32[]{:S(2)}) collective-permute-start(bf16[32,2048]{1,0:T(8,128)(2,1)S(1)} %dynamic-slice_bitcast_fusion.refs_0_.after_ref), channel_id=1, source_target_pairs={{0,4},{4,0},{1,5},{5,1},{2,6},{6,2},{3,7},{7,3},{8,12},{12,8},{9,1... | collective-permute-start | bytes 393224 | tf_op jit(solution)/shard_map/ppermute | solution.py:76
  298.1 33.0 %collective-permute-start.52 = (bf16[32,2048]{1,0:T(8,128)(2,1)}, bf16[32,2048]{1,0:T(8,128)(2,1)}, u32[]{:S(2)}, u32[]{:S(2)}) collective-permute-start(bf16[32,2048]{1,0:T(8,128)(2,1)} %collective-permute-done.48.refs_3_), channel_id=1, source_target_pairs={{0,4},{4,0},{1,5},{5,1},{2,6},{6,2},{3,7},{7,3},{8,12},{12,8},{9,1... | collective-permute-start | bytes 393224 | tf_op jit(solution)/shard_map/ppermute | solution.py:76
  299.9 46.6 %collective-permute-start.62 = (bf16[32,2048]{1,0:T(8,128)(2,1)}, bf16[32,2048]{1,0:T(8,128)(2,1)}, u32[]{:S(2)}, u32[]{:S(2)}) collective-permute-start(bf16[32,2048]{1,0:T(8,128)(2,1)} %collective-permute-done.58.refs_1_), channel_id=1, source_target_pairs={{0,4},{4,0},{1,5},{5,1},{2,6},{6,2},{3,7},{7,3},{8,12},{12,8},{9,1... | collective-permute-start | bytes 393224 | tf_op jit(solution)/shard_map/ppermute | solution.py:76
  300.6 46.0 %collective-permute-start.63 = (bf16[32,2048]{1,0:T(8,128)(2,1)}, bf16[32,2048]{1,0:T(8,128)(2,1)}, u32[]{:S(2)}, u32[]{:S(2)}) collective-permute-start(bf16[32,2048]{1,0:T(8,128)(2,1)} %collective-permute-done.59.refs_2_), channel_id=1, source_target_pairs={{0,4},{4,0},{1,5},{5,1},{2,6},{6,2},{3,7},{7,3},{8,12},{12,8},{9,1... | collective-permute-start | bytes 393224 | tf_op jit(solution)/shard_map/ppermute | solution.py:76
  301.7 44.8 %collective-permute-start.64 = (bf16[32,2048]{1,0:T(8,128)(2,1)}, bf16[32,2048]{1,0:T(8,128)(2,1)}, u32[]{:S(2)}, u32[]{:S(2)}) collective-permute-start(bf16[32,2048]{1,0:T(8,128)(2,1)} %collective-permute-done.60.refs_3_), channel_id=1, source_target_pairs={{0,4},{4,0},{1,5},{5,1},{2,6},{6,2},{3,7},{7,3},{8,12},{12,8},{9,1... | collective-permute-start | bytes 393224 | tf_op jit(solution)/shard_map/ppermute | solution.py:76
  362.1 196.8 %reduce-scatter.9.cloned.1.call-start = ((), (), s32[]{:S(2)}) async-start(), calls=%async_computation.13 | async-start | bytes 11141120 | tf_op jit(solution)/shard_map/reduce_scatter | solution.py:120
  475.0 155.3 %reduce-scatter.7.cloned.1.call-start = ((), (), s32[]{:S(2)}) async-start(), calls=%async_computation.12 | async-start | bytes 3932160 | tf_op jit(solution)/shard_map/reduce_scatter | solution.py:120
  475.6 163.9 %reduce-scatter.11.cloned.1.call-start = ((), (), s32[]{:S(2)}) async-start(), calls=%async_computation.14 | async-start | bytes 3932160 | tf_op jit(solution)/shard_map/reduce_scatter | solution.py:120
  550.5 25.3 %collective-permute-start.100 = (bf16[128,2048]{1,0:T(8,128)(2,1)}, bf16[128,2048]{1,0:T(8,128)(2,1)}, u32[]{:S(2)}, u32[]{:S(2)}) collective-permute-start(bf16[128,2048]{1,0:T(8,128)(2,1)} %copy-done.153), channel_id=1, source_target_pairs={{0,4},{4,0},{1,5},{5,1},{2,6},{6,2},{3,7},{7,3},{8,12},{12,8},{9,1... | collective-permute-start | bytes 1572872 | tf_op jit(solution)/shard_map/ppermute | solution.py:76
  565.9 64.4 %collective-permute-start.104 = (bf16[256,2176]{1,0:T(8,128)(2,1)}, bf16[256,2176]{1,0:T(8,128)(2,1)}, u32[]{:S(2)}, u32[]{:S(2)}) collective-permute-start(bf16[256,2176]{1,0:T(8,128)(2,1)} %get-tuple-element.281), channel_id=1, source_target_pairs={{0,8},{8,0},{1,9},{9,1},{2,10},{10,2},{3,11},{11,3},{4,12},{12,4},... | collective-permute-start | bytes 3342344 | tf_op jit(solution)/shard_map/ppermute | solution.py:80
  567.1 63.2 %collective-permute-start.105 = (bf16[256,2176]{1,0:T(8,128)(2,1)}, bf16[256,2176]{1,0:T(8,128)(2,1)}, u32[]{:S(2)}, u32[]{:S(2)}) collective-permute-start(bf16[256,2176]{1,0:T(8,128)(2,1)} %get-tuple-element.282), channel_id=1, source_target_pairs={{0,72},{72,0},{8,64},{64,8},{1,73},{73,1},{9,65},{65,9},{2,74},{74... | collective-permute-start | bytes 3342344 | tf_op jit(solution)/shard_map/ppermute | solution.py:88
  569.6 60.7 %collective-permute-start.106 = (bf16[256,2176]{1,0:T(8,128)(2,1)}, bf16[256,2176]{1,0:T(8,128)(2,1)}, u32[]{:S(2)}, u32[]{:S(2)}) collective-permute-start(bf16[256,2176]{1,0:T(8,128)(2,1)} %get-tuple-element.283), channel_id=1, source_target_pairs={{0,64},{64,0},{1,65},{65,1},{2,66},{66,2},{3,67},{67,3},{4,68},{68... | collective-permute-start | bytes 3342344 | tf_op jit(solution)/shard_map/ppermute | solution.py:84
  573.0 47.4 %collective-permute-start.57 = (bf16[32,2048]{1,0:T(8,128)(2,1)S(1)}, bf16[32,2048]{1,0:T(8,128)(2,1)S(1)}, u32[]{:S(2)}, u32[]{:S(2)}) collective-permute-start(bf16[32,2048]{1,0:T(8,128)(2,1)S(1)} %broadcast_select_fusion.3), channel_id=1, source_target_pairs={{0,64},{64,0},{1,65},{65,1},{2,66},{66,2},{3,67},{67,3},{4,68},{68... | collective-permute-start | bytes 393224 | tf_op jit(solution)/shard_map/ppermute | solution.py:84
  578.1 45.2 %collective-permute-start.101 = (bf16[32,2048]{1,0:T(8,128)(2,1)S(1)}, bf16[32,2048]{1,0:T(8,128)(2,1)S(1)}, u32[]{:S(2)}, u32[]{:S(2)}) collective-permute-start(bf16[32,2048]{1,0:T(8,128)(2,1)S(1)} %get-tuple-element.274), channel_id=1, source_target_pairs={{3,0},{0,1},{1,2},{2,3},{7,4},{4,5},{5,6},{6,7},{11,8},{8,9},{9,10... | collective-permute-start | bytes 393224 | tf_op jit(solution)/shard_map/ppermute | solution.py:68
  646.3 22.3 %collective-permute-start.107 = (bf16[32,2048]{1,0:T(8,128)(2,1)S(1)}, bf16[32,2048]{1,0:T(8,128)(2,1)S(1)}, u32[]{:S(2)}, u32[]{:S(2)}) collective-permute-start(bf16[32,2048]{1,0:T(8,128)(2,1)S(1)} %select_convert_fusion), channel_id=1, source_target_pairs={{0,64},{64,0},{1,65},{65,1},{2,66},{66,2},{3,67},{67,3},{4,68},{68... | collective-permute-start | bytes 393224 | tf_op jit(solution)/shard_map/ppermute | solution.py:84
  654.1 21.6 %collective-permute-start.115 = (bf16[128,2176]{1,0:T(8,128)(2,1)S(1)}, bf16[128,2176]{1,0:T(8,128)(2,1)S(1)}, u32[]{:S(2)}, u32[]{:S(2)}) collective-permute-start(bf16[128,2176]{1,0:T(8,128)(2,1)S(1)} %get-tuple-element.305), channel_id=1, source_target_pairs={{0,4},{4,0},{1,5},{5,1},{2,6},{6,2},{3,7},{7,3},{8,12},{12,8},{9,1... | collective-permute-start | bytes 1671176 | tf_op jit(solution)/shard_map/ppermute | solution.py:76
  (265 other events, 2056.6 us)
Sparse Core Ops, SparseCore 0:
  111.3 88.4 all-gather.3
  201.5 37.4 all-gather.5
  240.7 90.4 all-gather.7
  362.3 87.0 reduce-scatter.4
  475.1 83.7 reduce-scatter.8
  561.2 37.9 reduce-scatter.6
  601.5 37.9 reduce-scatter.10

commit v3 on v2

--- a/solution.py
+++ b/solution.py
@@ -14,7 +14,7 @@
 MASKED = -1e30
 KEYS_STEP = 512
 AXES = ("section", "x", "ylo", "core", "tp")
-SECTION, X, YLO, CORE, TP = range(5)
+SECTION, _, YLO, CORE, TP = range(5)
 BF16 = jnp.bfloat16
 F32 = jnp.float32
 VMEM = pl.BlockSpec(memory_space=pltpu.VMEM)
@@ -42,34 +42,43 @@
 SHORT = pl.CostEstimate(flops=1, bytes_accessed=1, transcendentals=0)
 
 
-def call(kernel, outs, args, scratch=(), room=8, spec=VMEM, out_spec=VMEM):
-    specs = []
+def held(dims, dtype=BF16):
+    return pltpu.HBM(tuple(dims), dtype)
+
+
+def pinned(v):
+    return pltpu.with_memory_space_constraint(v, pltpu.HBM)
+
+
+def call(kernel, outs, args, scratch=(), room=8, out_spec=None):
+    specs, values = [], []
     for a in args:
-        own = SMEM if not isinstance(a, list) and a.dtype == jnp.int32 else spec
-        specs += [HBM] * len(a) if isinstance(a, list) else [own]
-    args = [v for a in args for v in (a if isinstance(a, list) else [a])]
-    held = [m for m in scratch if isinstance(m, pltpu.VMEM((8, 128), F32).__class__)]
+        if isinstance(a, (list, tuple)):
+            specs += [HBM if isinstance(a, list) else pl.BlockSpec()] * len(a)
+            values += [pinned(v) for v in a]
+        else:
+            specs.append(SMEM if a.dtype == jnp.int32 else VMEM)
+            values.append(a)
+    mine = [m for m in scratch if isinstance(m, type(pltpu.VMEM((8, 128), F32)))]
     room = room * 2**20 + sum(
-        math.prod(m.shape) * jnp.dtype(m.dtype).itemsize for m in held if m.dtype in (BF16, F32)
+        math.prod(m.shape) * jnp.dtype(m.dtype).itemsize for m in mine if m.dtype in (BF16, F32)
     )
     return pl.pallas_call(
         kernel,
         out_shape=tuple(outs),
         in_specs=specs,
-        out_specs=(out_spec,) * len(outs),
+        out_specs=tuple(
+            VMEM if isinstance(o, jax.ShapeDtypeStruct) else out_spec or pl.BlockSpec() for o in outs
+        ),
         scratch_shapes=list(scratch),
         compiler_params=pltpu.CompilerParams(vmem_limit_bytes=room),
         cost_estimate=SHORT,
         name=getattr(kernel, "func", kernel).__name__,
-    )(*args)
+    )(*values)
 
 
 def from_z(rows, by):
     return lax.ppermute(rows, "tp", [((i + by) % 4, i) for i in range(4)])
-
-
-def from_x(v, by):
-    return lax.ppermute(v, "x", [((i + by) % 4, i) for i in range(4)])
 
 
 def swap_core(v):
@@ -110,6 +119,11 @@
 def reduce_rows(send, mine):
     own, *pieces = split(mine, swap_core(send))
     return [own] + [from_z(p, -k) for k, p in zip((1, 2, 3), pieces)]
+
+
+def summands(send, mine):
+    own, *others = reduce_rows(send, mine)
+    return [(own,), *others]
 
 
 def gather_x(block):
@@ -159,7 +173,7 @@
 
 def chip_rows(place, own, other):
     n, c = own.shape
-    return call(chip_rows_kernel, [shape((2 * n, c))], [place, own, other])[0]
+    return call(chip_rows_kernel, [held((2 * n, c))], [place, (own, other)], room=12)[0]
 
 
 def chip_attn_kernel(place, own_ref, other_ref, out_ref):
@@ -195,10 +209,27 @@
         fill(p1_ref, p0_ref)
 
 
+def both_pairs_kernel(place, own_ref, near_ref, far_ref, straight_ref, out_ref):
+    n = own_ref.shape[0]
+    mine, other, here = 2 * place[SECTION], 2 - 2 * place[SECTION], place[YLO]
+    for src, at in (
+        (own_ref, mine + here),
+        (near_ref, mine + 1 - here),
+        (straight_ref, other + here),
+        (far_ref, other + 1 - here),
+    ):
+        out_ref[pl.ds(pl.multiple_of(at * n, n), n), :] = src[...]
+
+
+def both_pairs(place, own, others):
+    n, c = own.shape
+    return call(both_pairs_kernel, [held((4 * n, c))], [place, (own, *others)], room=16)[0]
+
+
 def pairs(place, own, others):
     n, c = own.shape
-    out = shape((2 * n, c))
-    return call(pairs_kernel, [out, out], [place, own, *others])
+    out = held((2 * n, c))
+    return call(pairs_kernel, [out, out], [place, (own, *others)], room=20)
 
 
 def fetch(pieces, whole, sems):
@@ -217,6 +248,30 @@
     return wait
 
 
+def block_row(pack, layer, i):
+    return (i // 2 * 4 + 2 * layer + i % 2) * (pack.shape[0] // 16)
+
+
+def fetch_blocks(pack, layer, column, whole, sems):
+    n, c = whole.shape[0] // 8, whole.shape[1]
+    copies = [
+        pltpu.make_async_copy(
+            pack.at[pl.ds(block_row(pack, layer, i), n), pl.ds(column, c)],
+            whole.at[pl.ds(i * n, n), :],
+            sems.at[i],
+        )
+        for i in range(8)
+    ]
+    for c in copies:
+        c.start()
+
+    def wait():
+        for c in copies:
+            c.wait()
+
+    return wait
+
+
 def rms(rows):
     return lax.rsqrt(jnp.mean(rows * rows, axis=-1, keepdims=True) + EPS)
 
@@ -255,7 +310,7 @@
 
 def split(mine, other):
     n, d = mine.shape[0] // 4, mine.shape[1]
-    return call(split_kernel, [shape((n, d), F32)] + [shape((n, d))] * 3, [mine, other])
+    return call(split_kernel, [held((n, d), F32)] + [shape((n, d))] * 3, [(mine,), other])
 
 
 def total_of(refs):
@@ -286,33 +341,25 @@
     low_ref[...] = dx.astype(BF16)
 
 
-def qkv_kernel(place, *refs, parts):
-    pieces, refs = refs[:8], refs[8:]
-    weights, refs = refs[:parts], refs[parts:]
-    cos_ref, sin_ref, x_ref, a_ref, q_ref, kv_ref, w_ref, wo_ref, ga_ref, gf_ref, *refs = refs
-    gains_ref, x_sems, w_sems = refs
+def qkv_kernel(place, *refs, layer):
+    pieces, pack, refs = refs[:8], refs[8], refs[9:]
+    cos_ref, sin_ref, x_ref, a_ref, q_ref, kv_ref, ga_ref, gf_ref, *refs = refs
+    w_ref, gains_ref, x_sems, w_sems, g_sems = refs
     rows_there = fetch(pieces, x_ref, x_sems)
     n = w_ref.shape[0] // 8
-    step = n + GAIN_ROWS
-
-    def copies(i, block):
-        src, at = (weights[0], i * step) if parts == 1 else (weights[i // 2], i % 2 * step)
-        rows = pl.ds(pl.multiple_of(block * n, n), n)
-        cols, m = w_ref.shape[1], wo_ref.shape[1]
-        sides = (
-            (src.at[pl.ds(at, n), pl.ds(0, cols)], w_ref.at[rows, :]),
-            (src.at[pl.ds(at, n), pl.ds(cols, m)], wo_ref.at[rows, :]),
-            (src.at[pl.ds(at + n, GAIN_ROWS), pl.ds(0, n)], gains_ref.at[block]),
-        )
-        return [pltpu.make_async_copy(a, b, w_sems.at[i, j]) for j, (a, b) in enumerate(sides)]
-
-    for i in range(8):
-        block = i if parts == 1 else lax.rem(place[X] + i // 2, 4) * 2 + i % 2
-        for c in copies(i, block):
-            c.start()
-    for i in range(8):
-        for c in copies(i, i):
-            c.wait()
+    gain_copies = [
+        pltpu.make_async_copy(
+            pack.at[pl.ds(block_row(pack, layer, i) + n, GAIN_ROWS), pl.ds(0, n)],
+            gains_ref.at[i],
+            g_sems.at[i],
+        )
+        for i in range(8)
+    ]
+    for c in gain_copies:
+        c.start()
+    weights_there = fetch_blocks(pack, layer, 0, w_ref, w_sems)
+    for c in gain_copies:
+        c.wait()
     gains = jnp.concatenate([gains_ref[i] for i in range(8)], axis=1).astype(F32)
     ga_ref[...] = gains[0:1, :]
     gf_ref[...] = gains[1:2, :]
@@ -320,6 +367,7 @@
     x = x_ref[...].astype(F32)
     a = (x * rms(x) * ga_ref[...]).astype(BF16)
     a_ref[...] = a
+    weights_there()
     out = rope(nn(a, w_ref[...]), cos_ref[...], sin_ref[...])
     width = q_ref.shape[1]
     q_ref[...] = (out[:, :width].astype(BF16).astype(F32) * HD**-0.5).astype(BF16)
@@ -335,10 +383,9 @@
     return pl.ds(t % per * KEYS_STEP, KEYS_STEP), slice(t // per * HD, (t // per + 1) * HD)
 
 
-def attend_kernel(place, q_ref, own_ref, other_ref, bias_ref, w_hbm, *refs):
-    o_ref, lse_ref, k_ref, v_ref, send_ref, mine_ref, s_ref, w_ref, sem = refs
-    load = pltpu.make_async_copy(w_hbm, w_ref, sem)
-    load.start()
+def attend_kernel(place, q_ref, own_ref, other_ref, bias_ref, pack, *refs, layer):
+    o_ref, lse_ref, k_ref, v_ref, send_ref, mine_ref, s_ref, w_ref, sems = refs
+    weights_there = fetch_blocks(pack, layer, pack.shape[1] - w_ref.shape[1], w_ref, sems)
     odd = place[CORE] == 1
     k_ref[...] = jnp.where(odd, other_ref[...], own_ref[...])
     v_ref[...] = jnp.where(odd, own_ref[...], other_ref[...])
@@ -368,7 +415,7 @@
     flat = jnp.concatenate([outs[h] / sums[h] for h in range(heads)], axis=0)
     o_ref[...] = flat.T.astype(BF16)
     lse_ref[...] = jnp.concatenate([tops[h] + jnp.log(sums[h]) for h in range(heads)], axis=0)
-    load.wait()
+    weights_there()
     halves_out(nt(o_ref[...], w_ref[...]), send_ref, mine_ref)
 
 
@@ -425,18 +472,17 @@
     halves_out(nt(dgu_ref[...], gu_w[...]), send_ref, mine_ref)
 
 
-def attend_back_kernel(place, *refs):
+def attend_back_kernel(place, *refs, layer):
     pieces, refs = refs[:8], refs[8:]
-    w_hbm, q_ref, k_ref, v_ref, bias_ref, o_ref, lse_ref, cos_ref, sin_ref, *refs = refs
-    dattn_ref, dq_ref, own_ref, send_ref, w_ref, do_ref, dk_ref, dv_ref, sem, r_sems = refs
+    pack, q_ref, k_ref, v_ref, bias_ref, o_ref, lse_ref, cos_ref, sin_ref, *refs = refs
+    dattn_ref, dq_ref, own_ref, send_ref, w_ref, do_ref, dk_ref, dv_ref, sems, r_sems = refs
     rows_there = fetch(pieces, dattn_ref, r_sems)
-    load = pltpu.make_async_copy(w_hbm, w_ref, sem)
-    load.start()
+    weights_there = fetch_blocks(pack, layer, pack.shape[1] - w_ref.shape[1], w_ref, sems)
     rows, width = q_ref.shape
     heads = width // HD
     steps = 2 * k_ref.shape[0] // KEYS_STEP
     rows_there()
-    load.wait()
+    weights_there()
     do = nn(dattn_ref[...], w_ref[...])
     do_ref[...] = do.astype(BF16)
     both = (do_ref[...].astype(F32) * o_ref[...].astype(F32)).T
@@ -474,11 +520,10 @@
     out_ref[...] = (own_ref[...] + other_ref[...].astype(F32)).astype(BF16)
 
 
-def qkv_back_kernel(place, w_hbm, x_hbm, dq_ref, kv_ref, cos_ref, sin_ref, *refs):
-    dqkv_ref, send_ref, mine_ref, gain_grad_ref, w_ref, x_ref, sems = refs
-    load = pltpu.make_async_copy(w_hbm, w_ref, sems.at[0])
-    load.start()
-    rows_there = pltpu.make_async_copy(x_hbm, x_ref, sems.at[1])
+def qkv_back_kernel(place, pack, x_hbm, dq_ref, kv_ref, cos_ref, sin_ref, *refs, layer):
+    dqkv_ref, send_ref, mine_ref, gain_grad_ref, w_ref, x_ref, sems, x_sem = refs
+    weights_there = fetch_blocks(pack, layer, 0, w_ref, sems)
+    rows_there = pltpu.make_async_copy(x_hbm, x_ref, x_sem)
     rows_there.start()
     width, odd = dq_ref.shape[1], place[CORE] == 1
     both = sum((kv_ref[i].astype(F32) for i in range(1, 8)), kv_ref[0].astype(F32))
@@ -492,7 +537,7 @@
     dkv = rope_back(dkv, cos_ref[:, width:], sin_ref[:, width:])
     dqkv_ref[:, :width] = dq_ref[...]
     dqkv_ref[:, width:] = dkv.astype(BF16)
-    load.wait()
+    weights_there()
     da = nt(dqkv_ref[...], w_ref[...])
     halves_out(da, send_ref, mine_ref)
     rows_there.wait()
@@ -500,57 +545,63 @@
     gain_grad_ref[...] = jnp.sum(da * (x * rms(x)), axis=0, keepdims=True)
 
 
-def ffn_product_kernel(b_ref, dgu_ref, dff_ref, h_ref, out_ref):
-    n = dgu_ref.shape[1]
-    out_ref[:, :n] = tn(b_ref[...], dgu_ref[...]).astype(BF16)
-    out_ref[:, n:] = tn(dff_ref[...], h_ref[...]).astype(BF16)
+def ffn_product_kernel(b_ref, dgu_ref, dff_ref, h_ref, out, whole, sems):
+    n, steps = dgu_ref.shape[1], sems.shape[0]
+    rows = whole.shape[0] // steps
+    copies = []
+    for i in range(steps):
+        at = slice(i * rows, (i + 1) * rows)
+        whole[at, :n] = tn(b_ref[:, at], dgu_ref[...]).astype(BF16)
+        whole[at, n:] = tn(dff_ref[:, at], h_ref[...]).astype(BF16)
+        here = pl.ds(i * rows, rows)
+        copies.append(pltpu.make_async_copy(whole.at[here, :], out.at[here, :], sems.at[i]))
+        copies[-1].start()
+    for c in copies:
+        c.wait()
 
 
 def ffn_products(b, dgu, dff, hidden):
-    rows, d = b.shape
-    n, wide = 256, dgu.shape[1] + hidden.shape[1]
-    left = pl.BlockSpec((rows, n), lambda i: (0, i))
-    return pl.pallas_call(
+    dims = (b.shape[1], dgu.shape[1] + hidden.shape[1])
+    return call(
         ffn_product_kernel,
-        out_shape=shape((d, wide)),
-        grid=(d // n,),
-        in_specs=[
-            left,
-            pl.BlockSpec(dgu.shape, lambda i: (0, 0)),
-            left,
-            pl.BlockSpec(hidden.shape, lambda i: (0, 0)),
-        ],
-        out_specs=pl.BlockSpec((n, wide), lambda i: (i, 0)),
-        compiler_params=pltpu.CompilerParams(vmem_limit_bytes=16 * 1024 * 1024),
-        cost_estimate=SHORT,
-        name="ffn_product_kernel",
-    )(b, dgu, dff, hidden)
-
-
-def attn_product_kernel(dattn, a, gg_a, gg_f, ctx, dqkv, out):
-    m = ctx.shape[1]
+        [pltpu.HBM(dims, BF16)],
+        [(b, dgu, dff, hidden)],
+        [pltpu.VMEM(dims, BF16), DMA((8,))],
+        room=14,
+        out_spec=HBM,
+    )[0]
+
+
+def attn_product_kernel(dattn, a, gg_a, gg_f, ctx, dqkv, out, whole, sems):
+    m, steps = ctx.shape[1], sems.shape[0]
     wide = m + dqkv.shape[1]
-    out[:, :m] = tn(dattn[...], ctx[...]).astype(BF16)
-    out[:, m:wide] = tn(a[...], dqkv[...]).astype(BF16)
-    row = lax.broadcasted_iota(jnp.int32, (out.shape[1] - wide, a.shape[1]), 0)
-    ga, gf = (jnp.broadcast_to(g[...], row.shape) for g in (gg_a, gg_f))
-    out[:, wide:] = jnp.where(row == 0, ga, jnp.where(row == 1, gf, 0.0)).T.astype(BF16)
+    rows = whole.shape[0] // steps
+    row = lax.broadcasted_iota(jnp.int32, (whole.shape[1] - wide, rows), 0)
+    copies = []
+    for i in range(steps):
+        at = slice(i * rows, (i + 1) * rows)
+        whole[at, :m] = tn(dattn[:, at], ctx[...]).astype(BF16)
+        whole[at, m:wide] = tn(a[:, at], dqkv[...]).astype(BF16)
+        ga, gf = (jnp.broadcast_to(g[:, at], row.shape) for g in (gg_a, gg_f))
+        gains = jnp.where(row == 0, ga, jnp.where(row == 1, gf, 0.0))
+        whole[at, wide:] = gains.T.astype(BF16)
+        here = pl.ds(i * rows, rows)
+        copies.append(pltpu.make_async_copy(whole.at[here, :], out.at[here, :], sems.at[i]))
+        copies[-1].start()
+    for c in copies:
+        c.wait()
 
 
 def attn_products(dattn, ctx, a, dqkv, gg_a, gg_f):
-    rows, d = a.shape
-    n, wide = 512, ctx.shape[1] + dqkv.shape[1] + 128
-    by_columns = [pl.BlockSpec((v.shape[0], n), lambda i: (0, i)) for v in (dattn, a, gg_a, gg_f)]
-    return pl.pallas_call(
+    dims = (a.shape[1], ctx.shape[1] + dqkv.shape[1] + 128)
+    return call(
         attn_product_kernel,
-        out_shape=shape((d, wide)),
-        grid=(d // n,),
-        in_specs=by_columns + [pl.BlockSpec(v.shape, lambda i: (0, 0)) for v in (ctx, dqkv)],
-        out_specs=pl.BlockSpec((n, wide), lambda i: (i, 0)),
-        compiler_params=pltpu.CompilerParams(vmem_limit_bytes=16 * 1024 * 1024),
-        cost_estimate=SHORT,
-        name="attn_product_kernel",
-    )(dattn, a, gg_a, gg_f, ctx, dqkv)
+        [pltpu.HBM(dims, BF16)],
+        [(dattn, a, gg_a, gg_f, ctx, dqkv)],
+        [pltpu.VMEM(dims, BF16), DMA((4,))],
+        room=14,
+        out_spec=HBM,
+    )[0]
 
 
 def y_split_kernel(place, r0_ref, r1_ref, keep_ref, near_ref, far_ref, straight_ref):
@@ -584,13 +635,15 @@
 
 def by_core(parts, place):
     n, c = parts[0].shape[0] // 2, parts[0].shape[1]
-    own, send = call(by_core_kernel, [shape((n, c), F32), shape((n, c))], [place, *parts])
+    own, send = call(
+        by_core_kernel, [held((n, c), F32), shape((n, c))], [place, tuple(parts)], room=16
+    )
     return own, swap_core(send)
 
 
 def reduce_y(r0, r1, place):
     n, c = r0.shape[0] // 2, r0.shape[1]
-    keep, near, far, straight = call(y_split_kernel, [shape((n, c))] * 4, [place, r0, r1])
+    keep, near, far, straight = call(y_split_kernel, [held((n, c))] * 4, [place, (r0, r1)], room=16)
     return [keep, swap_ylo(near), swap_across(far), swap_section(straight)]
 
 
@@ -657,27 +710,23 @@
     attn_own, attn_send = call(
         pack_attn_kernel,
         [shape(attn_dims)] * 2,
-        [place, w_query[0], w_key[0], w_value[0], w_out[0], attn_gain, ffn_gain],
-        spec=pl.BlockSpec(),
+        [place, (w_query[0], w_key[0], w_value[0], w_out[0], attn_gain, ffn_gain)],
     )
     attn_shard = call(
         chip_attn_kernel,
-        [shape((2 * own_rows + GAIN_ROWS, attn_dims[1]))],
-        [place, attn_own, swap_core(attn_send)],
+        [held((2 * own_rows + GAIN_ROWS, attn_dims[1]))],
+        [place, (attn_own, swap_core(attn_send))],
     )[0]
-    attn_y = y_exchange(attn_shard)
-    attn_pairs = pairs(place, attn_shard, attn_y)
-    attn0 = [attn_pairs[0]] + [from_x(attn_pairs[0], k) for k in (1, 2, 3)]
-
     ffn_own, ffn_send = call(
         pack_ffn_kernel,
         [shape((own_rows, 2 * units + padded))] * 2,
-        [place, w_down[0], after(w_gate, attn_y[0])[0], w_up[0]],
-        room=12,
-        spec=pl.BlockSpec(),
+        [place, (w_down[0], w_gate[0], w_up[0])],
+        room=16,
     )
     ffn_shard = chip_rows(place, ffn_own, swap_core(ffn_send))
-    ffn_y = y_exchange(after(ffn_shard, attn_pairs[0]))
+    attn_y = y_exchange(after(attn_shard, ffn_shard))
+    w_attn = gather_x(both_pairs(place, attn_shard, attn_y))
+    ffn_y = y_exchange(ffn_shard)
 
     block = at["x"] * 2 + at["ylo"]
     seg_row = lax.dynamic_index_in_dim(seg_ids, section, 0, keepdims=False)
@@ -705,37 +754,40 @@
     cos, sin = (jnp.concatenate([t] * 12, axis=1) for t in (jnp.cos(angles), jnp.sin(angles)))
     cos, sin = jnp.where(plain, 1.0, cos), jnp.where(plain, 0.0, sin)
 
-    rows_low, rows_f32 = shape((micro_rows, d)), shape((micro_rows, d), F32)
-    all_low = shape((group, d))
-    partials = [shape((group // 2, d)), shape((group // 2, d), F32)]
+    rows_low = shape((micro_rows, d))
+    mid_outs = [held((micro_rows, d), F32), rows_low]
+    partials = [shape((group // 2, d)), held((group // 2, d), F32)]
     heads, keys = q_width // HD, seg_row.shape[0]
     gain_row = shape((1, d), F32)
 
-    def project(x, qkv_w):
+    def project(x, layer):
         return call(
-            functools.partial(qkv_kernel, parts=len(qkv_w)),
-            [all_low, all_low, shape((group, q_width)), shape((group // 2, 2 * HD))]
-            + [shape((d, wide)), shape((d, q_width)), gain_row, gain_row],
-            [place, gather_rows(x) + qkv_w, cos, sin],
+            functools.partial(qkv_kernel, layer=layer),
+            [held((group, d))] * 2
+            + [shape((group, q_width)), shape((group // 2, 2 * HD))]
+            + [gain_row, gain_row],
+            [place, gather_rows(x) + [w_attn], cos, sin],
             [
+                pltpu.VMEM((d, wide), BF16),
                 pltpu.VMEM((8, GAIN_ROWS, d // 8), BF16),
                 DMA((8,)),
-                DMA((8, 3)),
+                DMA((8,)),
+                DMA((8,)),
             ],
-            room=14,
-        )
-
-    both_kv = shape((keys // 2, 2 * HD))
-
-    def attention(q, kv, w_out):
+            room=18,
+        )
+
+    both_kv = held((keys // 2, 2 * HD))
+
+    def attention(q, kv, layer):
         return call(
-            attend_kernel,
-            [shape((group, q_width)), shape((heads, group), F32), both_kv, both_kv, *partials],
-            [place, q, *kv, bias, [w_out]],
+            functools.partial(attend_kernel, layer=layer),
+            [held((group, q_width)), held((heads, group), F32), both_kv, both_kv, *partials],
+            [place, q, *kv, bias, [w_attn]],
             [
                 pltpu.VMEM((heads, keys, group), F32),
                 pltpu.VMEM((d, q_width), BF16),
-                DMA,
+                DMA((8,)),
             ],
             room=12,
         )
@@ -743,7 +795,7 @@
     def feed_forward(b, w_ffn):
         return call(
             ffn_kernel,
-            [all_low, shape((group, 2 * units), F32), shape((group, padded)), *partials],
+            [held((group, d)), held((group, 2 * units), F32), held((group, padded)), *partials],
             [[*gather_rows(b), w_ffn]],
             [
                 pltpu.VMEM((d, 2 * units), BF16),
@@ -752,14 +804,15 @@
                 DMA((4,)),
                 DMA,
             ],
-            room=12,
-        )
-
-    def backward(dy, kept, early=()):
-        x, rows, qkv_w, a, q, k, v, ctx, lse, mid, b, gu, hidden, gain_a, gain_f, w_ffn, w_out = kept
+            room=16,
+        )
+
+    def backward(dy, kept, layer, pending=None):
+        x, rows, a, q, k, v, ctx, lse, mid, b, gu, hidden, gain_a, gain_f, w_ffn = kept
+        other = pending and reduce_x(after(pending[0], *pending[1:], dy))
         dff, dgu, send, mine = call(
             ffn_back_kernel,
-            [all_low, shape((group, 2 * units)), *partials],
+            [held((group, d)), held((group, 2 * units)), *partials],
             [[*gather_rows(dy), w_ffn, gu]],
             [
                 pltpu.VMEM((d, 2 * units), BF16),
@@ -768,81 +821,96 @@
                 DMA((8,)),
                 DMA((3,)),
             ],
-            room=12,
+            room=16,
         )
         g_ffn = ffn_products(b, dgu, dff, hidden)
         dmid, dattn, gg_f = call(
             norm_back_kernel,
-            [rows_f32, rows_low, gain_row],
-            [*reduce_rows(send, mine), dy, mid, gain_f],
-        )
-        dattn = after(dattn, g_ffn, *early)
+            [held((micro_rows, d), F32), rows_low, held((1, d), F32)],
+            [*summands(send, mine), (dy, mid), gain_f],
+        )
+        dattn = after(dattn, g_ffn)
         dattn, dq, dkv, dkv_send = call(
-            attend_back_kernel,
-            [all_low, shape((group, q_width)), shape((keys // 2, 2 * HD), F32), both_kv],
-            [place, gather_rows(dattn) + [w_out], q, k, v, bias, ctx, lse, cos, sin],
+            functools.partial(attend_back_kernel, layer=layer),
+            [
+                held((group, d)),
+                shape((group, q_width)),
+                shape((keys // 2, 2 * HD), F32),
+                shape((keys // 2, 2 * HD)),
+            ],
+            [place, gather_rows(dattn) + [w_attn], (q, k, v), bias, (ctx, lse), cos, sin],
             [
                 pltpu.VMEM((d, q_width), BF16),
                 pltpu.VMEM((group, q_width), BF16),
                 pltpu.VMEM((keys // 2, 2 * HD), F32),
                 pltpu.VMEM((keys // 2, 2 * HD), F32),
-                DMA,
+                DMA((8,)),
                 DMA((8,)),
             ],
             room=18,
         )
-        dkv = call(kv_add_kernel, [both_kv], [dkv, swap_core(dkv_send)])[0]
+        dkv = after(dkv, other) if pending else dkv
+        dkv = call(kv_add_kernel, [shape(dkv.shape)], [dkv, swap_core(dkv_send)])[0]
         arrived = lax.all_to_all(
             dkv.reshape(8, group // 2, 2 * HD), ("x", "ylo"), 0, 0, tiled=True
         )
         dqkv, send, mine, gg_a = call(
-            qkv_back_kernel,
-            [shape((group, wide)), *partials, gain_row],
-            [place, [qkv_w, rows], dq, arrived, cos, sin],
-            [pltpu.VMEM((d, wide), BF16), pltpu.VMEM((group, d), BF16), DMA((2,))],
+            functools.partial(qkv_back_kernel, layer=layer),
+            [held((group, wide)), *partials, held((1, d), F32)],
+            [place, [w_attn, rows], dq, arrived, cos, sin],
+            [pltpu.VMEM((d, wide), BF16), pltpu.VMEM((group, d), BF16), DMA((8,)), DMA],
             room=16,
         )
         g_attn = attn_products(dattn, ctx, a, dqkv, gg_a, gg_f)
         dx, dx_low, _ = call(
             norm_back_kernel,
-            [rows_f32, rows_low, gain_row],
-            [*reduce_rows(send, mine), dmid, x, gain_a],
-        )
-        return dx, after(dx_low, g_attn), g_attn, g_ffn
+            [held((micro_rows, d), F32), rows_low, held((1, d), F32)],
+            [*summands(send, mine), (dmid, x), gain_a],
+        )
+        return dx, after(dx_low, g_attn), g_attn, g_ffn, other
 
     x0 = lax.dynamic_index_in_dim(block_input, section, 0, keepdims=False)
     dy1 = lax.dynamic_index_in_dim(out_grad, section, 0, keepdims=False)
 
-    rows0, a0, q0, kv0, w_qkv0, w_out0, ga0, gf0 = project(x0, attn0)
-    ffn_pairs = pairs(place, ffn_shard, [after(v, a0) for v in ffn_y])
+    rows0, a0, q0, kv0, ga0, gf0 = project(x0, 0)
+    ffn_pairs = pairs(place, ffn_shard, ffn_y)
     w_ffn0 = gather_x(ffn_pairs[0])
     kv0 = gather_kv(kv0)
-    ctx0, lse0, k0, v0, send, mine = attention(q0, kv0, w_out0)
-    attn1 = gather_x(after(attn_pairs[1], ctx0))
-    mid0, b = call(add_norm_kernel, [rows_f32, rows_low], [*reduce_rows(send, mine), x0, gf0])
+    ctx0, lse0, k0, v0, send, mine = attention(q0, kv0, 0)
+    mid0, b = call(add_norm_kernel, mid_outs, [*summands(send, mine), x0, gf0])
     w_ffn1 = gather_x(after(ffn_pairs[1], b))
     b0, up0, hidden0, send, mine = feed_forward(b, w_ffn0)
-    y0 = call(add_kernel, [rows_low], [*reduce_rows(send, mine), mid0])[0]
-    kept0 = (x0, rows0, w_qkv0, a0, q0, k0, v0, ctx0, lse0, mid0, b0, up0, hidden0, ga0, gf0, w_ffn0, w_out0)
-    rows1, a1, q1, kv1, w_qkv1, w_out1, ga1, gf1 = project(y0, [attn1])
-    ctx1, lse1, k1, v1, send, mine = attention(q1, gather_kv(kv1), w_out1)
-    mid1, b = call(add_norm_kernel, [rows_f32, rows_low], [*reduce_rows(send, mine), y0, gf1])
+    y0 = call(add_kernel, [rows_low], [*summands(send, mine), (mid0,)])[0]
+    kept0 = (x0, rows0, a0, q0, k0, v0, ctx0, lse0, mid0, b0, up0, hidden0, ga0, gf0, w_ffn0)
+    rows1, a1, q1, kv1, ga1, gf1 = project(y0, 1)
+    ctx1, lse1, k1, v1, send, mine = attention(q1, gather_kv(kv1), 1)
+    mid1, b = call(add_norm_kernel, mid_outs, [*summands(send, mine), y0, gf1])
     b1, up1, hidden1, send, mine = feed_forward(b, w_ffn1)
-    y1 = call(add_kernel, [rows_low], [*reduce_rows(send, mine), mid1])[0]
-    kept1 = (y0, rows1, w_qkv1, a1, q1, k1, v1, ctx1, lse1, mid1, b1, up1, hidden1, ga1, gf1, w_ffn1, w_out1)
-
-    dx1, dx1_low, g_attn1, g_ffn1 = backward(dy1, kept1)
-    ffn1, r_attn1 = reduce_x(g_ffn1), reduce_x(g_attn1)
-    dx0, dx0_low, g_attn0, g_ffn0 = backward(dx1_low, kept0, [ffn1])
-    ffn_y = reduce_y(reduce_x(g_ffn0), ffn1, place)
-    dx0 = after(dx0, r_attn1, *ffn_y)
+    y1 = call(add_kernel, [rows_low], [*summands(send, mine), (mid1,)])[0]
+    kept1 = (y0, rows1, a1, q1, k1, v1, ctx1, lse1, mid1, b1, up1, hidden1, ga1, gf1, w_ffn1)
+
     early = section == 0
 
-    ffn_parts = by_core(ffn_y, place)
-    attn_parts = by_core(reduce_y(reduce_x(g_attn0), r_attn1, place), place)
+    def both_micros(layer0, layer1, dtype):
+        mine = jnp.where(early, layer0, layer1).astype(dtype)
+        other = jnp.where(early, layer1, layer0).astype(BF16)
+        other = swap_section(other).astype(dtype)
+        return jnp.stack([jnp.where(early, mine, other), jnp.where(early, other, mine)])[None]
+
+    block_output = both_micros(y0, y1, BF16)
+
+    dx1, dx1_low, g_attn1, g_ffn1, _ = backward(dy1, kept1, 1)
+    ffn1 = reduce_x(g_ffn1)
+    dx0, dx0_low, g_attn0, g_ffn0, r_attn1 = backward(dx1_low, kept0, 0, (g_attn1, ffn1, block_output))
+    input_grad = both_micros(dx0, dx1, F32)
+    ffn_y = reduce_y(after(reduce_x(g_ffn0), input_grad), ffn1, place)
+
+    attn_y = reduce_y(reduce_x(g_attn0), r_attn1, place)
+    ffn_parts = by_core([after(ffn_y[0], attn_y[0]), *ffn_y[1:]], place)
+    attn_parts = by_core(attn_y, place)
 
     def finish(kernel, dims, parts):
-        return call(kernel, [shape(s, F32) for s in dims], [place, *parts], room=12)
+        return call(kernel, [held(s, F32) for s in dims], [place, parts], room=20)
 
     own = own_rows
     grad_out, grad_query, grad_key, grad_value, *gain_pieces, _ = finish(
@@ -860,14 +928,6 @@
         gain_sums = gain_sums + from_z(gain_pieces[k], -k)
     gain_sums = gain_sums[:, :2].T
 
-    def both_micros(layer0, layer1, dtype):
-        mine = jnp.where(early, layer0, layer1).astype(dtype)
-        other = jnp.where(early, layer1, layer0).astype(BF16)
-        other = swap_section(other).astype(dtype)
-        return jnp.stack([jnp.where(early, mine, other), jnp.where(early, other, mine)])[None]
-
-    block_output = both_micros(y0, y1, BF16)
-    input_grad = both_micros(dx0, dx1, F32)
 
     return (
         block_output,

time: 698 us -> 649 us (0.930)
  local copies, waits for them, and re-layouts: 125 us -> 30.3 us
  Pallas kernels: 104 us -> 163 us
  blocking collectives: 40.2 us -> 26.5 us
  starting transfers between devices: 163 us -> 152 us
  waiting for transfers between devices: 236 us -> 245 us
    unnamed x336 -> x200, local copies, waits for them, and re-layouts: 122 us -> 25.6 us
    pallas_call x46, Pallas kernels: 104 us -> 163 us  [call(): pl.pallas_call(kernel, out_shape=tuple(outs), in_specs=specs, out_specs=t...]
    all_gather x3, waiting for transfers between devices: 63.3 us -> 25.2 us  [gather_x(): return lax.all_gather(block, 'x', axis=0, tiled=True)]
    ppermute x3 -> x0, waiting for transfers between devices: 30.3 us -> none  [from_x(): return lax.ppermute(v, 'x', [((i + by) % 4, i) for i in range(4)])]
    reduce_scatter x4, waiting for transfers between devices: 16.7 us -> 41.5 us  [reduce_x(): return lax.psum_scatter(grad, 'x', scatter_dimension=0, tiled=True)]
    ppermute x4, waiting for transfers between devices: 5.37 us -> 27.3 us  [swap_ylo(): return lax.ppermute(v, 'ylo', [(0, 1), (1, 0)])]
    ppermute x4, waiting for transfers between devices: 0.01 us -> 21.2 us  [swap_across(): return lax.ppermute(v, ('section', 'ylo'), [(0, 3), (3, 0), (1, 2), (2, 1)])]
    ppermute x51, waiting for transfers between devices: 42.9 us -> 58.5 us  [from_z(): return lax.ppermute(rows, 'tp', [((i + by) % 4, i) for i in range(4)])]
  transfers between devices with their start and end apart: 124 -> 122, of which waited for: 48 -> 56; matrix products, arithmetic and copies ran while one was open for 1% -> 3% of each run, Pallas kernels for 13% -> 22%
where the time goes in v3:
time: 649 us; the launch traced here: 640 us
  waiting for transfers between devices  245 us (38%)
  Pallas kernels  163 us (25%)
  starting transfers between devices  152 us (23%)
  local copies, waits for them, and re-layouts  30.3 us (5%)
  blocking collectives  26.5 us (4%)
  between operations  15.5 us (2%)
  other arithmetic  7 us (1%)
    pallas_call x46, Pallas kernels, call(): pl.pallas_call(kernel, out_shape=tuple(outs), in_specs=specs, out_specs=t...  163 us
    ppermute x48, starting transfers between devices, swap_core(): return lax.ppermute(v, 'core', [(0, 1), (1, 0)])  64.3 us
    ppermute x51, starting transfers between devices, from_z(): return lax.ppermute(rows, 'tp', [((i + by) % 4, i) for i in range(4)])  58.5 us
    ppermute x51, waiting for transfers between devices, from_z(): return lax.ppermute(rows, 'tp', [((i + by) % 4, i) for i in range(4)])  58.5 us
    reduce_scatter x4, waiting for transfers between devices, reduce_x(): return lax.psum_scatter(grad, 'x', scatter_dimension=0, tiled=True)  41.5 us
    ppermute x6, waiting for transfers between devices, swap_section(): return lax.ppermute(v, 'section', [(0, 1), (1, 0)])  38.4 us
    ppermute x4, waiting for transfers between devices, swap_ylo(): return lax.ppermute(v, 'ylo', [(0, 1), (1, 0)])  27.3 us
    unnamed x200, local copies, waits for them, and re-layouts  25.6 us
  transfers between devices with their start and end apart: 122, of which 56 were waited for; matrix products, arithmetic and copies ran while one was open for 3% of the time, Pallas kernels for 22%

profile of v3, /device:TPU:1, one launch (start us, length us, event | category | flops | bytes accessed | tf_op | source)
XLA Modules:
  0.0 640.0 jit_solution(9586379573697637309)
XLA Ops:
  32.4 8.1 %collective-permute-done.10.far_ref = bf16[272,640]{1,0:T(8,128)(2,1)S(1)} collective-permute-done((bf16[272,640]{1,0:T(8,128)(2,1)S(1)}, bf16[272,640]{1,0:T(8,128)(2,1)S(1)}, u32[]{:S(2)}, u32[]{:S(2)}) %collective-permute-start.10) | collective-permute-done | bytes 348192 | tf_op jit(solution)/shard_map/ppermute | solution.py:97
  49.3 21.6 %collective-permute-done.24.near_ref = bf16[256,2176]{1,0:T(8,128)(2,1)S(1)} collective-permute-done((bf16[256,2176]{1,0:T(8,128)(2,1)S(1)}, bf16[256,2176]{1,0:T(8,128)(2,1)S(1)}, u32[]{:S(2)}, u32[]{:S(2)}) %collective-permute-start.24) | collective-permute-done | bytes 1114144 | tf_op jit(solution)/shard_map/ppermute | solution.py:89
  72.2 24.3 %collective-permute-done.26.straight_ref = bf16[256,2176]{1,0:T(8,128)(2,1)S(1)} collective-permute-done((bf16[256,2176]{1,0:T(8,128)(2,1)S(1)}, bf16[256,2176]{1,0:T(8,128)(2,1)S(1)}, u32[]{:S(2)}, u32[]{:S(2)}) %collective-permute-start.26) | collective-permute-done | bytes 1114144 | tf_op jit(solution)/shard_map/ppermute | solution.py:93
  129.8 7.2 %all-to-all-done = bf16[8,128,128]{2,1,0:T(8,128)(2,1)S(1)} async-done(((bf16[8,128,128]{2,1,0:T(8,128)(2,1)}), bf16[8,128,128]{2,1,0:T(8,128)(2,1)S(1)}, u32[]{:S(2)}, u32[]{:S(2)}) %all-to-all-start) | async-done | bytes 262176 | tf_op jit(solution)/shard_map/all_to_all | solution.py:115
  152.9 6.4 collective-permute-done.14.b
  175.3 25.2 %all-gather.6.cloned.1.call-done.refs_8_ = bf16[2048,2176]{1,0:T(8,128)(2,1)} async-done(((bf16[512,2176]{1,0:T(8,128)(2,1)}), bf16[2048,2176]{1,0:T(8,128)(2,1)}) %all-gather.6.cloned.1.call-update) | async-done | bytes 8912912 | tf_op jit(solution)/shard_map/all_gather | solution.py:130
  200.5 7.1 %ffn_kernel.2 = (bf16[256,2048]{1,0:T(8,128)(2,1)}, f32[256,1408]{1,0:T(8,128)}, bf16[256,768]{1,0:T(8,128)(2,1)}, bf16[128,2048]{1,0:T(8,128)(2,1)S(1)}, f32[128,2048]{1,0:T(8,128)}) custom-call(bf16[32,2048]{1,0:T(8,128)(2,1)} %copy-done.15, bf16[32,2048]{1,0:T(8,128)(2,1)} %copy-done.54, bf16[32,2048]{1,0:T(8,128)(2,1)} %copy-done.58, ...), custom_call_target="tpu_custom_call" | custom-call | flops 1 | bytes 1 | tf_op jit(solution)/shard_map/ffn_kernel/pallas_call | solution.py:66
  241.0 13.8 %all_to_all.20 = bf16[8,128,128]{2,1,0:T(8,128)(2,1)S(1)} all-to-all(bf16[8,128,128]{2,1,0:T(8,128)(2,1)S(1)} %broadcast_in_dim.61), channel_id=1, replica_groups=mesh['section'=2,'x'=4,'ylo'=2,'core'=2,'tp'=4] {'x','ylo'}, dimensions={0} | all-to-all | bytes 524288 | tf_op jit(solution)/shard_map/all_to_all | solution.py:115
  257.7 5.9 attend_kernel.3
  296.0 7.1 %ffn_kernel.3 = (bf16[256,2048]{1,0:T(8,128)(2,1)}, f32[256,1408]{1,0:T(8,128)}, bf16[256,768]{1,0:T(8,128)(2,1)}, bf16[128,2048]{1,0:T(8,128)(2,1)S(1)}, f32[128,2048]{1,0:T(8,128)}) custom-call(bf16[32,2048]{1,0:T(8,128)(2,1)} %copy-done.14, bf16[32,2048]{1,0:T(8,128)(2,1)} %copy-done.48, bf16[32,2048]{1,0:T(8,128)(2,1)} %copy-done.49, ...), custom_call_target="tpu_custom_call" | custom-call | flops 1 | bytes 1 | tf_op jit(solution)/shard_map/ffn_kernel/pallas_call | solution.py:66
  303.9 7.8 %ffn_back_kernel.2 = (bf16[256,2048]{1,0:T(8,128)(2,1)}, bf16[256,1408]{1,0:T(8,128)(2,1)}, bf16[128,2048]{1,0:T(8,128)(2,1)S(1)}, f32[128,2048]{1,0:T(8,128)}) custom-call(bf16[32,2048]{1,0:T(8,128)(2,1)} %dynamic-slice_bitcast_fusion.refs_0_.after_ref, bf16[32,2048]{1,0:T(8,128)(2,1)} %collective-permute-done.55.refs_1_, ...), custom_call_target="tpu_custom_call" | custom-call | flops 1 | bytes 1 | tf_op jit(solution)/shard_map/ffn_back_kernel/pallas_call | solution.py:66
  311.8 6.0 ffn_product_kernel.2
  347.8 10.7 %attend_back_kernel.2 = (bf16[256,2048]{1,0:T(8,128)(2,1)}, bf16[256,256]{1,0:T(8,128)(2,1)S(1)}, f32[1024,128]{1,0:T(8,128)S(1)}, bf16[1024,128]{1,0:T(8,128)(2,1)}) custom-call(s32[5]{0:T(128)S(1)} %stack.41.place, bf16[32,2048]{1,0:T(8,128)(2,1)} %copy-done.17, bf16[32,2048]{1,0:T(8,128)(2,1)} %copy-done.55, bf16[32,2048]{1,0:T(8,128)(2,1)} %copy-done.59, ...), custom_call_target="tpu_custom_call" | custom-call | flops 1 | bytes 1 | tf_op jit(solution)/shard_map/attend_back_kernel/pallas_call | solution.py:66
  363.9 6.8 %collective-permute-done.51.b = bf16[32,2048]{1,0:T(8,128)(2,1)S(1)} collective-permute-done((bf16[32,2048]{1,0:T(8,128)(2,1)}, bf16[32,2048]{1,0:T(8,128)(2,1)S(1)}, u32[]{:S(2)}, u32[]{:S(2)}) %collective-permute-start.51) | collective-permute-done | bytes 131104 | tf_op jit(solution)/shard_map/ppermute | solution.py:81
  382.2 6.2 all-to-all-done.2.kv_ref
  425.2 7.8 %ffn_back_kernel.3 = (bf16[256,2048]{1,0:T(8,128)(2,1)}, bf16[256,1408]{1,0:T(8,128)(2,1)}, bf16[128,2048]{1,0:T(8,128)(2,1)S(1)}, f32[128,2048]{1,0:T(8,128)}) custom-call(bf16[32,2048]{1,0:T(8,128)(2,1)} %copy-done.10, bf16[32,2048]{1,0:T(8,128)(2,1)} %copy-done.60, bf16[32,2048]{1,0:T(8,128)(2,1)} %copy-done.64, bf16[32,2048]{1,0:T(8,128)(2,1)} %copy-done.68, ...), custom_call_target="tpu_custom_call" | custom-call | flops 1 | bytes 1 | tf_op jit(solution)/shard_map/ffn_back_kernel/pallas_call | solution.py:66
  433.0 5.9 ffn_product_kernel.3
  445.9 5.9 collective-permute-done.86.b
  468.8 10.7 %attend_back_kernel.3 = (bf16[256,2048]{1,0:T(8,128)(2,1)}, bf16[256,256]{1,0:T(8,128)(2,1)S(1)}, f32[1024,128]{1,0:T(8,128)S(1)}, bf16[1024,128]{1,0:T(8,128)(2,1)}) custom-call(s32[5]{0:T(128)S(1)} %stack.41.place, bf16[32,2048]{1,0:T(8,128)(2,1)} %copy-done.16, bf16[32,2048]{1,0:T(8,128)(2,1)} %copy-done.53, bf16[32,2048]{1,0:T(8,128)(2,1)} %copy-done.57, ...), custom_call_target="tpu_custom_call" | custom-call | flops 1 | bytes 1 | tf_op jit(solution)/shard_map/attend_back_kernel/pallas_call | solution.py:66
  482.0 12.8 %all_to_all.21.kv_ref = bf16[8,128,128]{2,1,0:T(8,128)(2,1)S(1)} all-to-all(bf16[8,128,128]{2,1,0:T(8,128)(2,1)S(1)} %bitcast.54), channel_id=1, replica_groups=mesh['section'=2,'x'=4,'ylo'=2,'core'=2,'tp'=4] {'x','ylo'}, dimensions={0} | all-to-all | bytes 524288 | tf_op jit(solution)/shard_map/all_to_all | solution.py:854
  528.4 9.4 %reduce-scatter.11.cloned.1.call-done.r0_ref = bf16[512,2176]{1,0:T(8,128)(2,1)} async-done(((bf16[2048,2176]{1,0:T(8,128)(2,1)}), bf16[512,2176]{1,0:T(8,128)(2,1)}) %reduce-scatter.11.cloned.1.call-update) | async-done | bytes 2228240 | tf_op jit(solution)/shard_map/reduce_scatter | solution.py:134
  546.1 32.1 %reduce-scatter.9.cloned.1.call-done.r0_ref = bf16[512,768]{1,0:T(8,128)(2,1)} async-done(((bf16[2048,768]{1,0:T(8,128)(2,1)}), bf16[512,768]{1,0:T(8,128)(2,1)}) %reduce-scatter.9.cloned.1.call-update) | async-done | bytes 786448 | tf_op jit(solution)/shard_map/reduce_scatter | solution.py:134
  584.6 9.8 %collective-permute-done.111.refs_3_ = bf16[256,2176]{1,0:T(8,128)(2,1)} collective-permute-done((bf16[256,2176]{1,0:T(8,128)(2,1)}, bf16[256,2176]{1,0:T(8,128)(2,1)}, u32[]{:S(2)}, u32[]{:S(2)}) %collective-permute-start.111) | collective-permute-done | bytes 1114144 | tf_op jit(solution)/shard_map/ppermute | solution.py:93
  600.5 11.8 %collective-permute-done.103.refs_2_ = bf16[256,768]{1,0:T(8,128)(2,1)S(1)} collective-permute-done((bf16[256,768]{1,0:T(8,128)(2,1)}, bf16[256,768]{1,0:T(8,128)(2,1)S(1)}, u32[]{:S(2)}, u32[]{:S(2)}) %collective-permute-start.103) | collective-permute-done | bytes 393248 | tf_op jit(solution)/shard_map/ppermute | solution.py:97
  (509 shorter events, 354.2 us)
Async XLA Ops:
  7.2 110.0 %all-gather.4.cloned.1.call-start = ((), (), s32[]{:S(2)}) async-start(), calls=%async_computation.8 | async-start | bytes 6963200 | tf_op jit(solution)/shard_map/all_gather | solution.py:130
  24.1 16.3 %collective-permute-start.10 = (bf16[272,640]{1,0:T(8,128)(2,1)S(1)}, bf16[272,640]{1,0:T(8,128)(2,1)S(1)}, u32[]{:S(2)}, u32[]{:S(2)}) collective-permute-start(bf16[272,640]{1,0:T(8,128)(2,1)S(1)} %copy-done.31), channel_id=1, source_target_pairs={{0,72},{72,0},{8,64},{64,8},{1,73},{73,1},{9,65},{65,9},{2,74},{74... | collective-permute-start | bytes 1044488 | tf_op jit(solution)/shard_map/ppermute | solution.py:97
  26.0 16.3 %collective-permute-start.11 = (bf16[272,640]{1,0:T(8,128)(2,1)S(1)}, bf16[272,640]{1,0:T(8,128)(2,1)S(1)}, u32[]{:S(2)}, u32[]{:S(2)}) collective-permute-start(bf16[272,640]{1,0:T(8,128)(2,1)S(1)} %copy-done.31), channel_id=1, source_target_pairs={{0,64},{64,0},{1,65},{65,1},{2,66},{66,2},{3,67},{67,3},{4,68},{68... | collective-permute-start | bytes 1044488 | tf_op jit(solution)/shard_map/ppermute | solution.py:93
  45.6 154.9 %all-gather.6.cloned.1.call-start = ((), (), s32[]{:S(2)}) async-start(), calls=%async_computation.9 | async-start | bytes 11141120 | tf_op jit(solution)/shard_map/all_gather | solution.py:130
  45.7 25.2 %collective-permute-start.24 = (bf16[256,2176]{1,0:T(8,128)(2,1)S(1)}, bf16[256,2176]{1,0:T(8,128)(2,1)S(1)}, u32[]{:S(2)}, u32[]{:S(2)}) collective-permute-start(bf16[256,2176]{1,0:T(8,128)(2,1)S(1)} %copy-done.30), channel_id=1, source_target_pairs={{0,8},{8,0},{1,9},{9,1},{2,10},{10,2},{3,11},{11,3},{4,12},{12,4},... | collective-permute-start | bytes 3342344 | tf_op jit(solution)/shard_map/ppermute | solution.py:89
  45.8 26.4 %collective-permute-start.25 = (bf16[256,2176]{1,0:T(8,128)(2,1)S(1)}, bf16[256,2176]{1,0:T(8,128)(2,1)S(1)}, u32[]{:S(2)}, u32[]{:S(2)}) collective-permute-start(bf16[256,2176]{1,0:T(8,128)(2,1)S(1)} %copy-done.30), channel_id=1, source_target_pairs={{0,72},{72,0},{8,64},{64,8},{1,73},{73,1},{9,65},{65,9},{2,74},{74... | collective-permute-start | bytes 3342344 | tf_op jit(solution)/shard_map/ppermute | solution.py:97
  48.2 48.3 %collective-permute-start.26 = (bf16[256,2176]{1,0:T(8,128)(2,1)S(1)}, bf16[256,2176]{1,0:T(8,128)(2,1)S(1)}, u32[]{:S(2)}, u32[]{:S(2)}) collective-permute-start(bf16[256,2176]{1,0:T(8,128)(2,1)S(1)} %copy-done.30), channel_id=1, source_target_pairs={{0,64},{64,0},{1,65},{65,1},{2,66},{66,2},{3,67},{67,3},{4,68},{68... | collective-permute-start | bytes 3342344 | tf_op jit(solution)/shard_map/ppermute | solution.py:93
  123.4 13.7 %all-to-all-start = ((bf16[8,128,128]{2,1,0:T(8,128)(2,1)}), bf16[8,128,128]{2,1,0:T(8,128)(2,1)S(1)}, u32[]{:S(2)}, u32[]{:S(2)}) async-start(bf16[8,128,128]{2,1,0:T(8,128)(2,1)} %broadcast_in_dim.58), calls=%async_computation | async-start | bytes 524288 | tf_op jit(solution)/shard_map/all_to_all | solution.py:115
  127.7 168.3 %all-gather.8.cloned.1.call-start = ((), (), s32[]{:S(2)}) async-start(), calls=%async_computation.10 | async-start | bytes 11141120 | tf_op jit(solution)/shard_map/all_gather | solution.py:130
  161.3 249.1 %reduce-scatter.5.cloned.1.call-start = ((), (), s32[]{:S(2)}) async-start(), calls=%async_computation.11 | async-start | bytes 11141120 | tf_op jit(solution)/shard_map/reduce_scatter | solution.py:134
  324.8 34.2 %collective-permute-start.50 = (bf16[128,2048]{1,0:T(8,128)(2,1)}, bf16[128,2048]{1,0:T(8,128)(2,1)S(1)}, u32[]{:S(2)}, u32[]{:S(2)}) collective-permute-start(bf16[128,2048]{1,0:T(8,128)(2,1)} %copy-done.28), channel_id=1, source_target_pairs={{0,4},{4,0},{1,5},{5,1},{2,6},{6,2},{3,7},{7,3},{8,12},{12,8},{9,1... | collective-permute-start | bytes 1572872 | tf_op jit(solution)/shard_map/ppermute | solution.py:85
  358.5 14.9 %collective-permute-start.73 = (bf16[1024,128]{1,0:T(8,128)(2,1)}, bf16[1024,128]{1,0:T(8,128)(2,1)S(1)}, u32[]{:S(2)}, u32[]{:S(2)}) collective-permute-start(bf16[1024,128]{1,0:T(8,128)(2,1)} %get-tuple-element.215), channel_id=1, source_target_pairs={{0,4},{4,0},{1,5},{5,1},{2,6},{6,2},{3,7},{7,3},{8,12},{12,8},{9,1... | collective-permute-start | bytes 786440 | tf_op jit(solution)/shard_map/ppermute | solution.py:85
  375.2 13.1 %all-to-all-start.2 = ((bf16[8,128,128]{2,1,0:T(8,128)(2,1)}), bf16[8,128,128]{2,1,0:T(8,128)(2,1)S(1)}, u32[]{:S(2)}, u32[]{:S(2)}) async-start(bf16[8,128,128]{2,1,0:T(8,128)(2,1)} %bitcast.53), calls=%async_computation.2 | async-start | bytes 524288 | tf_op jit(solution)/shard_map/all_to_all | solution.py:854
  378.7 101.9 %reduce-scatter.7.cloned.1.call-start = ((), (), s32[]{:S(2)}) async-start(), calls=%async_computation.12 | async-start | bytes 3932160 | tf_op jit(solution)/shard_map/reduce_scatter | solution.py:134
  379.4 15.8 %collective-permute-start.54 = (bf16[32,2048]{1,0:T(8,128)(2,1)}, bf16[32,2048]{1,0:T(8,128)(2,1)}, u32[]{:S(2)}, u32[]{:S(2)}) collective-permute-start(bf16[32,2048]{1,0:T(8,128)(2,1)} %broadcast_select_fusion.3), channel_id=1, source_target_pairs={{0,64},{64,0},{1,65},{65,1},{2,66},{66,2},{3,67},{67,3},{4,68},{68... | collective-permute-start | bytes 393224 | tf_op jit(solution)/shard_map/ppermute | solution.py:93
  410.4 127.4 %reduce-scatter.11.cloned.1.call-start = ((), (), s32[]{:S(2)}) async-start(), calls=%async_computation.14 | async-start | bytes 11141120 | tf_op jit(solution)/shard_map/reduce_scatter | solution.py:134
  439.0 139.2 %reduce-scatter.9.cloned.1.call-start = ((), (), s32[]{:S(2)}) async-start(), calls=%async_computation.13 | async-start | bytes 3932160 | tf_op jit(solution)/shard_map/reduce_scatter | solution.py:134
  542.5 41.4 %collective-permute-start.109 = (bf16[256,2176]{1,0:T(8,128)(2,1)}, bf16[256,2176]{1,0:T(8,128)(2,1)S(1)}, u32[]{:S(2)}, u32[]{:S(2)}) collective-permute-start(bf16[256,2176]{1,0:T(8,128)(2,1)} %get-tuple-element.285), channel_id=1, source_target_pairs={{0,8},{8,0},{1,9},{9,1},{2,10},{10,2},{3,11},{11,3},{4,12},{12,4},... | collective-permute-start | bytes 3342344 | tf_op jit(solution)/shard_map/ppermute | solution.py:89
  543.7 40.9 %collective-permute-start.110 = (bf16[256,2176]{1,0:T(8,128)(2,1)}, bf16[256,2176]{1,0:T(8,128)(2,1)}, u32[]{:S(2)}, u32[]{:S(2)}) collective-permute-start(bf16[256,2176]{1,0:T(8,128)(2,1)} %get-tuple-element.286), channel_id=1, source_target_pairs={{0,72},{72,0},{8,64},{64,8},{1,73},{73,1},{9,65},{65,9},{2,74},{74... | collective-permute-start | bytes 3342344 | tf_op jit(solution)/shard_map/ppermute | solution.py:97
  545.5 48.9 %collective-permute-start.111 = (bf16[256,2176]{1,0:T(8,128)(2,1)}, bf16[256,2176]{1,0:T(8,128)(2,1)}, u32[]{:S(2)}, u32[]{:S(2)}) collective-permute-start(bf16[256,2176]{1,0:T(8,128)(2,1)} %get-tuple-element.287), channel_id=1, source_target_pairs={{0,64},{64,0},{1,65},{65,1},{2,66},{66,2},{3,67},{67,3},{4,68},{68... | collective-permute-start | bytes 3342344 | tf_op jit(solution)/shard_map/ppermute | solution.py:93
  580.8 19.7 %collective-permute-start.102 = (bf16[256,768]{1,0:T(8,128)(2,1)}, bf16[256,768]{1,0:T(8,128)(2,1)S(1)}, u32[]{:S(2)}, u32[]{:S(2)}) collective-permute-start(bf16[256,768]{1,0:T(8,128)(2,1)} %get-tuple-element.269), channel_id=1, source_target_pairs={{0,8},{8,0},{1,9},{9,1},{2,10},{10,2},{3,11},{11,3},{4,12},{12,4},... | collective-permute-start | bytes 1179656 | tf_op jit(solution)/shard_map/ppermute | solution.py:89
  582.0 30.3 %collective-permute-start.103 = (bf16[256,768]{1,0:T(8,128)(2,1)}, bf16[256,768]{1,0:T(8,128)(2,1)S(1)}, u32[]{:S(2)}, u32[]{:S(2)}) collective-permute-start(bf16[256,768]{1,0:T(8,128)(2,1)} %get-tuple-element.270), channel_id=1, source_target_pairs={{0,72},{72,0},{8,64},{64,8},{1,73},{73,1},{9,65},{65,9},{2,74},{74... | collective-permute-start | bytes 1179656 | tf_op jit(solution)/shard_map/ppermute | solution.py:97
  583.9 28.5 %collective-permute-start.104 = (bf16[256,768]{1,0:T(8,128)(2,1)}, bf16[256,768]{1,0:T(8,128)(2,1)S(1)}, u32[]{:S(2)}, u32[]{:S(2)}) collective-permute-start(bf16[256,768]{1,0:T(8,128)(2,1)} %get-tuple-element.271), channel_id=1, source_target_pairs={{0,64},{64,0},{1,65},{65,1},{2,66},{66,2},{3,67},{67,3},{4,68},{68... | collective-permute-start | bytes 1179656 | tf_op jit(solution)/shard_map/ppermute | solution.py:93
  597.9 26.2 %collective-permute-start.112 = (bf16[128,2176]{1,0:T(8,128)(2,1)S(1)}, bf16[128,2176]{1,0:T(8,128)(2,1)S(1)}, u32[]{:S(2)}, u32[]{:S(2)}) collective-permute-start(bf16[128,2176]{1,0:T(8,128)(2,1)S(1)} %get-tuple-element.289), channel_id=1, source_target_pairs={{0,4},{4,0},{1,5},{5,1},{2,6},{6,2},{3,7},{7,3},{8,12},{12,8},{9,1... | collective-permute-start | bytes 1671176 | tf_op jit(solution)/shard_map/ppermute | solution.py:85
  (195 other events, 1404.3 us)
Sparse Core Ops, SparseCore 0:
  45.8 62.0 all-gather.3
  109.5 90.9 all-gather.5
  202.2 91.3 all-gather.7
  318.0 86.0 reduce-scatter.4
  410.5 37.6 reduce-scatter.6
  450.5 87.2 reduce-scatter.10
  540.2 37.9 reduce-scatter.8

commit v4 on v3

--- a/solution.py
+++ b/solution.py
@@ -14,7 +14,7 @@
 MASKED = -1e30
 KEYS_STEP = 512
 AXES = ("section", "x", "ylo", "core", "tp")
-SECTION, _, YLO, CORE, TP = range(5)
+SECTION, X, YLO, CORE, TP = range(5)
 BF16 = jnp.bfloat16
 F32 = jnp.float32
 VMEM = pl.BlockSpec(memory_space=pltpu.VMEM)
@@ -50,7 +50,7 @@
     return pltpu.with_memory_space_constraint(v, pltpu.HBM)
 
 
-def call(kernel, outs, args, scratch=(), room=8, out_spec=None):
+def call(kernel, outs, args, scratch=(), room=8, out_spec=None, moved=0):
     specs, values = [], []
     for a in args:
         if isinstance(a, (list, tuple)):
@@ -72,7 +72,9 @@
         ),
         scratch_shapes=list(scratch),
         compiler_params=pltpu.CompilerParams(vmem_limit_bytes=room),
-        cost_estimate=SHORT,
+        cost_estimate=pl.CostEstimate(flops=moved, bytes_accessed=moved, transcendentals=0)
+        if moved
+        else SHORT,
         name=getattr(kernel, "func", kernel).__name__,
     )(*values)
 
@@ -81,6 +83,10 @@
     return lax.ppermute(rows, "tp", [((i + by) % 4, i) for i in range(4)])
 
 
+def from_x(v, by):
+    return lax.ppermute(v, "x", [((i + by) % 4, i) for i in range(4)])
+
+
 def swap_core(v):
     return lax.ppermute(v, "core", [(0, 1), (1, 0)])
 
@@ -103,6 +109,12 @@
 
 def y_exchange(v):
     return swap_ylo(v), swap_across(v), swap_section(v)
+
+
+def y_exchange_on(v):
+    near, far = swap_ylo(v), swap_across(v)
+    n = v.shape[0] // 2
+    return near, far, swap_ylo(far[:n]), swap_across(near[n:])
 
 
 def gather_rows(rows):
@@ -121,11 +133,6 @@
     return [own] + [from_z(p, -k) for k, p in zip((1, 2, 3), pieces)]
 
 
-def summands(send, mine):
-    own, *others = reduce_rows(send, mine)
-    return [(own,), *others]
-
-
 def gather_x(block):
     return lax.all_gather(block, "x", axis=0, tiled=True)
 
@@ -137,7 +144,7 @@
 def pack_attn_kernel(place, q_ref, k_ref, v_ref, o_ref, ga_ref, gf_ref, own_ref, send_ref):
     n, rows = q_ref.shape[1] // 2, q_ref.shape[0]
     m = n + 2 * HD
-    kv = jnp.concatenate([k_ref[...], v_ref[...]], axis=1)
+    kv = jnp.concatenate([k_ref[...], v_ref[...]], axis=0).T
     o = o_ref[...].T
     odd = place[CORE] == 1
     row = lax.broadcasted_iota(jnp.int32, (GAIN_ROWS, ga_ref.shape[1]), 0)
@@ -189,15 +196,18 @@
     )
 
 
-def pairs_kernel(place, own_ref, near_ref, far_ref, straight_ref, p0_ref, p1_ref):
-    n = own_ref.shape[0]
+def pairs_kernel(place, own_ref, near_ref, far_ref, *refs):
+    *straight_refs, p0_ref, p1_ref = refs
+    n, part = own_ref.shape[0], straight_refs[0].shape[0]
     here = pl.ds(pl.multiple_of(place[YLO] * n, n), n)
     there = pl.ds(pl.multiple_of((1 - place[YLO]) * n, n), n)
 
     def fill(mine, other):
         mine[here, :] = own_ref[...]
         mine[there, :] = near_ref[...]
-        other[here, :] = straight_ref[...]
+        for i, ref in enumerate(straight_refs):
+            at = pl.multiple_of(place[YLO] * n + i * part, part)
+            other[pl.ds(at, part), :] = ref[...]
         other[there, :] = far_ref[...]
 
     @pl.when(place[SECTION] == 0)
@@ -207,23 +217,6 @@
     @pl.when(place[SECTION] == 1)
     def _():
         fill(p1_ref, p0_ref)
-
-
-def both_pairs_kernel(place, own_ref, near_ref, far_ref, straight_ref, out_ref):
-    n = own_ref.shape[0]
-    mine, other, here = 2 * place[SECTION], 2 - 2 * place[SECTION], place[YLO]
-    for src, at in (
-        (own_ref, mine + here),
-        (near_ref, mine + 1 - here),
-        (straight_ref, other + here),
-        (far_ref, other + 1 - here),
-    ):
-        out_ref[pl.ds(pl.multiple_of(at * n, n), n), :] = src[...]
-
-
-def both_pairs(place, own, others):
-    n, c = own.shape
-    return call(both_pairs_kernel, [held((4 * n, c))], [place, (own, *others)], room=16)[0]
 
 
 def pairs(place, own, others):
@@ -248,26 +241,29 @@
     return wait
 
 
-def block_row(pack, layer, i):
-    return (i // 2 * 4 + 2 * layer + i % 2) * (pack.shape[0] // 16)
-
-
-def fetch_blocks(pack, layer, column, whole, sems):
+def block_of(packs, place, i):
+    step = sum(p.shape[0] for p in packs) // 8
+    if len(packs) == 1:
+        return packs[0], i * step, i
+    return packs[i // 2], i % 2 * step, lax.rem(place[X] + i // 2, 4) * 2 + i % 2
+
+
+def fetch_blocks(packs, place, column, whole, sems):
     n, c = whole.shape[0] // 8, whole.shape[1]
-    copies = [
-        pltpu.make_async_copy(
-            pack.at[pl.ds(block_row(pack, layer, i), n), pl.ds(column, c)],
-            whole.at[pl.ds(i * n, n), :],
-            sems.at[i],
-        )
-        for i in range(8)
-    ]
-    for c in copies:
-        c.start()
+
+    def copy(i, pack, row, block):
+        rows = pl.ds(pl.multiple_of(block * n, n), n)
+        return pltpu.make_async_copy(
+            pack.at[pl.ds(row, n), pl.ds(column, c)], whole.at[rows, :], sems.at[i]
+        )
+
+    for i in range(8):
+        copy(i, *block_of(packs, place, i)).start()
 
     def wait():
-        for c in copies:
-            c.wait()
+        for i in range(8):
+            pack, row, _ = block_of(packs, place, i)
+            copy(i, pack, row, i).wait()
 
     return wait
 
@@ -310,7 +306,7 @@
 
 def split(mine, other):
     n, d = mine.shape[0] // 4, mine.shape[1]
-    return call(split_kernel, [held((n, d), F32)] + [shape((n, d))] * 3, [(mine,), other])
+    return call(split_kernel, [shape((n, d), F32)] + [shape((n, d))] * 3, [mine, other])
 
 
 def total_of(refs):
@@ -341,25 +337,24 @@
     low_ref[...] = dx.astype(BF16)
 
 
-def qkv_kernel(place, *refs, layer):
-    pieces, pack, refs = refs[:8], refs[8], refs[9:]
+def qkv_kernel(place, *refs, parts):
+    pieces, packs, refs = refs[:8], refs[8 : 8 + parts], refs[8 + parts :]
     cos_ref, sin_ref, x_ref, a_ref, q_ref, kv_ref, ga_ref, gf_ref, *refs = refs
     w_ref, gains_ref, x_sems, w_sems, g_sems = refs
     rows_there = fetch(pieces, x_ref, x_sems)
     n = w_ref.shape[0] // 8
-    gain_copies = [
-        pltpu.make_async_copy(
-            pack.at[pl.ds(block_row(pack, layer, i) + n, GAIN_ROWS), pl.ds(0, n)],
-            gains_ref.at[i],
-            g_sems.at[i],
-        )
-        for i in range(8)
-    ]
-    for c in gain_copies:
-        c.start()
-    weights_there = fetch_blocks(pack, layer, 0, w_ref, w_sems)
-    for c in gain_copies:
-        c.wait()
+
+    def gain_copy(i, pack, row, block):
+        return pltpu.make_async_copy(
+            pack.at[pl.ds(row + n, GAIN_ROWS), pl.ds(0, n)], gains_ref.at[block], g_sems.at[i]
+        )
+
+    for i in range(8):
+        gain_copy(i, *block_of(packs, place, i)).start()
+    weights_there = fetch_blocks(packs, place, 0, w_ref, w_sems)
+    for i in range(8):
+        pack, row, _ = block_of(packs, place, i)
+        gain_copy(i, pack, row, i).wait()
     gains = jnp.concatenate([gains_ref[i] for i in range(8)], axis=1).astype(F32)
     ga_ref[...] = gains[0:1, :]
     gf_ref[...] = gains[1:2, :]
@@ -383,9 +378,10 @@
     return pl.ds(t % per * KEYS_STEP, KEYS_STEP), slice(t // per * HD, (t // per + 1) * HD)
 
 
-def attend_kernel(place, q_ref, own_ref, other_ref, bias_ref, pack, *refs, layer):
+def attend_kernel(place, q_ref, own_ref, other_ref, bias_ref, *refs, parts):
+    packs, refs = refs[:parts], refs[parts:]
     o_ref, lse_ref, k_ref, v_ref, send_ref, mine_ref, s_ref, w_ref, sems = refs
-    weights_there = fetch_blocks(pack, layer, pack.shape[1] - w_ref.shape[1], w_ref, sems)
+    weights_there = fetch_blocks(packs, place, packs[0].shape[1] - w_ref.shape[1], w_ref, sems)
     odd = place[CORE] == 1
     k_ref[...] = jnp.where(odd, other_ref[...], own_ref[...])
     v_ref[...] = jnp.where(odd, own_ref[...], other_ref[...])
@@ -472,12 +468,12 @@
     halves_out(nt(dgu_ref[...], gu_w[...]), send_ref, mine_ref)
 
 
-def attend_back_kernel(place, *refs, layer):
-    pieces, refs = refs[:8], refs[8:]
-    pack, q_ref, k_ref, v_ref, bias_ref, o_ref, lse_ref, cos_ref, sin_ref, *refs = refs
+def attend_back_kernel(place, *refs, parts):
+    pieces, packs, refs = refs[:8], refs[8 : 8 + parts], refs[8 + parts :]
+    q_ref, k_ref, v_ref, bias_ref, o_ref, lse_ref, cos_ref, sin_ref, *refs = refs
     dattn_ref, dq_ref, own_ref, send_ref, w_ref, do_ref, dk_ref, dv_ref, sems, r_sems = refs
     rows_there = fetch(pieces, dattn_ref, r_sems)
-    weights_there = fetch_blocks(pack, layer, pack.shape[1] - w_ref.shape[1], w_ref, sems)
+    weights_there = fetch_blocks(packs, place, packs[0].shape[1] - w_ref.shape[1], w_ref, sems)
     rows, width = q_ref.shape
     heads = width // HD
     steps = 2 * k_ref.shape[0] // KEYS_STEP
@@ -520,9 +516,10 @@
     out_ref[...] = (own_ref[...] + other_ref[...].astype(F32)).astype(BF16)
 
 
-def qkv_back_kernel(place, pack, x_hbm, dq_ref, kv_ref, cos_ref, sin_ref, *refs, layer):
+def qkv_back_kernel(place, *refs, parts):
+    packs, (x_hbm, dq_ref, kv_ref, cos_ref, sin_ref, *refs) = refs[:parts], refs[parts:]
     dqkv_ref, send_ref, mine_ref, gain_grad_ref, w_ref, x_ref, sems, x_sem = refs
-    weights_there = fetch_blocks(pack, layer, 0, w_ref, sems)
+    weights_there = fetch_blocks(packs, place, 0, w_ref, sems)
     rows_there = pltpu.make_async_copy(x_hbm, x_ref, x_sem)
     rows_there.start()
     width, odd = dq_ref.shape[1], place[CORE] == 1
@@ -568,6 +565,7 @@
         [(b, dgu, dff, hidden)],
         [pltpu.VMEM(dims, BF16), DMA((8,))],
         room=14,
+        moved=20_000_000,
         out_spec=HBM,
     )[0]
 
@@ -600,6 +598,7 @@
         [(dattn, a, gg_a, gg_f, ctx, dqkv)],
         [pltpu.VMEM(dims, BF16), DMA((4,))],
         room=14,
+        moved=12_000_000,
         out_spec=HBM,
     )[0]
 
@@ -662,8 +661,9 @@
     o_ref[m:, :] = jnp.where(odd, own, other)
     q_ref[...] = ordered(odd, own_ref[:, m : m + n], other_ref[:, m : m + n])
     both = own_ref[:, m + n :] + other_ref[:, m + n :].astype(F32)
-    k_ref[...] = both[:, :HD]
-    v_ref[...] = both[:, HD : 2 * HD]
+    kv = both[:, : 2 * HD].T
+    k_ref[...] = kv[:HD, :]
+    v_ref[...] = kv[HD:, :]
     rows = gain_refs[0].shape[0]
     gain_refs[-1][...] = both[:, 2 * HD :]
     for k, ref in enumerate(gain_refs[:-1]):
@@ -710,7 +710,7 @@
     attn_own, attn_send = call(
         pack_attn_kernel,
         [shape(attn_dims)] * 2,
-        [place, (w_query[0], w_key[0], w_value[0], w_out[0], attn_gain, ffn_gain)],
+        [place, (w_query[0], w_key[0].T, w_value[0].T, w_out[0], attn_gain, ffn_gain)],
     )
     attn_shard = call(
         chip_attn_kernel,
@@ -725,8 +725,10 @@
     )
     ffn_shard = chip_rows(place, ffn_own, swap_core(ffn_send))
     attn_y = y_exchange(after(attn_shard, ffn_shard))
-    w_attn = gather_x(both_pairs(place, attn_shard, attn_y))
-    ffn_y = y_exchange(ffn_shard)
+    attn_pairs = pairs(place, attn_shard, attn_y)
+    attn0 = [attn_pairs[0]] + [from_x(attn_pairs[0], k) for k in (1, 2, 3)]
+    attn1 = [gather_x(attn_pairs[1])]
+    ffn_y = y_exchange_on(after(ffn_shard, *attn_y))
 
     block = at["x"] * 2 + at["ylo"]
     seg_row = lax.dynamic_index_in_dim(seg_ids, section, 0, keepdims=False)
@@ -755,18 +757,19 @@
     cos, sin = jnp.where(plain, 1.0, cos), jnp.where(plain, 0.0, sin)
 
     rows_low = shape((micro_rows, d))
-    mid_outs = [held((micro_rows, d), F32), rows_low]
-    partials = [shape((group // 2, d)), held((group // 2, d), F32)]
+    rows_f32 = shape((micro_rows, d), F32)
+    mid_outs = [rows_f32, rows_low]
+    partials = [shape((group // 2, d)), shape((group // 2, d), F32)]
     heads, keys = q_width // HD, seg_row.shape[0]
     gain_row = shape((1, d), F32)
 
-    def project(x, layer):
+    def project(x, packs):
         return call(
-            functools.partial(qkv_kernel, layer=layer),
+            functools.partial(qkv_kernel, parts=len(packs)),
             [held((group, d))] * 2
             + [shape((group, q_width)), shape((group // 2, 2 * HD))]
             + [gain_row, gain_row],
-            [place, gather_rows(x) + [w_attn], cos, sin],
+            [place, gather_rows(x) + packs, cos, sin],
             [
                 pltpu.VMEM((d, wide), BF16),
                 pltpu.VMEM((8, GAIN_ROWS, d // 8), BF16),
@@ -779,11 +782,11 @@
 
     both_kv = held((keys // 2, 2 * HD))
 
-    def attention(q, kv, layer):
+    def attention(q, kv, packs):
         return call(
-            functools.partial(attend_kernel, layer=layer),
+            functools.partial(attend_kernel, parts=len(packs)),
             [held((group, q_width)), held((heads, group), F32), both_kv, both_kv, *partials],
-            [place, q, *kv, bias, [w_attn]],
+            [place, q, *kv, bias, packs],
             [
                 pltpu.VMEM((heads, keys, group), F32),
                 pltpu.VMEM((d, q_width), BF16),
@@ -807,8 +810,8 @@
             room=16,
         )
 
-    def backward(dy, kept, layer, pending=None):
-        x, rows, a, q, k, v, ctx, lse, mid, b, gu, hidden, gain_a, gain_f, w_ffn = kept
+    def backward(dy, kept, pending=None):
+        x, rows, a, q, k, v, ctx, lse, mid, b, gu, hidden, gain_a, gain_f, w_ffn, packs = kept
         other = pending and reduce_x(after(pending[0], *pending[1:], dy))
         dff, dgu, send, mine = call(
             ffn_back_kernel,
@@ -826,19 +829,19 @@
         g_ffn = ffn_products(b, dgu, dff, hidden)
         dmid, dattn, gg_f = call(
             norm_back_kernel,
-            [held((micro_rows, d), F32), rows_low, held((1, d), F32)],
-            [*summands(send, mine), (dy, mid), gain_f],
+            [rows_f32, rows_low, held((1, d), F32)],
+            [*reduce_rows(send, mine), dy, mid, gain_f],
         )
         dattn = after(dattn, g_ffn)
         dattn, dq, dkv, dkv_send = call(
-            functools.partial(attend_back_kernel, layer=layer),
+            functools.partial(attend_back_kernel, parts=len(packs)),
             [
                 held((group, d)),
                 shape((group, q_width)),
                 shape((keys // 2, 2 * HD), F32),
                 shape((keys // 2, 2 * HD)),
             ],
-            [place, gather_rows(dattn) + [w_attn], (q, k, v), bias, (ctx, lse), cos, sin],
+            [place, gather_rows(dattn) + packs, (q, k, v), bias, (ctx, lse), cos, sin],
             [
                 pltpu.VMEM((d, q_width), BF16),
                 pltpu.VMEM((group, q_width), BF16),
@@ -855,39 +858,39 @@
             dkv.reshape(8, group // 2, 2 * HD), ("x", "ylo"), 0, 0, tiled=True
         )
         dqkv, send, mine, gg_a = call(
-            functools.partial(qkv_back_kernel, layer=layer),
+            functools.partial(qkv_back_kernel, parts=len(packs)),
             [held((group, wide)), *partials, held((1, d), F32)],
-            [place, [w_attn, rows], dq, arrived, cos, sin],
+            [place, packs + [rows], dq, arrived, cos, sin],
             [pltpu.VMEM((d, wide), BF16), pltpu.VMEM((group, d), BF16), DMA((8,)), DMA],
             room=16,
         )
         g_attn = attn_products(dattn, ctx, a, dqkv, gg_a, gg_f)
         dx, dx_low, _ = call(
             norm_back_kernel,
-            [held((micro_rows, d), F32), rows_low, held((1, d), F32)],
-            [*summands(send, mine), (dmid, x), gain_a],
-        )
-        return dx, after(dx_low, g_attn), g_attn, g_ffn, other
+            [rows_f32, rows_low, held((1, d), F32)],
+            [*reduce_rows(send, mine), dmid, x, gain_a],
+        )
+        return dx, after(dx_low, g_attn), g_attn, g_ffn, other, dqkv
 
     x0 = lax.dynamic_index_in_dim(block_input, section, 0, keepdims=False)
     dy1 = lax.dynamic_index_in_dim(out_grad, section, 0, keepdims=False)
 
-    rows0, a0, q0, kv0, ga0, gf0 = project(x0, 0)
+    rows0, a0, q0, kv0, ga0, gf0 = project(x0, attn0)
     ffn_pairs = pairs(place, ffn_shard, ffn_y)
-    w_ffn0 = gather_x(ffn_pairs[0])
+    w_ffn0 = gather_x(after(ffn_pairs[0], *attn0[1:], *attn1))
     kv0 = gather_kv(kv0)
-    ctx0, lse0, k0, v0, send, mine = attention(q0, kv0, 0)
-    mid0, b = call(add_norm_kernel, mid_outs, [*summands(send, mine), x0, gf0])
+    ctx0, lse0, k0, v0, send, mine = attention(q0, kv0, attn0)
+    mid0, b = call(add_norm_kernel, mid_outs, [*reduce_rows(send, mine), x0, gf0])
     w_ffn1 = gather_x(after(ffn_pairs[1], b))
     b0, up0, hidden0, send, mine = feed_forward(b, w_ffn0)
-    y0 = call(add_kernel, [rows_low], [*summands(send, mine), (mid0,)])[0]
-    kept0 = (x0, rows0, a0, q0, k0, v0, ctx0, lse0, mid0, b0, up0, hidden0, ga0, gf0, w_ffn0)
-    rows1, a1, q1, kv1, ga1, gf1 = project(y0, 1)
-    ctx1, lse1, k1, v1, send, mine = attention(q1, gather_kv(kv1), 1)
-    mid1, b = call(add_norm_kernel, mid_outs, [*summands(send, mine), y0, gf1])
+    y0 = call(add_kernel, [rows_low], [*reduce_rows(send, mine), mid0])[0]
+    kept0 = (x0, rows0, a0, q0, k0, v0, ctx0, lse0, mid0, b0, up0, hidden0, ga0, gf0, w_ffn0, attn0)
+    rows1, a1, q1, kv1, ga1, gf1 = project(y0, attn1)
+    ctx1, lse1, k1, v1, send, mine = attention(q1, gather_kv(kv1), attn1)
+    mid1, b = call(add_norm_kernel, mid_outs, [*reduce_rows(send, mine), y0, gf1])
     b1, up1, hidden1, send, mine = feed_forward(b, w_ffn1)
-    y1 = call(add_kernel, [rows_low], [*summands(send, mine), (mid1,)])[0]
-    kept1 = (y0, rows1, a1, q1, k1, v1, ctx1, lse1, mid1, b1, up1, hidden1, ga1, gf1, w_ffn1)
+    last = (send, mine, mid1)
+    kept1 = (y0, rows1, a1, q1, k1, v1, ctx1, lse1, mid1, b1, up1, hidden1, ga1, gf1, w_ffn1, attn1)
 
     early = section == 0
 
@@ -897,31 +900,32 @@
         other = swap_section(other).astype(dtype)
         return jnp.stack([jnp.where(early, mine, other), jnp.where(early, other, mine)])[None]
 
+    dx1, dx1_low, g_attn1, g_ffn1, _, _ = backward(dy1, kept1)
+    ffn1 = reduce_x(g_ffn1)
+    dx0, dx0_low, g_attn0, g_ffn0, r_attn1, dqkv0 = backward(dx1_low, kept0, (g_attn1, ffn1))
+    send, mine, mid1 = last
+    y1 = call(add_kernel, [rows_low], [*reduce_rows(after(send, dqkv0), mine), mid1])[0]
     block_output = both_micros(y0, y1, BF16)
-
-    dx1, dx1_low, g_attn1, g_ffn1, _ = backward(dy1, kept1, 1)
-    ffn1 = reduce_x(g_ffn1)
-    dx0, dx0_low, g_attn0, g_ffn0, r_attn1 = backward(dx1_low, kept0, 0, (g_attn1, ffn1, block_output))
     input_grad = both_micros(dx0, dx1, F32)
-    ffn_y = reduce_y(after(reduce_x(g_ffn0), input_grad), ffn1, place)
+    ffn_y = reduce_y(after(reduce_x(g_ffn0), input_grad, block_output), ffn1, place)
 
     attn_y = reduce_y(reduce_x(g_attn0), r_attn1, place)
     ffn_parts = by_core([after(ffn_y[0], attn_y[0]), *ffn_y[1:]], place)
-    attn_parts = by_core(attn_y, place)
 
     def finish(kernel, dims, parts):
         return call(kernel, [held(s, F32) for s in dims], [place, parts], room=20)
 
     own = own_rows
+    grad_gate, grad_up, grad_down = finish(
+        ffn_grads_kernel, [(own, 2 * units)] * 2 + [(2 * units, own)], ffn_parts
+    )
+    attn_parts = by_core(attn_y, place)
     grad_out, grad_query, grad_key, grad_value, *gain_pieces, _ = finish(
         attn_grads_kernel,
-        [(2 * q_width, own), (own, 2 * q_width), (own, HD), (own, HD)]
+        [(2 * q_width, own), (own, 2 * q_width), (HD, own), (HD, own)]
         + [(micro_rows, 128)] * 4
         + [(own, 128)],
         attn_parts,
-    )
-    grad_gate, grad_up, grad_down = finish(
-        ffn_grads_kernel, [(own, 2 * units)] * 2 + [(2 * units, own)], ffn_parts
     )
     gain_sums = gain_pieces[0]
     for k in (1, 2, 3):
@@ -934,8 +938,8 @@
         input_grad,
         gain_sums[0][None],
         grad_query[None],
-        grad_key[None],
-        grad_value[None],
+        grad_key.T[None],
+        grad_value.T[None],
         grad_out[None],
         gain_sums[1][None],
         grad_gate[None],

time: 649 us -> 639 us (0.985)
  Pallas kernels: 163 us -> 135 us
  blocking collectives: 26.5 us -> 40.8 us
  local copies, waits for them, and re-layouts: 30.3 us -> 39 us
    pallas_call x46, Pallas kernels: 163 us -> 135 us  [call(): pl.pallas_call(kernel, out_shape=tuple(outs), in_specs=specs, out_specs=t...]
    ppermute x4 -> x5, waiting for transfers between devices: 21.2 us -> 41.2 us  [swap_across(): return lax.ppermute(v, ('section', 'ylo'), [(0, 3), (3, 0), (1, 2), (2, 1)])]
    ppermute x6 -> x5, waiting for transfers between devices: 38.4 us -> 19.3 us  [swap_section(): return lax.ppermute(v, 'section', [(0, 1), (1, 0)])]
    ppermute x51, waiting for transfers between devices: 58.5 us -> 40.6 us  [from_z(): return lax.ppermute(rows, 'tp', [((i + by) % 4, i) for i in range(4)])]
    ppermute x51, starting transfers between devices: 58.5 us -> 75 us  [from_z(): return lax.ppermute(rows, 'tp', [((i + by) % 4, i) for i in range(4)])]
    ppermute x4 -> x5, waiting for transfers between devices: 27.3 us -> 11.3 us  [swap_ylo(): return lax.ppermute(v, 'ylo', [(0, 1), (1, 0)])]
    all_to_all x1 -> x2, blocking collectives: 12.8 us -> 27.1 us  [backward(): lax.all_to_all(dkv.reshape(8, group // 2, 2 * HD), ('x', 'ylo'), 0, 0, ti...]
    ppermute x48, starting transfers between devices: 64.3 us -> 50.4 us  [swap_core(): return lax.ppermute(v, 'core', [(0, 1), (1, 0)])]
  transfers between devices with their start and end apart: 122 -> 125, of which waited for: 56 -> 68; matrix products, arithmetic and copies ran while one was open for 3% -> 1% of each run, Pallas kernels for 22% -> 18%
where the time goes in v4:
time: 639 us; the launch traced here: 629 us
  waiting for transfers between devices  239 us (37%)
  starting transfers between devices  156 us (24%)
  Pallas kernels  135 us (21%)
  blocking collectives  40.8 us (6%)
  local copies, waits for them, and re-layouts  39 us (6%)
  between operations  15.5 us (2%)
    pallas_call x46, Pallas kernels, call(): pl.pallas_call(kernel, out_shape=tuple(outs), in_specs=specs, out_specs=t...  135 us
    ppermute x51, starting transfers between devices, from_z(): return lax.ppermute(rows, 'tp', [((i + by) % 4, i) for i in range(4)])  75 us
    ppermute x48, starting transfers between devices, swap_core(): return lax.ppermute(v, 'core', [(0, 1), (1, 0)])  50.4 us
    reduce_scatter x4, waiting for transfers between devices, reduce_x(): return lax.psum_scatter(grad, 'x', scatter_dimension=0, tiled=True)  50 us
    ppermute x5, waiting for transfers between devices, swap_across(): return lax.ppermute(v, ('section', 'ylo'), [(0, 3), (3, 0), (1, 2), (2, 1)])  41.2 us
    ppermute x51, waiting for transfers between devices, from_z(): return lax.ppermute(rows, 'tp', [((i + by) % 4, i) for i in range(4)])  40.6 us
    unnamed x240, local copies, waits for them, and re-layouts  35.9 us
    all_gather x3, waiting for transfers between devices, gather_x(): return lax.all_gather(block, 'x', axis=0, tiled=True)  32.5 us
  transfers between devices with their start and end apart: 125, of which 68 were waited for; matrix products, arithmetic and copies ran while one was open for 1% of the time, Pallas kernels for 18%

profile of v4, /device:TPU:1, one launch (start us, length us, event | category | flops | bytes accessed | tf_op | source)
XLA Modules:
  0.0 629.3 jit_solution(2830814681934238663)
XLA Ops:
  23.0 7.4 %collective-permute-done.11.refs_0_ = bf16[272,640]{1,0:T(8,128)(2,1)S(1)} collective-permute-done((bf16[272,640]{1,0:T(8,128)(2,1)S(1)}, bf16[272,640]{1,0:T(8,128)(2,1)S(1)}, u32[]{:S(2)}, u32[]{:S(2)}) %collective-permute-start.11) | collective-permute-done | bytes 348192 | tf_op jit(solution)/shard_map/ppermute | solution.py:99
  30.5 7.9 %collective-permute-done.10.far_ref = bf16[272,640]{1,0:T(8,128)(2,1)S(1)} collective-permute-done((bf16[272,640]{1,0:T(8,128)(2,1)S(1)}, bf16[272,640]{1,0:T(8,128)(2,1)S(1)}, u32[]{:S(2)}, u32[]{:S(2)}) %collective-permute-start.10) | collective-permute-done | bytes 348192 | tf_op jit(solution)/shard_map/ppermute | solution.py:103
  50.0 19.8 %collective-permute-done.28.far_ref = bf16[256,2176]{1,0:T(8,128)(2,1)S(1)} collective-permute-done((bf16[256,2176]{1,0:T(8,128)(2,1)}, bf16[256,2176]{1,0:T(8,128)(2,1)S(1)}, u32[]{:S(2)}, u32[]{:S(2)}) %collective-permute-start.28) | collective-permute-done | bytes 1114144 | tf_op jit(solution)/shard_map/ppermute | solution.py:103
  72.7 10.4 %collective-permute-done.29.refs_0_ = bf16[128,2176]{1,0:T(8,128)(2,1)S(1)} collective-permute-done((bf16[128,2176]{1,0:T(8,128)(2,1)S(1)}, bf16[128,2176]{1,0:T(8,128)(2,1)S(1)}, u32[]{:S(2)}, u32[]{:S(2)}) %collective-permute-start.29) | collective-permute-done | bytes 557088 | tf_op jit(solution)/shard_map/ppermute | solution.py:95
  90.4 8.5 %collective-permute-done.13.refs_10_.refs_2_ = bf16[544,640]{1,0:T(8,128)(2,1)S(1)} collective-permute-done((bf16[544,640]{1,0:T(8,128)(2,1)}, bf16[544,640]{1,0:T(8,128)(2,1)S(1)}, u32[]{:S(2)}, u32[]{:S(2)}) %collective-permute-start.13) | collective-permute-done | bytes 696352 | tf_op jit(solution)/shard_map/ppermute | solution.py:87
  128.4 9.3 %all-to-all-done = bf16[8,128,128]{2,1,0:T(8,128)(2,1)S(1)} async-done(((bf16[8,128,128]{2,1,0:T(8,128)(2,1)}), bf16[8,128,128]{2,1,0:T(8,128)(2,1)S(1)}, u32[]{:S(2)}, u32[]{:S(2)}) %all-to-all-start) | async-done | bytes 262176 | tf_op jit(solution)/shard_map/all_to_all | solution.py:127
  170.9 24.0 %all-gather.6.cloned.1.call-done.refs_8_ = bf16[2048,2176]{1,0:T(8,128)(2,1)} async-done(((bf16[512,2176]{1,0:T(8,128)(2,1)}), bf16[2048,2176]{1,0:T(8,128)(2,1)}) %all-gather.6.cloned.1.call-update) | async-done | bytes 8912912 | tf_op jit(solution)/shard_map/all_gather | solution.py:137
  194.9 6.8 %ffn_kernel.2 = (bf16[256,2048]{1,0:T(8,128)(2,1)}, f32[256,1408]{1,0:T(8,128)}, bf16[256,768]{1,0:T(8,128)(2,1)}, bf16[128,2048]{1,0:T(8,128)(2,1)S(1)}, f32[128,2048]{1,0:T(8,128)S(1)}) custom-call(bf16[32,2048]{1,0:T(8,128)(2,1)} %copy-done.35, bf16[32,2048]{1,0:T(8,128)(2,1)} %copy-done.87, bf16[32,2048]{1,0:T(8,128)(2,1)} %copy-done.83, ...), custom_call_target="tpu_custom_call" | custom-call | flops 1 | bytes 1 | tf_op jit(solution)/shard_map/ffn_kernel/pallas_call | solution.py:66
  231.5 13.7 %all_to_all.20 = bf16[8,128,128]{2,1,0:T(8,128)(2,1)S(1)} all-to-all(bf16[8,128,128]{2,1,0:T(8,128)(2,1)S(1)} %broadcast_in_dim.61), channel_id=1, replica_groups=mesh['section'=2,'x'=4,'ylo'=2,'core'=2,'tp'=4] {'x','ylo'}, dimensions={0} | all-to-all | bytes 524288 | tf_op jit(solution)/shard_map/all_to_all | solution.py:127
  282.3 5.6 all-gather.8.cloned.1.call-done.refs_8_
  287.9 6.9 %ffn_kernel.3 = (bf16[256,2048]{1,0:T(8,128)(2,1)}, f32[256,1408]{1,0:T(8,128)}, bf16[256,768]{1,0:T(8,128)(2,1)}, bf16[128,2048]{1,0:T(8,128)(2,1)}, f32[128,2048]{1,0:T(8,128)S(1)}) custom-call(bf16[32,2048]{1,0:T(8,128)(2,1)} %copy-done.34, bf16[32,2048]{1,0:T(8,128)(2,1)} %collective-permute-done.47.refs_1_, bf16[32,2048]{1,0:T(8,128)(2,1)} %copy-done.75, ...), custom_call_target="tpu_custom_call" | custom-call | flops 1 | bytes 1 | tf_op jit(solution)/shard_map/ffn_kernel/pallas_call | solution.py:66
  295.8 6.8 %ffn_back_kernel.2 = (bf16[256,2048]{1,0:T(8,128)(2,1)}, bf16[256,1408]{1,0:T(8,128)(2,1)}, bf16[128,2048]{1,0:T(8,128)(2,1)S(1)}, f32[128,2048]{1,0:T(8,128)S(1)}) custom-call(bf16[32,2048]{1,0:T(8,128)(2,1)} %copy-done.6, bf16[32,2048]{1,0:T(8,128)(2,1)} %collective-permute-done.54.refs_1_, bf16[32,2048]{1,0:T(8,128)(2,1)} %collective-permute-done.55.refs_2_, ...), custom_call_target="tpu_custom_call" | custom-call | flops 1 | bytes 1 | tf_op jit(solution)/shard_map/ffn_back_kernel/pallas_call | solution.py:66
  304.5 5.9 ffn_product_kernel.2
  339.1 10.6 %attend_back_kernel.2 = (bf16[256,2048]{1,0:T(8,128)(2,1)}, bf16[256,256]{1,0:T(8,128)(2,1)S(1)}, f32[1024,128]{1,0:T(8,128)S(1)}, bf16[1024,128]{1,0:T(8,128)(2,1)S(1)}) custom-call(s32[5]{0:T(128)S(1)} %stack.41.place, bf16[32,2048]{1,0:T(8,128)(2,1)} %copy-done.37, bf16[32,2048]{1,0:T(8,128)(2,1)} %copy-done.88, bf16[32,2048]{1,0:T(8,128)(2,1)} %copy-done.84, ...), custom_call_target="tpu_custom_call" | custom-call | flops 1 | bytes 1 | tf_op jit(solution)/shard_map/attend_back_kernel/pallas_call | solution.py:66
  351.4 14.1 %all_to_all.21.refs_3_ = bf16[8,128,128]{2,1,0:T(8,128)(2,1)S(1)} all-to-all(bf16[8,128,128]{2,1,0:T(8,128)(2,1)S(1)} %bitcast.61), channel_id=1, replica_groups=mesh['section'=2,'x'=4,'ylo'=2,'core'=2,'tp'=4] {'x','ylo'}, dimensions={0} | all-to-all | bytes 524288 | tf_op jit(solution)/shard_map/all_to_all | solution.py:857
  391.5 7.6 %reduce-scatter.5.cloned.1.call-done.r1_ref = bf16[512,2176]{1,0:T(8,128)(2,1)} async-done(((bf16[2048,2176]{1,0:T(8,128)(2,1)}), bf16[512,2176]{1,0:T(8,128)(2,1)}) %reduce-scatter.5.cloned.1.call-update) | async-done | bytes 2228240 | tf_op jit(solution)/shard_map/reduce_scatter | solution.py:141
  412.4 6.8 %ffn_back_kernel.3 = (bf16[256,2048]{1,0:T(8,128)(2,1)}, bf16[256,1408]{1,0:T(8,128)(2,1)}, bf16[128,2048]{1,0:T(8,128)(2,1)S(1)}, f32[128,2048]{1,0:T(8,128)S(1)}) custom-call(bf16[32,2048]{1,0:T(8,128)(2,1)} %copy-done.21, bf16[32,2048]{1,0:T(8,128)(2,1)} %copy-done.93, bf16[32,2048]{1,0:T(8,128)(2,1)} %copy-done.89, bf16[32,2048]{1,0:T(8,128)(2,1)} %copy-done.85, ...), custom_call_target="tpu_custom_call" | custom-call | flops 1 | bytes 1 | tf_op jit(solution)/shard_map/ffn_back_kernel/pallas_call | solution.py:66
  421.0 6.0 ffn_product_kernel.3
  455.7 10.8 %attend_back_kernel.3 = (bf16[256,2048]{1,0:T(8,128)(2,1)}, bf16[256,256]{1,0:T(8,128)(2,1)S(1)}, f32[1024,128]{1,0:T(8,128)S(1)}, bf16[1024,128]{1,0:T(8,128)(2,1)}) custom-call(s32[5]{0:T(128)S(1)} %stack.41.place, bf16[32,2048]{1,0:T(8,128)(2,1)} %copy-done.36, bf16[32,2048]{1,0:T(8,128)(2,1)} %copy-done.86, bf16[32,2048]{1,0:T(8,128)(2,1)} %copy-done.82, ...), custom_call_target="tpu_custom_call" | custom-call | flops 1 | bytes 1 | tf_op jit(solution)/shard_map/attend_back_kernel/pallas_call | solution.py:66
  470.1 13.0 %all_to_all.22.refs_6_ = bf16[8,128,128]{2,1,0:T(8,128)(2,1)S(1)} all-to-all(bf16[8,128,128]{2,1,0:T(8,128)(2,1)S(1)} %bitcast.62), channel_id=1, replica_groups=mesh['section'=2,'x'=4,'ylo'=2,'core'=2,'tp'=4] {'x','ylo'}, dimensions={0} | all-to-all | bytes 524288 | tf_op jit(solution)/shard_map/all_to_all | solution.py:857
  518.7 10.3 %reduce-scatter.11.cloned.1.call-done.r0_ref = bf16[512,2176]{1,0:T(8,128)(2,1)} async-done(((bf16[2048,2176]{1,0:T(8,128)(2,1)}), bf16[512,2176]{1,0:T(8,128)(2,1)}) %reduce-scatter.11.cloned.1.call-update) | async-done | bytes 2228240 | tf_op jit(solution)/shard_map/reduce_scatter | solution.py:141
  537.3 32.0 %reduce-scatter.9.cloned.1.call-done.r0_ref = bf16[512,768]{1,0:T(8,128)(2,1)} async-done(((bf16[2048,768]{1,0:T(8,128)(2,1)}), bf16[512,768]{1,0:T(8,128)(2,1)}) %reduce-scatter.9.cloned.1.call-update) | async-done | bytes 786448 | tf_op jit(solution)/shard_map/reduce_scatter | solution.py:141
  575.8 9.8 %collective-permute-done.115.refs_3_ = bf16[256,2176]{1,0:T(8,128)(2,1)} collective-permute-done((bf16[256,2176]{1,0:T(8,128)(2,1)}, bf16[256,2176]{1,0:T(8,128)(2,1)}, u32[]{:S(2)}, u32[]{:S(2)}) %collective-permute-start.115) | collective-permute-done | bytes 1114144 | tf_op jit(solution)/shard_map/ppermute | solution.py:99
  591.8 11.7 %collective-permute-done.107.refs_2_ = bf16[256,768]{1,0:T(8,128)(2,1)S(1)} collective-permute-done((bf16[256,768]{1,0:T(8,128)(2,1)}, bf16[256,768]{1,0:T(8,128)(2,1)S(1)}, u32[]{:S(2)}, u32[]{:S(2)}) %collective-permute-start.107) | collective-permute-done | bytes 393248 | tf_op jit(solution)/shard_map/ppermute | solution.py:103
  (558 shorter events, 348.0 us)
Async XLA Ops:
  7.2 94.6 %all-gather.4.cloned.1.call-start = ((), (), s32[]{:S(2)}) async-start(), calls=%async_computation.8 | async-start | bytes 3481600 | tf_op jit(solution)/shard_map/all_gather | solution.py:137
  22.2 16.1 %collective-permute-start.10 = (bf16[272,640]{1,0:T(8,128)(2,1)S(1)}, bf16[272,640]{1,0:T(8,128)(2,1)S(1)}, u32[]{:S(2)}, u32[]{:S(2)}) collective-permute-start(bf16[272,640]{1,0:T(8,128)(2,1)S(1)} %copy-done.59), channel_id=1, source_target_pairs={{0,72},{72,0},{8,64},{64,8},{1,73},{73,1},{9,65},{65,9},{2,74},{74... | collective-permute-start | bytes 1044488 | tf_op jit(solution)/shard_map/ppermute | solution.py:103
  23.0 15.3 %collective-permute-start.9 = (bf16[272,640]{1,0:T(8,128)(2,1)S(1)}, bf16[272,640]{1,0:T(8,128)(2,1)S(1)}, u32[]{:S(2)}, u32[]{:S(2)}) collective-permute-start(bf16[272,640]{1,0:T(8,128)(2,1)S(1)} %copy-done.59), channel_id=1, source_target_pairs={{0,8},{8,0},{1,9},{9,1},{2,10},{10,2},{3,11},{11,3},{4,12},{12,4},... | collective-permute-start | bytes 1044488 | tf_op jit(solution)/shard_map/ppermute | solution.py:95
  42.3 152.6 %all-gather.6.cloned.1.call-start = ((), (), s32[]{:S(2)}) async-start(), calls=%async_computation.9 | async-start | bytes 11141120 | tf_op jit(solution)/shard_map/all_gather | solution.py:137
  42.3 27.5 %collective-permute-start.28 = (bf16[256,2176]{1,0:T(8,128)(2,1)}, bf16[256,2176]{1,0:T(8,128)(2,1)S(1)}, u32[]{:S(2)}, u32[]{:S(2)}) collective-permute-start(bf16[256,2176]{1,0:T(8,128)(2,1)} %chip_rows_kernel.1.own_ref), channel_id=1, source_target_pairs={{0,72},{72,0},{8,64},{64,8},{1,73},{73,1},{9,65},{65,9},{2,74},{74... | collective-permute-start | bytes 3342344 | tf_op jit(solution)/shard_map/ppermute | solution.py:103
  45.2 25.6 %collective-permute-start.27 = (bf16[256,2176]{1,0:T(8,128)(2,1)}, bf16[256,2176]{1,0:T(8,128)(2,1)S(1)}, u32[]{:S(2)}, u32[]{:S(2)}) collective-permute-start(bf16[256,2176]{1,0:T(8,128)(2,1)} %chip_rows_kernel.1.own_ref), channel_id=1, source_target_pairs={{0,8},{8,0},{1,9},{9,1},{2,10},{10,2},{3,11},{11,3},{4,12},{12,4},... | collective-permute-start | bytes 3342344 | tf_op jit(solution)/shard_map/ppermute | solution.py:95
  45.2 45.2 %collective-permute-start.14 = (bf16[544,640]{1,0:T(8,128)(2,1)}, bf16[544,640]{1,0:T(8,128)(2,1)S(1)}, u32[]{:S(2)}, u32[]{:S(2)}) collective-permute-start(bf16[544,640]{1,0:T(8,128)(2,1)} %get-tuple-element.162.refs_8_.refs_0_), channel_id=1, source_target_pairs={{48,0},{0,16},{16,32},{32,48},{49,1},{1,17},{17,33},{33,49},{50,2}... | collective-permute-start | bytes 2088968 | tf_op jit(solution)/shard_map/ppermute | solution.py:87
  46.4 52.5 %collective-permute-start.13 = (bf16[544,640]{1,0:T(8,128)(2,1)}, bf16[544,640]{1,0:T(8,128)(2,1)S(1)}, u32[]{:S(2)}, u32[]{:S(2)}) collective-permute-start(bf16[544,640]{1,0:T(8,128)(2,1)} %get-tuple-element.162.refs_8_.refs_0_), channel_id=1, source_target_pairs={{32,0},{48,16},{0,32},{16,48},{33,1},{49,17},{1,33},{17,49},{34,2}... | collective-permute-start | bytes 2088968 | tf_op jit(solution)/shard_map/ppermute | solution.py:87
  48.9 50.0 %collective-permute-start.12 = (bf16[544,640]{1,0:T(8,128)(2,1)}, bf16[544,640]{1,0:T(8,128)(2,1)S(1)}, u32[]{:S(2)}, u32[]{:S(2)}) collective-permute-start(bf16[544,640]{1,0:T(8,128)(2,1)} %get-tuple-element.162.refs_8_.refs_0_), channel_id=1, source_target_pairs={{16,0},{32,16},{48,32},{0,48},{17,1},{33,17},{49,33},{1,49},{18,2}... | collective-permute-start | bytes 2088968 | tf_op jit(solution)/shard_map/ppermute | solution.py:87
  128.0 159.9 %all-gather.8.cloned.1.call-start = ((), (), s32[]{:S(2)}) async-start(), calls=%async_computation.10 | async-start | bytes 11141120 | tf_op jit(solution)/shard_map/all_gather | solution.py:137
  157.4 241.8 %reduce-scatter.5.cloned.1.call-start = ((), (), s32[]{:S(2)}) async-start(), calls=%async_computation.11 | async-start | bytes 11141120 | tf_op jit(solution)/shard_map/reduce_scatter | solution.py:141
  277.8 18.1 %collective-permute-start.57 = (bf16[32,2048]{1,0:T(8,128)(2,1)S(1)}, bf16[32,2048]{1,0:T(8,128)(2,1)}, u32[]{:S(2)}, u32[]{:S(2)}) collective-permute-start(bf16[32,2048]{1,0:T(8,128)(2,1)S(1)} %dynamic-slice_bitcast_fusion.refs_0_.after_ref), channel_id=1, source_target_pairs={{0,4},{4,0},{1,5},{5,1},{2,6},{6,2},{3,7},{7,3},{8,12},{12,8},{9,1... | collective-permute-start | bytes 393224 | tf_op jit(solution)/shard_map/ppermute | solution.py:91
  280.4 15.4 %collective-permute-start.60 = (bf16[32,2048]{1,0:T(8,128)(2,1)}, bf16[32,2048]{1,0:T(8,128)(2,1)}, u32[]{:S(2)}, u32[]{:S(2)}) collective-permute-start(bf16[32,2048]{1,0:T(8,128)(2,1)} %collective-permute-done.56.refs_3_), channel_id=1, source_target_pairs={{0,4},{4,0},{1,5},{5,1},{2,6},{6,2},{3,7},{7,3},{8,12},{12,8},{9,1... | collective-permute-start | bytes 393224 | tf_op jit(solution)/shard_map/ppermute | solution.py:91
  280.5 15.3 %collective-permute-start.59 = (bf16[32,2048]{1,0:T(8,128)(2,1)}, bf16[32,2048]{1,0:T(8,128)(2,1)}, u32[]{:S(2)}, u32[]{:S(2)}) collective-permute-start(bf16[32,2048]{1,0:T(8,128)(2,1)} %collective-permute-done.55.refs_2_), channel_id=1, source_target_pairs={{0,4},{4,0},{1,5},{5,1},{2,6},{6,2},{3,7},{7,3},{8,12},{12,8},{9,1... | collective-permute-start | bytes 393224 | tf_op jit(solution)/shard_map/ppermute | solution.py:91
  310.4 157.0 %reduce-scatter.7.cloned.1.call-start = ((), (), s32[]{:S(2)}) async-start(), calls=%async_computation.12 | async-start | bytes 3932160 | tf_op jit(solution)/shard_map/reduce_scatter | solution.py:141
  399.1 129.9 %reduce-scatter.11.cloned.1.call-start = ((), (), s32[]{:S(2)}) async-start(), calls=%async_computation.14 | async-start | bytes 11141120 | tf_op jit(solution)/shard_map/reduce_scatter | solution.py:141
  427.0 142.4 %reduce-scatter.9.cloned.1.call-start = ((), (), s32[]{:S(2)}) async-start(), calls=%async_computation.13 | async-start | bytes 3932160 | tf_op jit(solution)/shard_map/reduce_scatter | solution.py:141
  533.7 41.3 %collective-permute-start.113 = (bf16[256,2176]{1,0:T(8,128)(2,1)}, bf16[256,2176]{1,0:T(8,128)(2,1)S(1)}, u32[]{:S(2)}, u32[]{:S(2)}) collective-permute-start(bf16[256,2176]{1,0:T(8,128)(2,1)} %get-tuple-element.295), channel_id=1, source_target_pairs={{0,8},{8,0},{1,9},{9,1},{2,10},{10,2},{3,11},{11,3},{4,12},{12,4},... | collective-permute-start | bytes 3342344 | tf_op jit(solution)/shard_map/ppermute | solution.py:95
  534.9 40.9 %collective-permute-start.114 = (bf16[256,2176]{1,0:T(8,128)(2,1)}, bf16[256,2176]{1,0:T(8,128)(2,1)S(1)}, u32[]{:S(2)}, u32[]{:S(2)}) collective-permute-start(bf16[256,2176]{1,0:T(8,128)(2,1)} %get-tuple-element.296), channel_id=1, source_target_pairs={{0,72},{72,0},{8,64},{64,8},{1,73},{73,1},{9,65},{65,9},{2,74},{74... | collective-permute-start | bytes 3342344 | tf_op jit(solution)/shard_map/ppermute | solution.py:103
  536.7 48.9 %collective-permute-start.115 = (bf16[256,2176]{1,0:T(8,128)(2,1)}, bf16[256,2176]{1,0:T(8,128)(2,1)}, u32[]{:S(2)}, u32[]{:S(2)}) collective-permute-start(bf16[256,2176]{1,0:T(8,128)(2,1)} %get-tuple-element.297), channel_id=1, source_target_pairs={{0,64},{64,0},{1,65},{65,1},{2,66},{66,2},{3,67},{67,3},{4,68},{68... | collective-permute-start | bytes 3342344 | tf_op jit(solution)/shard_map/ppermute | solution.py:99
  572.0 19.8 %collective-permute-start.106 = (bf16[256,768]{1,0:T(8,128)(2,1)}, bf16[256,768]{1,0:T(8,128)(2,1)S(1)}, u32[]{:S(2)}, u32[]{:S(2)}) collective-permute-start(bf16[256,768]{1,0:T(8,128)(2,1)} %get-tuple-element.279), channel_id=1, source_target_pairs={{0,8},{8,0},{1,9},{9,1},{2,10},{10,2},{3,11},{11,3},{4,12},{12,4},... | collective-permute-start | bytes 1179656 | tf_op jit(solution)/shard_map/ppermute | solution.py:95
  573.2 30.3 %collective-permute-start.107 = (bf16[256,768]{1,0:T(8,128)(2,1)}, bf16[256,768]{1,0:T(8,128)(2,1)S(1)}, u32[]{:S(2)}, u32[]{:S(2)}) collective-permute-start(bf16[256,768]{1,0:T(8,128)(2,1)} %get-tuple-element.280), channel_id=1, source_target_pairs={{0,72},{72,0},{8,64},{64,8},{1,73},{73,1},{9,65},{65,9},{2,74},{74... | collective-permute-start | bytes 1179656 | tf_op jit(solution)/shard_map/ppermute | solution.py:103
  575.0 28.5 %collective-permute-start.108 = (bf16[256,768]{1,0:T(8,128)(2,1)}, bf16[256,768]{1,0:T(8,128)(2,1)S(1)}, u32[]{:S(2)}, u32[]{:S(2)}) collective-permute-start(bf16[256,768]{1,0:T(8,128)(2,1)} %get-tuple-element.281), channel_id=1, source_target_pairs={{0,64},{64,0},{1,65},{65,1},{2,66},{66,2},{3,67},{67,3},{4,68},{68... | collective-permute-start | bytes 1179656 | tf_op jit(solution)/shard_map/ppermute | solution.py:99
  589.2 27.3 %collective-permute-start.116 = (bf16[128,2176]{1,0:T(8,128)(2,1)S(1)}, bf16[128,2176]{1,0:T(8,128)(2,1)S(1)}, u32[]{:S(2)}, u32[]{:S(2)}) collective-permute-start(bf16[128,2176]{1,0:T(8,128)(2,1)S(1)} %get-tuple-element.299), channel_id=1, source_target_pairs={{0,4},{4,0},{1,5},{5,1},{2,6},{6,2},{3,7},{7,3},{8,12},{12,8},{9,1... | collective-permute-start | bytes 1671176 | tf_op jit(solution)/shard_map/ppermute | solution.py:91
  (220 other events, 1555.2 us)
Sparse Core Ops, SparseCore 0:
  42.4 59.3 all-gather.3
  103.5 91.3 all-gather.5
  196.5 91.3 all-gather.7
  310.5 88.5 reduce-scatter.4
  401.4 37.9 reduce-scatter.6
  441.7 87.2 reduce-scatter.10
  531.4 37.9 reduce-scatter.8

commit v5 on v4

--- a/solution.py
+++ b/solution.py
@@ -50,7 +50,7 @@
     return pltpu.with_memory_space_constraint(v, pltpu.HBM)
 
 
-def call(kernel, outs, args, scratch=(), room=8, out_spec=None, moved=0):
+def call(kernel, outs, args, scratch=(), room=8, out_spec=None, moved=0, aliases=None):
     specs, values = [], []
     for a in args:
         if isinstance(a, (list, tuple)):
@@ -71,6 +71,7 @@
             VMEM if isinstance(o, jax.ShapeDtypeStruct) else out_spec or pl.BlockSpec() for o in outs
         ),
         scratch_shapes=list(scratch),
+        input_output_aliases=aliases or {},
         compiler_params=pltpu.CompilerParams(vmem_limit_bytes=room),
         cost_estimate=pl.CostEstimate(flops=moved, bytes_accessed=moved, transcendentals=0)
         if moved
@@ -570,7 +571,9 @@
     )[0]
 
 
-def attn_product_kernel(dattn, a, gg_a, gg_f, ctx, dqkv, out, whole, sems):
+def attn_product_kernel(dattn, a, gg_a, gg_f, ctx, dqkv, *refs, layer):
+    *_, out, whole, sems = refs
+    cols = pl.ds(layer * whole.shape[1], whole.shape[1])
     m, steps = ctx.shape[1], sems.shape[0]
     wide = m + dqkv.shape[1]
     rows = whole.shape[0] // steps
@@ -584,23 +587,53 @@
         gains = jnp.where(row == 0, ga, jnp.where(row == 1, gf, 0.0))
         whole[at, wide:] = gains.T.astype(BF16)
         here = pl.ds(i * rows, rows)
-        copies.append(pltpu.make_async_copy(whole.at[here, :], out.at[here, :], sems.at[i]))
+        copies.append(pltpu.make_async_copy(whole.at[here, :], out.at[here, cols], sems.at[i]))
         copies[-1].start()
     for c in copies:
         c.wait()
 
 
-def attn_products(dattn, ctx, a, dqkv, gg_a, gg_f):
-    dims = (a.shape[1], ctx.shape[1] + dqkv.shape[1] + 128)
+def attn_products(dattn, ctx, a, dqkv, gg_a, gg_f, layer, filled=None):
+    d, wide = a.shape[1], ctx.shape[1] + dqkv.shape[1] + 128
+    args = [(dattn, a, gg_a, gg_f, ctx, dqkv)]
     return call(
-        attn_product_kernel,
-        [pltpu.HBM(dims, BF16)],
-        [(dattn, a, gg_a, gg_f, ctx, dqkv)],
-        [pltpu.VMEM(dims, BF16), DMA((4,))],
+        functools.partial(attn_product_kernel, layer=layer),
+        [pltpu.HBM((d, 2 * wide), BF16)],
+        args if filled is None else args + [[filled]],
+        [pltpu.VMEM((d, wide), BF16), DMA((4,))],
         room=14,
+        out_spec=HBM,
         moved=12_000_000,
-        out_spec=HBM,
+        aliases=None if filled is None else {6: 0},
     )[0]
+
+
+def y_split_both_kernel(place, r_ref, keep_ref, near_ref, far_ref, straight_ref):
+    n, c = keep_ref.shape
+    here = pl.ds(pl.multiple_of(place[YLO] * n, n), n)
+    there = pl.ds(pl.multiple_of((1 - place[YLO]) * n, n), n)
+
+    def fill(mine, other):
+        keep_ref[...] = r_ref[here, mine]
+        near_ref[...] = r_ref[there, mine]
+        straight_ref[...] = r_ref[here, other]
+        far_ref[...] = r_ref[there, other]
+
+    @pl.when(place[SECTION] == 0)
+    def _():
+        fill(slice(0, c), slice(c, 2 * c))
+
+    @pl.when(place[SECTION] == 1)
+    def _():
+        fill(slice(c, 2 * c), slice(0, c))
+
+
+def reduce_y_both(r, place):
+    dims = (r.shape[0] // 2, r.shape[1] // 2)
+    keep, near, far, straight = call(
+        y_split_both_kernel, [held(dims)] * 4, [place, (r,)], room=16
+    )
+    return [keep, swap_ylo(near), swap_across(far), swap_section(straight)]
 
 
 def y_split_kernel(place, r0_ref, r1_ref, keep_ref, near_ref, far_ref, straight_ref):
@@ -810,9 +843,8 @@
             room=16,
         )
 
-    def backward(dy, kept, pending=None):
+    def backward(dy, kept, layer, filled=None, pending=()):
         x, rows, a, q, k, v, ctx, lse, mid, b, gu, hidden, gain_a, gain_f, w_ffn, packs = kept
-        other = pending and reduce_x(after(pending[0], *pending[1:], dy))
         dff, dgu, send, mine = call(
             ffn_back_kernel,
             [held((group, d)), held((group, 2 * units)), *partials],
@@ -832,7 +864,7 @@
             [rows_f32, rows_low, held((1, d), F32)],
             [*reduce_rows(send, mine), dy, mid, gain_f],
         )
-        dattn = after(dattn, g_ffn)
+        dattn = after(dattn, g_ffn, *pending)
         dattn, dq, dkv, dkv_send = call(
             functools.partial(attend_back_kernel, parts=len(packs)),
             [
@@ -852,7 +884,6 @@
             ],
             room=18,
         )
-        dkv = after(dkv, other) if pending else dkv
         dkv = call(kv_add_kernel, [shape(dkv.shape)], [dkv, swap_core(dkv_send)])[0]
         arrived = lax.all_to_all(
             dkv.reshape(8, group // 2, 2 * HD), ("x", "ylo"), 0, 0, tiled=True
@@ -864,13 +895,13 @@
             [pltpu.VMEM((d, wide), BF16), pltpu.VMEM((group, d), BF16), DMA((8,)), DMA],
             room=16,
         )
-        g_attn = attn_products(dattn, ctx, a, dqkv, gg_a, gg_f)
+        g_attn = attn_products(dattn, ctx, a, dqkv, gg_a, gg_f, layer, filled)
         dx, dx_low, _ = call(
             norm_back_kernel,
             [rows_f32, rows_low, held((1, d), F32)],
             [*reduce_rows(send, mine), dmid, x, gain_a],
         )
-        return dx, after(dx_low, g_attn), g_attn, g_ffn, other, dqkv
+        return dx, after(dx_low, g_attn), g_attn, g_ffn, dqkv
 
     x0 = lax.dynamic_index_in_dim(block_input, section, 0, keepdims=False)
     dy1 = lax.dynamic_index_in_dim(out_grad, section, 0, keepdims=False)
@@ -900,16 +931,16 @@
         other = swap_section(other).astype(dtype)
         return jnp.stack([jnp.where(early, mine, other), jnp.where(early, other, mine)])[None]
 
-    dx1, dx1_low, g_attn1, g_ffn1, _, _ = backward(dy1, kept1)
+    dx1, dx1_low, g_attn1, g_ffn1, _ = backward(dy1, kept1, 1)
     ffn1 = reduce_x(g_ffn1)
-    dx0, dx0_low, g_attn0, g_ffn0, r_attn1, dqkv0 = backward(dx1_low, kept0, (g_attn1, ffn1))
+    dx0, dx0_low, g_attn, g_ffn0, dqkv0 = backward(dx1_low, kept0, 0, g_attn1, [ffn1])
     send, mine, mid1 = last
     y1 = call(add_kernel, [rows_low], [*reduce_rows(after(send, dqkv0), mine), mid1])[0]
     block_output = both_micros(y0, y1, BF16)
     input_grad = both_micros(dx0, dx1, F32)
     ffn_y = reduce_y(after(reduce_x(g_ffn0), input_grad, block_output), ffn1, place)
 
-    attn_y = reduce_y(reduce_x(g_attn0), r_attn1, place)
+    attn_y = reduce_y_both(reduce_x(g_attn), place)
     ffn_parts = by_core([after(ffn_y[0], attn_y[0]), *ffn_y[1:]], place)
 
     def finish(kernel, dims, parts):

time: 639 us -> 622 us (0.973)
  local copies, waits for them, and re-layouts: 39 us -> 29.4 us
  waiting for transfers between devices: 239 us -> 231 us
    ppermute x5, waiting for transfers between devices: 41.2 us -> 31.5 us  [swap_across(): return lax.ppermute(v, ('section', 'ylo'), [(0, 3), (3, 0), (1, 2), (2, 1)])]
    unnamed x240 -> x216, local copies, waits for them, and re-layouts: 35.9 us -> 26.4 us
    reduce_scatter x4 -> x3, waiting for transfers between devices: 50 us -> 52.7 us  [reduce_x(): return lax.psum_scatter(grad, 'x', scatter_dimension=0, tiled=True)]
  transfers between devices with their start and end apart: 125 -> 124, of which waited for: 68 -> 68; matrix products, arithmetic and copies ran while one was open for 1% -> 1% of each run, Pallas kernels for 18% -> 19%
where the time goes in v5:
time: 622 us; the launch traced here: 612 us
  waiting for transfers between devices  231 us (37%)
  starting transfers between devices  158 us (25%)
  Pallas kernels  134 us (22%)
  blocking collectives  40.3 us (6%)
  local copies, waits for them, and re-layouts  29.4 us (5%)
  between operations  15.4 us (2%)
    pallas_call x46, Pallas kernels, call(): pl.pallas_call(kernel, out_shape=tuple(outs), in_specs=specs, out_specs=t...  134 us
    ppermute x51, starting transfers between devices, from_z(): return lax.ppermute(rows, 'tp', [((i + by) % 4, i) for i in range(4)])  73.9 us
    ppermute x48, starting transfers between devices, swap_core(): return lax.ppermute(v, 'core', [(0, 1), (1, 0)])  52.8 us
    reduce_scatter x3, waiting for transfers between devices, reduce_x(): return lax.psum_scatter(grad, 'x', scatter_dimension=0, tiled=True)  52.7 us
    ppermute x51, waiting for transfers between devices, from_z(): return lax.ppermute(rows, 'tp', [((i + by) % 4, i) for i in range(4)])  41.1 us
    all_gather x3, waiting for transfers between devices, gather_x(): return lax.all_gather(block, 'x', axis=0, tiled=True)  32.6 us
    ppermute x5, waiting for transfers between devices, swap_across(): return lax.ppermute(v, ('section', 'ylo'), [(0, 3), (3, 0), (1, 2), (2, 1)])  31.5 us
    all_to_all x2, blocking collectives, backward(): lax.all_to_all(dkv.reshape(8, group // 2, 2 * HD), ('x', 'ylo'), 0, 0, ti...  26.5 us
  transfers between devices with their start and end apart: 124, of which 68 were waited for; matrix products, arithmetic and copies ran while one was open for 1% of the time, Pallas kernels for 19%

profile of v5, /device:TPU:1, one launch (start us, length us, event | category | flops | bytes accessed | tf_op | source)
XLA Modules:
  0.0 612.4 jit_solution(4283623855390319797)
XLA Ops:
  23.0 7.4 %collective-permute-done.11.refs_0_ = bf16[272,640]{1,0:T(8,128)(2,1)S(1)} collective-permute-done((bf16[272,640]{1,0:T(8,128)(2,1)S(1)}, bf16[272,640]{1,0:T(8,128)(2,1)S(1)}, u32[]{:S(2)}, u32[]{:S(2)}) %collective-permute-start.11) | collective-permute-done | bytes 348192 | tf_op jit(solution)/shard_map/ppermute | solution.py:100
  30.4 7.9 %collective-permute-done.10.far_ref = bf16[272,640]{1,0:T(8,128)(2,1)S(1)} collective-permute-done((bf16[272,640]{1,0:T(8,128)(2,1)S(1)}, bf16[272,640]{1,0:T(8,128)(2,1)S(1)}, u32[]{:S(2)}, u32[]{:S(2)}) %collective-permute-start.10) | collective-permute-done | bytes 348192 | tf_op jit(solution)/shard_map/ppermute | solution.py:104
  50.0 19.8 %collective-permute-done.28.far_ref = bf16[256,2176]{1,0:T(8,128)(2,1)S(1)} collective-permute-done((bf16[256,2176]{1,0:T(8,128)(2,1)}, bf16[256,2176]{1,0:T(8,128)(2,1)S(1)}, u32[]{:S(2)}, u32[]{:S(2)}) %collective-permute-start.28) | collective-permute-done | bytes 1114144 | tf_op jit(solution)/shard_map/ppermute | solution.py:104
  72.6 10.4 %collective-permute-done.29.refs_0_ = bf16[128,2176]{1,0:T(8,128)(2,1)S(1)} collective-permute-done((bf16[128,2176]{1,0:T(8,128)(2,1)S(1)}, bf16[128,2176]{1,0:T(8,128)(2,1)S(1)}, u32[]{:S(2)}, u32[]{:S(2)}) %collective-permute-start.29) | collective-permute-done | bytes 557088 | tf_op jit(solution)/shard_map/ppermute | solution.py:96
  90.4 8.5 %collective-permute-done.13.refs_10_.refs_2_ = bf16[544,640]{1,0:T(8,128)(2,1)S(1)} collective-permute-done((bf16[544,640]{1,0:T(8,128)(2,1)}, bf16[544,640]{1,0:T(8,128)(2,1)S(1)}, u32[]{:S(2)}, u32[]{:S(2)}) %collective-permute-start.13) | collective-permute-done | bytes 696352 | tf_op jit(solution)/shard_map/ppermute | solution.py:88
  123.1 4.8 all-to-all-start
  128.3 9.3 %all-to-all-done = bf16[8,128,128]{2,1,0:T(8,128)(2,1)S(1)} async-done(((bf16[8,128,128]{2,1,0:T(8,128)(2,1)}), bf16[8,128,128]{2,1,0:T(8,128)(2,1)S(1)}, u32[]{:S(2)}, u32[]{:S(2)}) %all-to-all-start) | async-done | bytes 262176 | tf_op jit(solution)/shard_map/all_to_all | solution.py:128
  140.2 5.5 attend_kernel.2
  170.8 24.0 %all-gather.6.cloned.1.call-done.refs_8_ = bf16[2048,2176]{1,0:T(8,128)(2,1)} async-done(((bf16[512,2176]{1,0:T(8,128)(2,1)}), bf16[2048,2176]{1,0:T(8,128)(2,1)}) %all-gather.6.cloned.1.call-update) | async-done | bytes 8912912 | tf_op jit(solution)/shard_map/all_gather | solution.py:138
  194.8 6.7 %ffn_kernel.2 = (bf16[256,2048]{1,0:T(8,128)(2,1)}, f32[256,1408]{1,0:T(8,128)}, bf16[256,768]{1,0:T(8,128)(2,1)}, bf16[128,2048]{1,0:T(8,128)(2,1)S(1)}, f32[128,2048]{1,0:T(8,128)S(1)}) custom-call(bf16[32,2048]{1,0:T(8,128)(2,1)} %copy-done.29, bf16[32,2048]{1,0:T(8,128)(2,1)} %copy-done.75, bf16[32,2048]{1,0:T(8,128)(2,1)} %copy-done.71, ...), custom_call_target="tpu_custom_call" | custom-call | flops 1 | bytes 1 | tf_op jit(solution)/shard_map/ffn_kernel/pallas_call | solution.py:66
  231.4 13.7 %all_to_all.20 = bf16[8,128,128]{2,1,0:T(8,128)(2,1)S(1)} all-to-all(bf16[8,128,128]{2,1,0:T(8,128)(2,1)S(1)} %broadcast_in_dim.61), channel_id=1, replica_groups=mesh['section'=2,'x'=4,'ylo'=2,'core'=2,'tp'=4] {'x','ylo'}, dimensions={0} | all-to-all | bytes 524288 | tf_op jit(solution)/shard_map/all_to_all | solution.py:128
  248.1 5.3 attend_kernel.3
  282.2 5.7 all-gather.8.cloned.1.call-done.refs_8_
  287.8 6.9 %ffn_kernel.3 = (bf16[256,2048]{1,0:T(8,128)(2,1)}, f32[256,1408]{1,0:T(8,128)}, bf16[256,768]{1,0:T(8,128)(2,1)}, bf16[128,2048]{1,0:T(8,128)(2,1)}, f32[128,2048]{1,0:T(8,128)S(1)}) custom-call(bf16[32,2048]{1,0:T(8,128)(2,1)} %copy-done.28, bf16[32,2048]{1,0:T(8,128)(2,1)} %collective-permute-done.47.refs_1_, bf16[32,2048]{1,0:T(8,128)(2,1)} %copy-done.63, ...), custom_call_target="tpu_custom_call" | custom-call | flops 1 | bytes 1 | tf_op jit(solution)/shard_map/ffn_kernel/pallas_call | solution.py:66
  295.8 6.8 %ffn_back_kernel.2 = (bf16[256,2048]{1,0:T(8,128)(2,1)}, bf16[256,1408]{1,0:T(8,128)(2,1)}, bf16[128,2048]{1,0:T(8,128)(2,1)S(1)}, f32[128,2048]{1,0:T(8,128)S(1)}) custom-call(bf16[32,2048]{1,0:T(8,128)(2,1)} %copy-done.6, bf16[32,2048]{1,0:T(8,128)(2,1)} %collective-permute-done.54.refs_1_, bf16[32,2048]{1,0:T(8,128)(2,1)} %collective-permute-done.55.refs_2_, ...), custom_call_target="tpu_custom_call" | custom-call | flops 1 | bytes 1 | tf_op jit(solution)/shard_map/ffn_back_kernel/pallas_call | solution.py:66
  304.5 5.9 ffn_product_kernel.2
  338.4 10.6 %attend_back_kernel.2 = (bf16[256,2048]{1,0:T(8,128)(2,1)}, bf16[256,256]{1,0:T(8,128)(2,1)S(1)}, f32[1024,128]{1,0:T(8,128)S(1)}, bf16[1024,128]{1,0:T(8,128)(2,1)S(1)}) custom-call(s32[5]{0:T(128)S(1)} %stack.41.place, bf16[32,2048]{1,0:T(8,128)(2,1)} %copy-done.31, bf16[32,2048]{1,0:T(8,128)(2,1)} %copy-done.76, bf16[32,2048]{1,0:T(8,128)(2,1)} %copy-done.72, ...), custom_call_target="tpu_custom_call" | custom-call | flops 1 | bytes 1 | tf_op jit(solution)/shard_map/attend_back_kernel/pallas_call | solution.py:66
  350.6 14.2 %all_to_all.21.refs_3_ = bf16[8,128,128]{2,1,0:T(8,128)(2,1)S(1)} all-to-all(bf16[8,128,128]{2,1,0:T(8,128)(2,1)S(1)} %bitcast.61), channel_id=1, replica_groups=mesh['section'=2,'x'=4,'ylo'=2,'core'=2,'tp'=4] {'x','ylo'}, dimensions={0} | all-to-all | bytes 524288 | tf_op jit(solution)/shard_map/all_to_all | solution.py:888
  395.8 6.9 %ffn_back_kernel.3 = (bf16[256,2048]{1,0:T(8,128)(2,1)}, bf16[256,1408]{1,0:T(8,128)(2,1)}, bf16[128,2048]{1,0:T(8,128)(2,1)S(1)}, f32[128,2048]{1,0:T(8,128)S(1)}) custom-call(bf16[32,2048]{1,0:T(8,128)(2,1)} %copy-done.21, bf16[32,2048]{1,0:T(8,128)(2,1)} %copy-done.81, bf16[32,2048]{1,0:T(8,128)(2,1)} %copy-done.77, bf16[32,2048]{1,0:T(8,128)(2,1)} %copy-done.73, ...), custom_call_target="tpu_custom_call" | custom-call | flops 1 | bytes 1 | tf_op jit(solution)/shard_map/ffn_back_kernel/pallas_call | solution.py:66
  404.4 5.9 ffn_product_kernel.3
  440.2 10.7 %attend_back_kernel.3 = (bf16[256,2048]{1,0:T(8,128)(2,1)}, bf16[256,256]{1,0:T(8,128)(2,1)S(1)}, f32[1024,128]{1,0:T(8,128)S(1)}, bf16[1024,128]{1,0:T(8,128)(2,1)S(1)}) custom-call(s32[5]{0:T(128)S(1)} %stack.41.place, bf16[32,2048]{1,0:T(8,128)(2,1)} %copy-done.30, bf16[32,2048]{1,0:T(8,128)(2,1)} %copy-done.74, bf16[32,2048]{1,0:T(8,128)(2,1)} %copy-done.70, ...), custom_call_target="tpu_custom_call" | custom-call | flops 1 | bytes 1 | tf_op jit(solution)/shard_map/attend_back_kernel/pallas_call | solution.py:66
  452.6 12.4 %all_to_all.22.refs_6_ = bf16[8,128,128]{2,1,0:T(8,128)(2,1)S(1)} all-to-all(bf16[8,128,128]{2,1,0:T(8,128)(2,1)S(1)} %bitcast.62), channel_id=1, replica_groups=mesh['section'=2,'x'=4,'ylo'=2,'core'=2,'tp'=4] {'x','ylo'}, dimensions={0} | all-to-all | bytes 524288 | tf_op jit(solution)/shard_map/all_to_all | solution.py:888
  509.1 52.7 %reduce-scatter.6.cloned.1.call-done.r_ref = bf16[512,1536]{1,0:T(8,128)(2,1)} async-done(((bf16[2048,1536]{1,0:T(8,128)(2,1)}), bf16[512,1536]{1,0:T(8,128)(2,1)}) %reduce-scatter.6.cloned.1.call-update) | async-done | bytes 1572880 | tf_op jit(solution)/shard_map/reduce_scatter | solution.py:142
  576.9 8.5 %collective-permute-done.108.refs_3_ = bf16[256,768]{1,0:T(8,128)(2,1)S(1)} collective-permute-done((bf16[256,768]{1,0:T(8,128)(2,1)}, bf16[256,768]{1,0:T(8,128)(2,1)S(1)}, u32[]{:S(2)}, u32[]{:S(2)}) %collective-permute-start.108) | collective-permute-done | bytes 393248 | tf_op jit(solution)/shard_map/ppermute | solution.py:100
  (531 shorter events, 326.3 us)
Async XLA Ops:
  7.2 94.6 %all-gather.4.cloned.1.call-start = ((), (), s32[]{:S(2)}) async-start(), calls=%async_computation.7 | async-start | bytes 3481600 | tf_op jit(solution)/shard_map/all_gather | solution.py:138
  22.2 16.1 %collective-permute-start.10 = (bf16[272,640]{1,0:T(8,128)(2,1)S(1)}, bf16[272,640]{1,0:T(8,128)(2,1)S(1)}, u32[]{:S(2)}, u32[]{:S(2)}) collective-permute-start(bf16[272,640]{1,0:T(8,128)(2,1)S(1)} %copy-done.47), channel_id=1, source_target_pairs={{0,72},{72,0},{8,64},{64,8},{1,73},{73,1},{9,65},{65,9},{2,74},{74... | collective-permute-start | bytes 1044488 | tf_op jit(solution)/shard_map/ppermute | solution.py:104
  22.9 15.3 %collective-permute-start.9 = (bf16[272,640]{1,0:T(8,128)(2,1)S(1)}, bf16[272,640]{1,0:T(8,128)(2,1)S(1)}, u32[]{:S(2)}, u32[]{:S(2)}) collective-permute-start(bf16[272,640]{1,0:T(8,128)(2,1)S(1)} %copy-done.47), channel_id=1, source_target_pairs={{0,8},{8,0},{1,9},{9,1},{2,10},{10,2},{3,11},{11,3},{4,12},{12,4},... | collective-permute-start | bytes 1044488 | tf_op jit(solution)/shard_map/ppermute | solution.py:96
  42.3 152.6 %all-gather.6.cloned.1.call-start = ((), (), s32[]{:S(2)}) async-start(), calls=%async_computation.8 | async-start | bytes 11141120 | tf_op jit(solution)/shard_map/all_gather | solution.py:138
  42.3 27.5 %collective-permute-start.28 = (bf16[256,2176]{1,0:T(8,128)(2,1)}, bf16[256,2176]{1,0:T(8,128)(2,1)S(1)}, u32[]{:S(2)}, u32[]{:S(2)}) collective-permute-start(bf16[256,2176]{1,0:T(8,128)(2,1)} %chip_rows_kernel.1.own_ref), channel_id=1, source_target_pairs={{0,72},{72,0},{8,64},{64,8},{1,73},{73,1},{9,65},{65,9},{2,74},{74... | collective-permute-start | bytes 3342344 | tf_op jit(solution)/shard_map/ppermute | solution.py:104
  45.2 25.6 %collective-permute-start.27 = (bf16[256,2176]{1,0:T(8,128)(2,1)}, bf16[256,2176]{1,0:T(8,128)(2,1)S(1)}, u32[]{:S(2)}, u32[]{:S(2)}) collective-permute-start(bf16[256,2176]{1,0:T(8,128)(2,1)} %chip_rows_kernel.1.own_ref), channel_id=1, source_target_pairs={{0,8},{8,0},{1,9},{9,1},{2,10},{10,2},{3,11},{11,3},{4,12},{12,4},... | collective-permute-start | bytes 3342344 | tf_op jit(solution)/shard_map/ppermute | solution.py:96
  45.2 45.2 %collective-permute-start.14 = (bf16[544,640]{1,0:T(8,128)(2,1)}, bf16[544,640]{1,0:T(8,128)(2,1)S(1)}, u32[]{:S(2)}, u32[]{:S(2)}) collective-permute-start(bf16[544,640]{1,0:T(8,128)(2,1)} %get-tuple-element.160.refs_8_.refs_0_), channel_id=1, source_target_pairs={{48,0},{0,16},{16,32},{32,48},{49,1},{1,17},{17,33},{33,49},{50,2}... | collective-permute-start | bytes 2088968 | tf_op jit(solution)/shard_map/ppermute | solution.py:88
  46.4 52.5 %collective-permute-start.13 = (bf16[544,640]{1,0:T(8,128)(2,1)}, bf16[544,640]{1,0:T(8,128)(2,1)S(1)}, u32[]{:S(2)}, u32[]{:S(2)}) collective-permute-start(bf16[544,640]{1,0:T(8,128)(2,1)} %get-tuple-element.160.refs_8_.refs_0_), channel_id=1, source_target_pairs={{32,0},{48,16},{0,32},{16,48},{33,1},{49,17},{1,33},{17,49},{34,2}... | collective-permute-start | bytes 2088968 | tf_op jit(solution)/shard_map/ppermute | solution.py:88
  48.8 50.0 %collective-permute-start.12 = (bf16[544,640]{1,0:T(8,128)(2,1)}, bf16[544,640]{1,0:T(8,128)(2,1)S(1)}, u32[]{:S(2)}, u32[]{:S(2)}) collective-permute-start(bf16[544,640]{1,0:T(8,128)(2,1)} %get-tuple-element.160.refs_8_.refs_0_), channel_id=1, source_target_pairs={{16,0},{32,16},{48,32},{0,48},{17,1},{33,17},{49,33},{1,49},{18,2}... | collective-permute-start | bytes 2088968 | tf_op jit(solution)/shard_map/ppermute | solution.py:88
  70.9 14.0 %collective-permute-start.30 = (bf16[128,2176]{1,0:T(8,128)(2,1)S(1)}, bf16[128,2176]{1,0:T(8,128)(2,1)S(1)}, u32[]{:S(2)}, u32[]{:S(2)}) collective-permute-start(bf16[128,2176]{1,0:T(8,128)(2,1)S(1)} %slice.21), channel_id=1, source_target_pairs={{0,72},{72,0},{8,64},{64,8},{1,73},{73,1},{9,65},{65,9},{2,74},{74... | collective-permute-start | bytes 1671176 | tf_op jit(solution)/shard_map/ppermute | solution.py:104
  123.1 14.5 %all-to-all-start = ((bf16[8,128,128]{2,1,0:T(8,128)(2,1)}), bf16[8,128,128]{2,1,0:T(8,128)(2,1)S(1)}, u32[]{:S(2)}, u32[]{:S(2)}) async-start(bf16[8,128,128]{2,1,0:T(8,128)(2,1)} %broadcast_in_dim.58), calls=%async_computation | async-start | bytes 524288 | tf_op jit(solution)/shard_map/all_to_all | solution.py:128
  127.9 159.9 %all-gather.8.cloned.1.call-start = ((), (), s32[]{:S(2)}) async-start(), calls=%async_computation.9 | async-start | bytes 11141120 | tf_op jit(solution)/shard_map/all_gather | solution.py:138
  157.3 269.0 %reduce-scatter.4.cloned.1.call-start = ((), (), s32[]{:S(2)}) async-start(), calls=%async_computation.10 | async-start | bytes 11141120 | tf_op jit(solution)/shard_map/reduce_scatter | solution.py:142
  277.7 18.1 %collective-permute-start.57 = (bf16[32,2048]{1,0:T(8,128)(2,1)S(1)}, bf16[32,2048]{1,0:T(8,128)(2,1)}, u32[]{:S(2)}, u32[]{:S(2)}) collective-permute-start(bf16[32,2048]{1,0:T(8,128)(2,1)S(1)} %dynamic-slice_bitcast_fusion.refs_0_.after_ref), channel_id=1, source_target_pairs={{0,4},{4,0},{1,5},{5,1},{2,6},{6,2},{3,7},{7,3},{8,12},{12,8},{9,1... | collective-permute-start | bytes 393224 | tf_op jit(solution)/shard_map/ppermute | solution.py:92
  280.3 15.4 %collective-permute-start.60 = (bf16[32,2048]{1,0:T(8,128)(2,1)}, bf16[32,2048]{1,0:T(8,128)(2,1)}, u32[]{:S(2)}, u32[]{:S(2)}) collective-permute-start(bf16[32,2048]{1,0:T(8,128)(2,1)} %collective-permute-done.56.refs_3_), channel_id=1, source_target_pairs={{0,4},{4,0},{1,5},{5,1},{2,6},{6,2},{3,7},{7,3},{8,12},{12,8},{9,1... | collective-permute-start | bytes 393224 | tf_op jit(solution)/shard_map/ppermute | solution.py:92
  280.4 15.3 %collective-permute-start.59 = (bf16[32,2048]{1,0:T(8,128)(2,1)}, bf16[32,2048]{1,0:T(8,128)(2,1)}, u32[]{:S(2)}, u32[]{:S(2)}) collective-permute-start(bf16[32,2048]{1,0:T(8,128)(2,1)} %collective-permute-done.55.refs_2_), channel_id=1, source_target_pairs={{0,4},{4,0},{1,5},{5,1},{2,6},{6,2},{3,7},{7,3},{8,12},{12,8},{9,1... | collective-permute-start | bytes 393224 | tf_op jit(solution)/shard_map/ppermute | solution.py:92
  281.7 14.0 %collective-permute-start.58 = (bf16[32,2048]{1,0:T(8,128)(2,1)}, bf16[32,2048]{1,0:T(8,128)(2,1)}, u32[]{:S(2)}, u32[]{:S(2)}) collective-permute-start(bf16[32,2048]{1,0:T(8,128)(2,1)} %collective-permute-done.54.refs_1_), channel_id=1, source_target_pairs={{0,4},{4,0},{1,5},{5,1},{2,6},{6,2},{3,7},{7,3},{8,12},{12,8},{9,1... | collective-permute-start | bytes 393224 | tf_op jit(solution)/shard_map/ppermute | solution.py:92
  310.4 190.5 %reduce-scatter.8.cloned.1.call-start = ((), (), s32[]{:S(2)}) async-start(), calls=%async_computation.12 | async-start | bytes 11141120 | tf_op jit(solution)/shard_map/reduce_scatter | solution.py:142
  410.4 151.5 %reduce-scatter.6.cloned.1.call-start = ((), (), s32[]{:S(2)}) async-start(), calls=%async_computation.11 | async-start | bytes 7864320 | tf_op jit(solution)/shard_map/reduce_scatter | solution.py:142
  505.5 62.1 %collective-permute-start.113 = (bf16[256,2176]{1,0:T(8,128)(2,1)}, bf16[256,2176]{1,0:T(8,128)(2,1)S(1)}, u32[]{:S(2)}, u32[]{:S(2)}) collective-permute-start(bf16[256,2176]{1,0:T(8,128)(2,1)} %get-tuple-element.291), channel_id=1, source_target_pairs={{0,8},{8,0},{1,9},{9,1},{2,10},{10,2},{3,11},{11,3},{4,12},{12,4},... | collective-permute-start | bytes 3342344 | tf_op jit(solution)/shard_map/ppermute | solution.py:96
  506.7 61.6 %collective-permute-start.114 = (bf16[256,2176]{1,0:T(8,128)(2,1)}, bf16[256,2176]{1,0:T(8,128)(2,1)S(1)}, u32[]{:S(2)}, u32[]{:S(2)}) collective-permute-start(bf16[256,2176]{1,0:T(8,128)(2,1)} %get-tuple-element.292), channel_id=1, source_target_pairs={{0,72},{72,0},{8,64},{64,8},{1,73},{73,1},{9,65},{65,9},{2,74},{74... | collective-permute-start | bytes 3342344 | tf_op jit(solution)/shard_map/ppermute | solution.py:104
  508.3 60.1 %collective-permute-start.115 = (bf16[256,2176]{1,0:T(8,128)(2,1)}, bf16[256,2176]{1,0:T(8,128)(2,1)}, u32[]{:S(2)}, u32[]{:S(2)}) collective-permute-start(bf16[256,2176]{1,0:T(8,128)(2,1)} %get-tuple-element.293), channel_id=1, source_target_pairs={{0,64},{64,0},{1,65},{65,1},{2,66},{66,2},{3,67},{67,3},{4,68},{68... | collective-permute-start | bytes 3342344 | tf_op jit(solution)/shard_map/ppermute | solution.py:100
  567.6 17.9 %collective-permute-start.108 = (bf16[256,768]{1,0:T(8,128)(2,1)}, bf16[256,768]{1,0:T(8,128)(2,1)S(1)}, u32[]{:S(2)}, u32[]{:S(2)}) collective-permute-start(bf16[256,768]{1,0:T(8,128)(2,1)} %get-tuple-element.277), channel_id=1, source_target_pairs={{0,64},{64,0},{1,65},{65,1},{2,66},{66,2},{3,67},{67,3},{4,68},{68... | collective-permute-start | bytes 1179656 | tf_op jit(solution)/shard_map/ppermute | solution.py:100
  572.9 26.7 %collective-permute-start.116 = (bf16[128,2176]{1,0:T(8,128)(2,1)S(1)}, bf16[128,2176]{1,0:T(8,128)(2,1)S(1)}, u32[]{:S(2)}, u32[]{:S(2)}) collective-permute-start(bf16[128,2176]{1,0:T(8,128)(2,1)S(1)} %get-tuple-element.295), channel_id=1, source_target_pairs={{0,4},{4,0},{1,5},{5,1},{2,6},{6,2},{3,7},{7,3},{8,12},{12,8},{9,1... | collective-permute-start | bytes 1671176 | tf_op jit(solution)/shard_map/ppermute | solution.py:92
  (207 other events, 1500.3 us)
Sparse Core Ops, SparseCore 0:
  42.4 59.3 all-gather.3
  103.5 91.3 all-gather.5
  196.5 91.3 all-gather.7
  310.5 88.5 reduce-scatter.3
  410.5 85.3 reduce-scatter.7
  498.2 63.6 reduce-scatter.5

commit v6 on v5

--- a/solution.py
+++ b/solution.py
@@ -668,7 +668,7 @@
 def by_core(parts, place):
     n, c = parts[0].shape[0] // 2, parts[0].shape[1]
     own, send = call(
-        by_core_kernel, [held((n, c), F32), shape((n, c))], [place, tuple(parts)], room=16
+        by_core_kernel, [held((n, c), F32), shape((n, c))], [place, tuple(parts)], room=16, moved=10_000_000
     )
     return own, swap_core(send)
 
@@ -944,13 +944,15 @@
     ffn_parts = by_core([after(ffn_y[0], attn_y[0]), *ffn_y[1:]], place)
 
     def finish(kernel, dims, parts):
-        return call(kernel, [held(s, F32) for s in dims], [place, parts], room=20)
+        return call(
+            kernel, [held(s, F32) for s in dims], [place, parts], room=20, moved=10_000_000
+        )
 
     own = own_rows
     grad_gate, grad_up, grad_down = finish(
         ffn_grads_kernel, [(own, 2 * units)] * 2 + [(2 * units, own)], ffn_parts
     )
-    attn_parts = by_core(attn_y, place)
+    attn_parts = by_core([after(attn_y[0], grad_gate), *attn_y[1:]], place)
     grad_out, grad_query, grad_key, grad_value, *gain_pieces, _ = finish(
         attn_grads_kernel,
         [(2 * q_width, own), (own, 2 * q_width), (HD, own), (HD, own)]

time: 622 us -> 626 us (level)
    ppermute x5, waiting for transfers between devices: 31.5 us -> 38.2 us  [swap_across(): return lax.ppermute(v, ('section', 'ylo'), [(0, 3), (3, 0), (1, 2), (2, 1)])]
    ppermute x5, waiting for transfers between devices: 18.1 us -> 11.4 us  [swap_section(): return lax.ppermute(v, 'section', [(0, 1), (1, 0)])]
    unnamed x216 -> x222, local copies, waits for them, and re-layouts: 26.4 us -> 26.6 us
  transfers between devices with their start and end apart: 124 -> 124, of which waited for: 68 -> 70; matrix products, arithmetic and copies ran while one was open for 1% -> 1% of each run, Pallas kernels for 19% -> 17%
where the time goes in v6:
time: 626 us; the launch traced here: 616 us
  waiting for transfers between devices  236 us (38%)
  starting transfers between devices  156 us (25%)
  Pallas kernels  134 us (21%)
  blocking collectives  40.2 us (6%)
  local copies, waits for them, and re-layouts  29.7 us (5%)
  between operations  15.5 us (2%)
    pallas_call x46, Pallas kernels, call(): pl.pallas_call(kernel, out_shape=tuple(outs), in_specs=specs, out_specs=t...  134 us
    ppermute x51, starting transfers between devices, from_z(): return lax.ppermute(rows, 'tp', [((i + by) % 4, i) for i in range(4)])  73.9 us
    reduce_scatter x3, waiting for transfers between devices, reduce_x(): return lax.psum_scatter(grad, 'x', scatter_dimension=0, tiled=True)  52.8 us
    ppermute x48, starting transfers between devices, swap_core(): return lax.ppermute(v, 'core', [(0, 1), (1, 0)])  51.7 us
    ppermute x51, waiting for transfers between devices, from_z(): return lax.ppermute(rows, 'tp', [((i + by) % 4, i) for i in range(4)])  42.9 us
    ppermute x5, waiting for transfers between devices, swap_across(): return lax.ppermute(v, ('section', 'ylo'), [(0, 3), (3, 0), (1, 2), (2, 1)])  38.2 us
    all_gather x3, waiting for transfers between devices, gather_x(): return lax.all_gather(block, 'x', axis=0, tiled=True)  32.7 us
    unnamed x222, local copies, waits for them, and re-layouts  26.6 us
  transfers between devices with their start and end apart: 124, of which 70 were waited for; matrix products, arithmetic and copies ran while one was open for 1% of the time, Pallas kernels for 17%

profile of v6, /device:TPU:1, one launch (start us, length us, event | category | flops | bytes accessed | tf_op | source)
XLA Modules:
  0.0 616.0 jit_solution(3104922677447974796)
XLA Ops:
  23.0 7.4 %collective-permute-done.11.refs_0_ = bf16[272,640]{1,0:T(8,128)(2,1)S(1)} collective-permute-done((bf16[272,640]{1,0:T(8,128)(2,1)S(1)}, bf16[272,640]{1,0:T(8,128)(2,1)S(1)}, u32[]{:S(2)}, u32[]{:S(2)}) %collective-permute-start.11) | collective-permute-done | bytes 348192 | tf_op jit(solution)/shard_map/ppermute | solution.py:100
  30.4 7.9 %collective-permute-done.10.far_ref = bf16[272,640]{1,0:T(8,128)(2,1)S(1)} collective-permute-done((bf16[272,640]{1,0:T(8,128)(2,1)S(1)}, bf16[272,640]{1,0:T(8,128)(2,1)S(1)}, u32[]{:S(2)}, u32[]{:S(2)}) %collective-permute-start.10) | collective-permute-done | bytes 348192 | tf_op jit(solution)/shard_map/ppermute | solution.py:104
  50.0 19.8 %collective-permute-done.28.far_ref = bf16[256,2176]{1,0:T(8,128)(2,1)S(1)} collective-permute-done((bf16[256,2176]{1,0:T(8,128)(2,1)}, bf16[256,2176]{1,0:T(8,128)(2,1)S(1)}, u32[]{:S(2)}, u32[]{:S(2)}) %collective-permute-start.28) | collective-permute-done | bytes 1114144 | tf_op jit(solution)/shard_map/ppermute | solution.py:104
  72.7 10.4 %collective-permute-done.29.refs_0_ = bf16[128,2176]{1,0:T(8,128)(2,1)S(1)} collective-permute-done((bf16[128,2176]{1,0:T(8,128)(2,1)S(1)}, bf16[128,2176]{1,0:T(8,128)(2,1)S(1)}, u32[]{:S(2)}, u32[]{:S(2)}) %collective-permute-start.29) | collective-permute-done | bytes 557088 | tf_op jit(solution)/shard_map/ppermute | solution.py:96
  90.4 8.5 %collective-permute-done.13.refs_10_.refs_2_ = bf16[544,640]{1,0:T(8,128)(2,1)S(1)} collective-permute-done((bf16[544,640]{1,0:T(8,128)(2,1)}, bf16[544,640]{1,0:T(8,128)(2,1)S(1)}, u32[]{:S(2)}, u32[]{:S(2)}) %collective-permute-start.13) | collective-permute-done | bytes 696352 | tf_op jit(solution)/shard_map/ppermute | solution.py:88
  123.1 4.8 all-to-all-start
  128.3 9.3 %all-to-all-done = bf16[8,128,128]{2,1,0:T(8,128)(2,1)S(1)} async-done(((bf16[8,128,128]{2,1,0:T(8,128)(2,1)}), bf16[8,128,128]{2,1,0:T(8,128)(2,1)S(1)}, u32[]{:S(2)}, u32[]{:S(2)}) %all-to-all-start) | async-done | bytes 262176 | tf_op jit(solution)/shard_map/all_to_all | solution.py:128
  140.2 5.5 attend_kernel.2
  170.8 24.0 %all-gather.6.cloned.1.call-done.refs_8_ = bf16[2048,2176]{1,0:T(8,128)(2,1)} async-done(((bf16[512,2176]{1,0:T(8,128)(2,1)}), bf16[2048,2176]{1,0:T(8,128)(2,1)}) %all-gather.6.cloned.1.call-update) | async-done | bytes 8912912 | tf_op jit(solution)/shard_map/all_gather | solution.py:138
  194.8 6.7 %ffn_kernel.2 = (bf16[256,2048]{1,0:T(8,128)(2,1)}, f32[256,1408]{1,0:T(8,128)}, bf16[256,768]{1,0:T(8,128)(2,1)}, bf16[128,2048]{1,0:T(8,128)(2,1)S(1)}, f32[128,2048]{1,0:T(8,128)S(1)}) custom-call(bf16[32,2048]{1,0:T(8,128)(2,1)} %copy-done.29, bf16[32,2048]{1,0:T(8,128)(2,1)} %copy-done.75, bf16[32,2048]{1,0:T(8,128)(2,1)} %copy-done.71, ...), custom_call_target="tpu_custom_call" | custom-call | flops 1 | bytes 1 | tf_op jit(solution)/shard_map/ffn_kernel/pallas_call | solution.py:66
  231.4 13.7 %all_to_all.20 = bf16[8,128,128]{2,1,0:T(8,128)(2,1)S(1)} all-to-all(bf16[8,128,128]{2,1,0:T(8,128)(2,1)S(1)} %broadcast_in_dim.61), channel_id=1, replica_groups=mesh['section'=2,'x'=4,'ylo'=2,'core'=2,'tp'=4] {'x','ylo'}, dimensions={0} | all-to-all | bytes 524288 | tf_op jit(solution)/shard_map/all_to_all | solution.py:128
  248.1 5.3 attend_kernel.3
  282.2 5.7 all-gather.8.cloned.1.call-done.refs_8_
  287.9 6.9 %ffn_kernel.3 = (bf16[256,2048]{1,0:T(8,128)(2,1)}, f32[256,1408]{1,0:T(8,128)}, bf16[256,768]{1,0:T(8,128)(2,1)}, bf16[128,2048]{1,0:T(8,128)(2,1)}, f32[128,2048]{1,0:T(8,128)S(1)}) custom-call(bf16[32,2048]{1,0:T(8,128)(2,1)} %copy-done.28, bf16[32,2048]{1,0:T(8,128)(2,1)} %collective-permute-done.47.refs_1_, bf16[32,2048]{1,0:T(8,128)(2,1)} %copy-done.63, ...), custom_call_target="tpu_custom_call" | custom-call | flops 1 | bytes 1 | tf_op jit(solution)/shard_map/ffn_kernel/pallas_call | solution.py:66
  295.8 6.8 %ffn_back_kernel.2 = (bf16[256,2048]{1,0:T(8,128)(2,1)}, bf16[256,1408]{1,0:T(8,128)(2,1)}, bf16[128,2048]{1,0:T(8,128)(2,1)S(1)}, f32[128,2048]{1,0:T(8,128)S(1)}) custom-call(bf16[32,2048]{1,0:T(8,128)(2,1)} %copy-done.6, bf16[32,2048]{1,0:T(8,128)(2,1)} %collective-permute-done.54.refs_1_, bf16[32,2048]{1,0:T(8,128)(2,1)} %collective-permute-done.55.refs_2_, ...), custom_call_target="tpu_custom_call" | custom-call | flops 1 | bytes 1 | tf_op jit(solution)/shard_map/ffn_back_kernel/pallas_call | solution.py:66
  304.5 5.9 ffn_product_kernel.2
  338.4 10.6 %attend_back_kernel.2 = (bf16[256,2048]{1,0:T(8,128)(2,1)}, bf16[256,256]{1,0:T(8,128)(2,1)S(1)}, f32[1024,128]{1,0:T(8,128)S(1)}, bf16[1024,128]{1,0:T(8,128)(2,1)S(1)}) custom-call(s32[5]{0:T(128)S(1)} %stack.41.place, bf16[32,2048]{1,0:T(8,128)(2,1)} %copy-done.31, bf16[32,2048]{1,0:T(8,128)(2,1)} %copy-done.76, bf16[32,2048]{1,0:T(8,128)(2,1)} %copy-done.72, ...), custom_call_target="tpu_custom_call" | custom-call | flops 1 | bytes 1 | tf_op jit(solution)/shard_map/attend_back_kernel/pallas_call | solution.py:66
  350.7 14.1 %all_to_all.21.refs_3_ = bf16[8,128,128]{2,1,0:T(8,128)(2,1)S(1)} all-to-all(bf16[8,128,128]{2,1,0:T(8,128)(2,1)S(1)} %bitcast.61), channel_id=1, replica_groups=mesh['section'=2,'x'=4,'ylo'=2,'core'=2,'tp'=4] {'x','ylo'}, dimensions={0} | all-to-all | bytes 524288 | tf_op jit(solution)/shard_map/all_to_all | solution.py:888
  395.8 6.9 %ffn_back_kernel.3 = (bf16[256,2048]{1,0:T(8,128)(2,1)}, bf16[256,1408]{1,0:T(8,128)(2,1)}, bf16[128,2048]{1,0:T(8,128)(2,1)S(1)}, f32[128,2048]{1,0:T(8,128)S(1)}) custom-call(bf16[32,2048]{1,0:T(8,128)(2,1)} %copy-done.21, bf16[32,2048]{1,0:T(8,128)(2,1)} %copy-done.81, bf16[32,2048]{1,0:T(8,128)(2,1)} %copy-done.77, bf16[32,2048]{1,0:T(8,128)(2,1)} %copy-done.73, ...), custom_call_target="tpu_custom_call" | custom-call | flops 1 | bytes 1 | tf_op jit(solution)/shard_map/ffn_back_kernel/pallas_call | solution.py:66
  404.4 5.9 ffn_product_kernel.3
  440.2 10.7 %attend_back_kernel.3 = (bf16[256,2048]{1,0:T(8,128)(2,1)}, bf16[256,256]{1,0:T(8,128)(2,1)S(1)}, f32[1024,128]{1,0:T(8,128)S(1)}, bf16[1024,128]{1,0:T(8,128)(2,1)S(1)}) custom-call(s32[5]{0:T(128)S(1)} %stack.41.place, bf16[32,2048]{1,0:T(8,128)(2,1)} %copy-done.30, bf16[32,2048]{1,0:T(8,128)(2,1)} %copy-done.74, bf16[32,2048]{1,0:T(8,128)(2,1)} %copy-done.70, ...), custom_call_target="tpu_custom_call" | custom-call | flops 1 | bytes 1 | tf_op jit(solution)/shard_map/attend_back_kernel/pallas_call | solution.py:66
  452.6 12.4 %all_to_all.22.refs_6_ = bf16[8,128,128]{2,1,0:T(8,128)(2,1)S(1)} all-to-all(bf16[8,128,128]{2,1,0:T(8,128)(2,1)S(1)} %bitcast.62), channel_id=1, replica_groups=mesh['section'=2,'x'=4,'ylo'=2,'core'=2,'tp'=4] {'x','ylo'}, dimensions={0} | all-to-all | bytes 524288 | tf_op jit(solution)/shard_map/all_to_all | solution.py:888
  509.1 52.8 %reduce-scatter.6.cloned.1.call-done.r_ref = bf16[512,1536]{1,0:T(8,128)(2,1)} async-done(((bf16[2048,1536]{1,0:T(8,128)(2,1)}), bf16[512,1536]{1,0:T(8,128)(2,1)}) %reduce-scatter.6.cloned.1.call-update) | async-done | bytes 1572880 | tf_op jit(solution)/shard_map/reduce_scatter | solution.py:142
  580.8 8.8 %collective-permute-done.111.refs_2_ = bf16[256,768]{1,0:T(8,128)(2,1)S(1)} collective-permute-done((bf16[256,768]{1,0:T(8,128)(2,1)S(1)}, bf16[256,768]{1,0:T(8,128)(2,1)S(1)}, u32[]{:S(2)}, u32[]{:S(2)}) %collective-permute-start.111) | collective-permute-done | bytes 393248 | tf_op jit(solution)/shard_map/ppermute | solution.py:104
  (537 shorter events, 329.6 us)
Async XLA Ops:
  7.2 94.6 %all-gather.4.cloned.1.call-start = ((), (), s32[]{:S(2)}) async-start(), calls=%async_computation.7 | async-start | bytes 3481600 | tf_op jit(solution)/shard_map/all_gather | solution.py:138
  22.2 16.1 %collective-permute-start.10 = (bf16[272,640]{1,0:T(8,128)(2,1)S(1)}, bf16[272,640]{1,0:T(8,128)(2,1)S(1)}, u32[]{:S(2)}, u32[]{:S(2)}) collective-permute-start(bf16[272,640]{1,0:T(8,128)(2,1)S(1)} %copy-done.47), channel_id=1, source_target_pairs={{0,72},{72,0},{8,64},{64,8},{1,73},{73,1},{9,65},{65,9},{2,74},{74... | collective-permute-start | bytes 1044488 | tf_op jit(solution)/shard_map/ppermute | solution.py:104
  23.0 15.3 %collective-permute-start.9 = (bf16[272,640]{1,0:T(8,128)(2,1)S(1)}, bf16[272,640]{1,0:T(8,128)(2,1)S(1)}, u32[]{:S(2)}, u32[]{:S(2)}) collective-permute-start(bf16[272,640]{1,0:T(8,128)(2,1)S(1)} %copy-done.47), channel_id=1, source_target_pairs={{0,8},{8,0},{1,9},{9,1},{2,10},{10,2},{3,11},{11,3},{4,12},{12,4},... | collective-permute-start | bytes 1044488 | tf_op jit(solution)/shard_map/ppermute | solution.py:96
  42.3 152.6 %all-gather.6.cloned.1.call-start = ((), (), s32[]{:S(2)}) async-start(), calls=%async_computation.8 | async-start | bytes 11141120 | tf_op jit(solution)/shard_map/all_gather | solution.py:138
  42.3 27.5 %collective-permute-start.28 = (bf16[256,2176]{1,0:T(8,128)(2,1)}, bf16[256,2176]{1,0:T(8,128)(2,1)S(1)}, u32[]{:S(2)}, u32[]{:S(2)}) collective-permute-start(bf16[256,2176]{1,0:T(8,128)(2,1)} %chip_rows_kernel.1.own_ref), channel_id=1, source_target_pairs={{0,72},{72,0},{8,64},{64,8},{1,73},{73,1},{9,65},{65,9},{2,74},{74... | collective-permute-start | bytes 3342344 | tf_op jit(solution)/shard_map/ppermute | solution.py:104
  45.2 25.6 %collective-permute-start.27 = (bf16[256,2176]{1,0:T(8,128)(2,1)}, bf16[256,2176]{1,0:T(8,128)(2,1)S(1)}, u32[]{:S(2)}, u32[]{:S(2)}) collective-permute-start(bf16[256,2176]{1,0:T(8,128)(2,1)} %chip_rows_kernel.1.own_ref), channel_id=1, source_target_pairs={{0,8},{8,0},{1,9},{9,1},{2,10},{10,2},{3,11},{11,3},{4,12},{12,4},... | collective-permute-start | bytes 3342344 | tf_op jit(solution)/shard_map/ppermute | solution.py:96
  45.2 45.2 %collective-permute-start.14 = (bf16[544,640]{1,0:T(8,128)(2,1)}, bf16[544,640]{1,0:T(8,128)(2,1)S(1)}, u32[]{:S(2)}, u32[]{:S(2)}) collective-permute-start(bf16[544,640]{1,0:T(8,128)(2,1)} %get-tuple-element.161.refs_8_.refs_0_), channel_id=1, source_target_pairs={{48,0},{0,16},{16,32},{32,48},{49,1},{1,17},{17,33},{33,49},{50,2}... | collective-permute-start | bytes 2088968 | tf_op jit(solution)/shard_map/ppermute | solution.py:88
  46.4 52.5 %collective-permute-start.13 = (bf16[544,640]{1,0:T(8,128)(2,1)}, bf16[544,640]{1,0:T(8,128)(2,1)S(1)}, u32[]{:S(2)}, u32[]{:S(2)}) collective-permute-start(bf16[544,640]{1,0:T(8,128)(2,1)} %get-tuple-element.161.refs_8_.refs_0_), channel_id=1, source_target_pairs={{32,0},{48,16},{0,32},{16,48},{33,1},{49,17},{1,33},{17,49},{34,2}... | collective-permute-start | bytes 2088968 | tf_op jit(solution)/shard_map/ppermute | solution.py:88
  48.9 50.0 %collective-permute-start.12 = (bf16[544,640]{1,0:T(8,128)(2,1)}, bf16[544,640]{1,0:T(8,128)(2,1)S(1)}, u32[]{:S(2)}, u32[]{:S(2)}) collective-permute-start(bf16[544,640]{1,0:T(8,128)(2,1)} %get-tuple-element.161.refs_8_.refs_0_), channel_id=1, source_target_pairs={{16,0},{32,16},{48,32},{0,48},{17,1},{33,17},{49,33},{1,49},{18,2}... | collective-permute-start | bytes 2088968 | tf_op jit(solution)/shard_map/ppermute | solution.py:88
  70.9 14.0 %collective-permute-start.30 = (bf16[128,2176]{1,0:T(8,128)(2,1)S(1)}, bf16[128,2176]{1,0:T(8,128)(2,1)S(1)}, u32[]{:S(2)}, u32[]{:S(2)}) collective-permute-start(bf16[128,2176]{1,0:T(8,128)(2,1)S(1)} %slice.21), channel_id=1, source_target_pairs={{0,72},{72,0},{8,64},{64,8},{1,73},{73,1},{9,65},{65,9},{2,74},{74... | collective-permute-start | bytes 1671176 | tf_op jit(solution)/shard_map/ppermute | solution.py:104
  123.1 14.5 %all-to-all-start = ((bf16[8,128,128]{2,1,0:T(8,128)(2,1)}), bf16[8,128,128]{2,1,0:T(8,128)(2,1)S(1)}, u32[]{:S(2)}, u32[]{:S(2)}) async-start(bf16[8,128,128]{2,1,0:T(8,128)(2,1)} %broadcast_in_dim.58), calls=%async_computation | async-start | bytes 524288 | tf_op jit(solution)/shard_map/all_to_all | solution.py:128
  127.9 159.9 %all-gather.8.cloned.1.call-start = ((), (), s32[]{:S(2)}) async-start(), calls=%async_computation.9 | async-start | bytes 11141120 | tf_op jit(solution)/shard_map/all_gather | solution.py:138
  157.3 269.0 %reduce-scatter.4.cloned.1.call-start = ((), (), s32[]{:S(2)}) async-start(), calls=%async_computation.10 | async-start | bytes 11141120 | tf_op jit(solution)/shard_map/reduce_scatter | solution.py:142
  277.7 18.1 %collective-permute-start.57 = (bf16[32,2048]{1,0:T(8,128)(2,1)S(1)}, bf16[32,2048]{1,0:T(8,128)(2,1)}, u32[]{:S(2)}, u32[]{:S(2)}) collective-permute-start(bf16[32,2048]{1,0:T(8,128)(2,1)S(1)} %dynamic-slice_bitcast_fusion.refs_0_.after_ref), channel_id=1, source_target_pairs={{0,4},{4,0},{1,5},{5,1},{2,6},{6,2},{3,7},{7,3},{8,12},{12,8},{9,1... | collective-permute-start | bytes 393224 | tf_op jit(solution)/shard_map/ppermute | solution.py:92
  280.3 15.5 %collective-permute-start.60 = (bf16[32,2048]{1,0:T(8,128)(2,1)}, bf16[32,2048]{1,0:T(8,128)(2,1)}, u32[]{:S(2)}, u32[]{:S(2)}) collective-permute-start(bf16[32,2048]{1,0:T(8,128)(2,1)} %collective-permute-done.56.refs_3_), channel_id=1, source_target_pairs={{0,4},{4,0},{1,5},{5,1},{2,6},{6,2},{3,7},{7,3},{8,12},{12,8},{9,1... | collective-permute-start | bytes 393224 | tf_op jit(solution)/shard_map/ppermute | solution.py:92
  280.4 15.4 %collective-permute-start.59 = (bf16[32,2048]{1,0:T(8,128)(2,1)}, bf16[32,2048]{1,0:T(8,128)(2,1)}, u32[]{:S(2)}, u32[]{:S(2)}) collective-permute-start(bf16[32,2048]{1,0:T(8,128)(2,1)} %collective-permute-done.55.refs_2_), channel_id=1, source_target_pairs={{0,4},{4,0},{1,5},{5,1},{2,6},{6,2},{3,7},{7,3},{8,12},{12,8},{9,1... | collective-permute-start | bytes 393224 | tf_op jit(solution)/shard_map/ppermute | solution.py:92
  281.7 14.1 %collective-permute-start.58 = (bf16[32,2048]{1,0:T(8,128)(2,1)}, bf16[32,2048]{1,0:T(8,128)(2,1)}, u32[]{:S(2)}, u32[]{:S(2)}) collective-permute-start(bf16[32,2048]{1,0:T(8,128)(2,1)} %collective-permute-done.54.refs_1_), channel_id=1, source_target_pairs={{0,4},{4,0},{1,5},{5,1},{2,6},{6,2},{3,7},{7,3},{8,12},{12,8},{9,1... | collective-permute-start | bytes 393224 | tf_op jit(solution)/shard_map/ppermute | solution.py:92
  310.4 190.4 %reduce-scatter.8.cloned.1.call-start = ((), (), s32[]{:S(2)}) async-start(), calls=%async_computation.12 | async-start | bytes 11141120 | tf_op jit(solution)/shard_map/reduce_scatter | solution.py:142
  410.4 151.5 %reduce-scatter.6.cloned.1.call-start = ((), (), s32[]{:S(2)}) async-start(), calls=%async_computation.11 | async-start | bytes 7864320 | tf_op jit(solution)/shard_map/reduce_scatter | solution.py:142
  505.5 59.1 %collective-permute-start.106 = (bf16[256,2176]{1,0:T(8,128)(2,1)}, bf16[256,2176]{1,0:T(8,128)(2,1)S(1)}, u32[]{:S(2)}, u32[]{:S(2)}) collective-permute-start(bf16[256,2176]{1,0:T(8,128)(2,1)} %get-tuple-element.279), channel_id=1, source_target_pairs={{0,8},{8,0},{1,9},{9,1},{2,10},{10,2},{3,11},{11,3},{4,12},{12,4},... | collective-permute-start | bytes 3342344 | tf_op jit(solution)/shard_map/ppermute | solution.py:96
  506.7 57.9 %collective-permute-start.107 = (bf16[256,2176]{1,0:T(8,128)(2,1)}, bf16[256,2176]{1,0:T(8,128)(2,1)S(1)}, u32[]{:S(2)}, u32[]{:S(2)}) collective-permute-start(bf16[256,2176]{1,0:T(8,128)(2,1)} %get-tuple-element.280), channel_id=1, source_target_pairs={{0,72},{72,0},{8,64},{64,8},{1,73},{73,1},{9,65},{65,9},{2,74},{74... | collective-permute-start | bytes 3342344 | tf_op jit(solution)/shard_map/ppermute | solution.py:104
  508.2 56.4 %collective-permute-start.108 = (bf16[256,2176]{1,0:T(8,128)(2,1)}, bf16[256,2176]{1,0:T(8,128)(2,1)}, u32[]{:S(2)}, u32[]{:S(2)}) collective-permute-start(bf16[256,2176]{1,0:T(8,128)(2,1)} %get-tuple-element.281), channel_id=1, source_target_pairs={{0,64},{64,0},{1,65},{65,1},{2,66},{66,2},{3,67},{67,3},{4,68},{68... | collective-permute-start | bytes 3342344 | tf_op jit(solution)/shard_map/ppermute | solution.py:100
  571.3 18.3 %collective-permute-start.111 = (bf16[256,768]{1,0:T(8,128)(2,1)S(1)}, bf16[256,768]{1,0:T(8,128)(2,1)S(1)}, u32[]{:S(2)}, u32[]{:S(2)}) collective-permute-start(bf16[256,768]{1,0:T(8,128)(2,1)S(1)} %copy-done.108), channel_id=1, source_target_pairs={{0,72},{72,0},{8,64},{64,8},{1,73},{73,1},{9,65},{65,9},{2,74},{74... | collective-permute-start | bytes 1179656 | tf_op jit(solution)/shard_map/ppermute | solution.py:104
  573.2 18.3 %collective-permute-start.112 = (bf16[256,768]{1,0:T(8,128)(2,1)S(1)}, bf16[256,768]{1,0:T(8,128)(2,1)S(1)}, u32[]{:S(2)}, u32[]{:S(2)}) collective-permute-start(bf16[256,768]{1,0:T(8,128)(2,1)S(1)} %copy-done.107), channel_id=1, source_target_pairs={{0,64},{64,0},{1,65},{65,1},{2,66},{66,2},{3,67},{67,3},{4,68},{68... | collective-permute-start | bytes 1179656 | tf_op jit(solution)/shard_map/ppermute | solution.py:100
  (210 other events, 1506.4 us)
Sparse Core Ops, SparseCore 0:
  42.4 59.3 all-gather.3
  103.5 91.3 all-gather.5
  196.5 91.3 all-gather.7
  310.5 88.5 reduce-scatter.3
  410.5 85.3 reduce-scatter.7
  498.2 63.6 reduce-scatter.5

commit v7 on v5

--- a/solution.py
+++ b/solution.py
@@ -901,7 +901,7 @@
             [rows_f32, rows_low, held((1, d), F32)],
             [*reduce_rows(send, mine), dmid, x, gain_a],
         )
-        return dx, after(dx_low, g_attn), g_attn, g_ffn, dqkv
+        return dx, dx_low, g_attn, g_ffn, dqkv
 
     x0 = lax.dynamic_index_in_dim(block_input, section, 0, keepdims=False)
     dy1 = lax.dynamic_index_in_dim(out_grad, section, 0, keepdims=False)

time: 622 us -> 622 us (level)
  blocking collectives: 40.3 us -> 27.9 us
  waiting for transfers between devices: 231 us -> 241 us
    all_to_all x2 -> x1, blocking collectives: 26.5 us -> 14.1 us  [backward(): lax.all_to_all(dkv.reshape(8, group // 2, 2 * HD), ('x', 'ylo'), 0, 0, ti...]
  transfers between devices with their start and end apart: 124 -> 125, of which waited for: 68 -> 69; matrix products, arithmetic and copies ran while one was open for 1% -> 1% of each run, Pallas kernels for 19% -> 19%
where the time goes in v7:
time: 622 us; the launch traced here: 613 us
  waiting for transfers between devices  241 us (39%)
  starting transfers between devices  161 us (26%)
  Pallas kernels  136 us (22%)
  local copies, waits for them, and re-layouts  28.5 us (5%)
  blocking collectives  27.9 us (4%)
  between operations  15.4 us (2%)
    pallas_call x46, Pallas kernels, call(): pl.pallas_call(kernel, out_shape=tuple(outs), in_specs=specs, out_specs=t...  136 us
    ppermute x51, starting transfers between devices, from_z(): return lax.ppermute(rows, 'tp', [((i + by) % 4, i) for i in range(4)])  73.8 us
    ppermute x48, starting transfers between devices, swap_core(): return lax.ppermute(v, 'core', [(0, 1), (1, 0)])  53 us
    reduce_scatter x3, waiting for transfers between devices, reduce_x(): return lax.psum_scatter(grad, 'x', scatter_dimension=0, tiled=True)  52.2 us
    ppermute x51, waiting for transfers between devices, from_z(): return lax.ppermute(rows, 'tp', [((i + by) % 4, i) for i in range(4)])  45.7 us
    all_gather x3, waiting for transfers between devices, gather_x(): return lax.all_gather(block, 'x', axis=0, tiled=True)  32.5 us
    ppermute x5, waiting for transfers between devices, swap_across(): return lax.ppermute(v, ('section', 'ylo'), [(0, 3), (3, 0), (1, 2), (2, 1)])  31.5 us
    unnamed x216, local copies, waits for them, and re-layouts  25.5 us
  transfers between devices with their start and end apart: 125, of which 69 were waited for; matrix products, arithmetic and copies ran while one was open for 1% of the time, Pallas kernels for 19%

profile of v7, /device:TPU:1, one launch (start us, length us, event | category | flops | bytes accessed | tf_op | source)
XLA Modules:
  0.0 612.6 jit_solution(15555422987638993604)
XLA Ops:
  23.0 7.4 %collective-permute-done.11.refs_0_ = bf16[272,640]{1,0:T(8,128)(2,1)S(1)} collective-permute-done((bf16[272,640]{1,0:T(8,128)(2,1)S(1)}, bf16[272,640]{1,0:T(8,128)(2,1)S(1)}, u32[]{:S(2)}, u32[]{:S(2)}) %collective-permute-start.11) | collective-permute-done | bytes 348192 | tf_op jit(solution)/shard_map/ppermute | solution.py:100
  30.4 7.9 %collective-permute-done.10.far_ref = bf16[272,640]{1,0:T(8,128)(2,1)S(1)} collective-permute-done((bf16[272,640]{1,0:T(8,128)(2,1)S(1)}, bf16[272,640]{1,0:T(8,128)(2,1)S(1)}, u32[]{:S(2)}, u32[]{:S(2)}) %collective-permute-start.10) | collective-permute-done | bytes 348192 | tf_op jit(solution)/shard_map/ppermute | solution.py:104
  50.0 19.8 %collective-permute-done.28.far_ref = bf16[256,2176]{1,0:T(8,128)(2,1)S(1)} collective-permute-done((bf16[256,2176]{1,0:T(8,128)(2,1)}, bf16[256,2176]{1,0:T(8,128)(2,1)S(1)}, u32[]{:S(2)}, u32[]{:S(2)}) %collective-permute-start.28) | collective-permute-done | bytes 1114144 | tf_op jit(solution)/shard_map/ppermute | solution.py:104
  72.7 10.4 %collective-permute-done.29.refs_0_ = bf16[128,2176]{1,0:T(8,128)(2,1)S(1)} collective-permute-done((bf16[128,2176]{1,0:T(8,128)(2,1)S(1)}, bf16[128,2176]{1,0:T(8,128)(2,1)S(1)}, u32[]{:S(2)}, u32[]{:S(2)}) %collective-permute-start.29) | collective-permute-done | bytes 557088 | tf_op jit(solution)/shard_map/ppermute | solution.py:96
  90.4 8.5 %collective-permute-done.13.refs_10_.refs_2_ = bf16[544,640]{1,0:T(8,128)(2,1)S(1)} collective-permute-done((bf16[544,640]{1,0:T(8,128)(2,1)}, bf16[544,640]{1,0:T(8,128)(2,1)S(1)}, u32[]{:S(2)}, u32[]{:S(2)}) %collective-permute-start.13) | collective-permute-done | bytes 696352 | tf_op jit(solution)/shard_map/ppermute | solution.py:88
  123.1 4.8 all-to-all-start
  128.4 9.3 %all-to-all-done = bf16[8,128,128]{2,1,0:T(8,128)(2,1)S(1)} async-done(((bf16[8,128,128]{2,1,0:T(8,128)(2,1)}), bf16[8,128,128]{2,1,0:T(8,128)(2,1)S(1)}, u32[]{:S(2)}, u32[]{:S(2)}) %all-to-all-start) | async-done | bytes 262176 | tf_op jit(solution)/shard_map/all_to_all | solution.py:128
  140.3 5.5 attend_kernel.2
  170.9 24.0 %all-gather.6.cloned.1.call-done.refs_8_ = bf16[2048,2176]{1,0:T(8,128)(2,1)} async-done(((bf16[512,2176]{1,0:T(8,128)(2,1)}), bf16[2048,2176]{1,0:T(8,128)(2,1)}) %all-gather.6.cloned.1.call-update) | async-done | bytes 8912912 | tf_op jit(solution)/shard_map/all_gather | solution.py:138
  194.9 6.8 %ffn_kernel.2 = (bf16[256,2048]{1,0:T(8,128)(2,1)}, f32[256,1408]{1,0:T(8,128)}, bf16[256,768]{1,0:T(8,128)(2,1)}, bf16[128,2048]{1,0:T(8,128)(2,1)S(1)}, f32[128,2048]{1,0:T(8,128)S(1)}) custom-call(bf16[32,2048]{1,0:T(8,128)(2,1)} %copy-done.29, bf16[32,2048]{1,0:T(8,128)(2,1)} %copy-done.75, bf16[32,2048]{1,0:T(8,128)(2,1)} %copy-done.71, ...), custom_call_target="tpu_custom_call" | custom-call | flops 1 | bytes 1 | tf_op jit(solution)/shard_map/ffn_kernel/pallas_call | solution.py:66
  231.5 13.7 %all_to_all.20 = bf16[8,128,128]{2,1,0:T(8,128)(2,1)S(1)} all-to-all(bf16[8,128,128]{2,1,0:T(8,128)(2,1)S(1)} %broadcast_in_dim.61), channel_id=1, replica_groups=mesh['section'=2,'x'=4,'ylo'=2,'core'=2,'tp'=4] {'x','ylo'}, dimensions={0} | all-to-all | bytes 524288 | tf_op jit(solution)/shard_map/all_to_all | solution.py:128
  248.2 5.3 attend_kernel.3
  282.2 5.6 all-gather.8.cloned.1.call-done.refs_8_
  287.9 6.9 %ffn_kernel.3 = (bf16[256,2048]{1,0:T(8,128)(2,1)}, f32[256,1408]{1,0:T(8,128)}, bf16[256,768]{1,0:T(8,128)(2,1)}, bf16[128,2048]{1,0:T(8,128)(2,1)}, f32[128,2048]{1,0:T(8,128)S(1)}) custom-call(bf16[32,2048]{1,0:T(8,128)(2,1)} %copy-done.28, bf16[32,2048]{1,0:T(8,128)(2,1)} %collective-permute-done.47.refs_1_, bf16[32,2048]{1,0:T(8,128)(2,1)} %copy-done.63, ...), custom_call_target="tpu_custom_call" | custom-call | flops 1 | bytes 1 | tf_op jit(solution)/shard_map/ffn_kernel/pallas_call | solution.py:66
  295.8 6.8 %ffn_back_kernel.2 = (bf16[256,2048]{1,0:T(8,128)(2,1)}, bf16[256,1408]{1,0:T(8,128)(2,1)}, bf16[128,2048]{1,0:T(8,128)(2,1)S(1)}, f32[128,2048]{1,0:T(8,128)S(1)}) custom-call(bf16[32,2048]{1,0:T(8,128)(2,1)} %copy-done.6, bf16[32,2048]{1,0:T(8,128)(2,1)} %collective-permute-done.54.refs_1_, bf16[32,2048]{1,0:T(8,128)(2,1)} %collective-permute-done.55.refs_2_, ...), custom_call_target="tpu_custom_call" | custom-call | flops 1 | bytes 1 | tf_op jit(solution)/shard_map/ffn_back_kernel/pallas_call | solution.py:66
  304.5 5.9 ffn_product_kernel.2
  338.4 10.6 %attend_back_kernel.2 = (bf16[256,2048]{1,0:T(8,128)(2,1)}, bf16[256,256]{1,0:T(8,128)(2,1)S(1)}, f32[1024,128]{1,0:T(8,128)S(1)}, bf16[1024,128]{1,0:T(8,128)(2,1)S(1)}) custom-call(s32[5]{0:T(128)S(1)} %stack.41.place, bf16[32,2048]{1,0:T(8,128)(2,1)} %copy-done.31, bf16[32,2048]{1,0:T(8,128)(2,1)} %copy-done.76, bf16[32,2048]{1,0:T(8,128)(2,1)} %copy-done.72, ...), custom_call_target="tpu_custom_call" | custom-call | flops 1 | bytes 1 | tf_op jit(solution)/shard_map/attend_back_kernel/pallas_call | solution.py:66
  350.6 14.1 %all_to_all.21.refs_3_ = bf16[8,128,128]{2,1,0:T(8,128)(2,1)S(1)} all-to-all(bf16[8,128,128]{2,1,0:T(8,128)(2,1)S(1)} %bitcast.61), channel_id=1, replica_groups=mesh['section'=2,'x'=4,'ylo'=2,'core'=2,'tp'=4] {'x','ylo'}, dimensions={0} | all-to-all | bytes 524288 | tf_op jit(solution)/shard_map/all_to_all | solution.py:888
  395.8 6.9 %ffn_back_kernel.3 = (bf16[256,2048]{1,0:T(8,128)(2,1)}, bf16[256,1408]{1,0:T(8,128)(2,1)}, bf16[128,2048]{1,0:T(8,128)(2,1)S(1)}, f32[128,2048]{1,0:T(8,128)S(1)}) custom-call(bf16[32,2048]{1,0:T(8,128)(2,1)} %copy-done.21, bf16[32,2048]{1,0:T(8,128)(2,1)} %copy-done.81, bf16[32,2048]{1,0:T(8,128)(2,1)} %copy-done.77, bf16[32,2048]{1,0:T(8,128)(2,1)} %copy-done.73, ...), custom_call_target="tpu_custom_call" | custom-call | flops 1 | bytes 1 | tf_op jit(solution)/shard_map/ffn_back_kernel/pallas_call | solution.py:66
  404.5 5.9 ffn_product_kernel.3
  440.3 10.7 %attend_back_kernel.3 = (bf16[256,2048]{1,0:T(8,128)(2,1)}, bf16[256,256]{1,0:T(8,128)(2,1)S(1)}, f32[1024,128]{1,0:T(8,128)S(1)}, bf16[1024,128]{1,0:T(8,128)(2,1)S(1)}) custom-call(s32[5]{0:T(128)S(1)} %stack.41.place, bf16[32,2048]{1,0:T(8,128)(2,1)} %copy-done.30, bf16[32,2048]{1,0:T(8,128)(2,1)} %copy-done.74, bf16[32,2048]{1,0:T(8,128)(2,1)} %copy-done.70, ...), custom_call_target="tpu_custom_call" | custom-call | flops 1 | bytes 1 | tf_op jit(solution)/shard_map/attend_back_kernel/pallas_call | solution.py:66
  461.2 5.4 all-to-all-done.3.refs_6_
  509.9 52.2 %reduce-scatter.6.cloned.1.call-done.r_ref = bf16[512,1536]{1,0:T(8,128)(2,1)} async-done(((bf16[2048,1536]{1,0:T(8,128)(2,1)}), bf16[512,1536]{1,0:T(8,128)(2,1)}) %reduce-scatter.6.cloned.1.call-update) | async-done | bytes 1572880 | tf_op jit(solution)/shard_map/reduce_scatter | solution.py:142
  577.1 8.5 %collective-permute-done.108.refs_3_ = bf16[256,768]{1,0:T(8,128)(2,1)S(1)} collective-permute-done((bf16[256,768]{1,0:T(8,128)(2,1)}, bf16[256,768]{1,0:T(8,128)(2,1)S(1)}, u32[]{:S(2)}, u32[]{:S(2)}) %collective-permute-start.108) | collective-permute-done | bytes 393248 | tf_op jit(solution)/shard_map/ppermute | solution.py:100
  (532 shorter events, 334.1 us)
Async XLA Ops:
  7.2 94.6 %all-gather.4.cloned.1.call-start = ((), (), s32[]{:S(2)}) async-start(), calls=%async_computation.7 | async-start | bytes 3481600 | tf_op jit(solution)/shard_map/all_gather | solution.py:138
  22.2 16.1 %collective-permute-start.10 = (bf16[272,640]{1,0:T(8,128)(2,1)S(1)}, bf16[272,640]{1,0:T(8,128)(2,1)S(1)}, u32[]{:S(2)}, u32[]{:S(2)}) collective-permute-start(bf16[272,640]{1,0:T(8,128)(2,1)S(1)} %copy-done.47), channel_id=1, source_target_pairs={{0,72},{72,0},{8,64},{64,8},{1,73},{73,1},{9,65},{65,9},{2,74},{74... | collective-permute-start | bytes 1044488 | tf_op jit(solution)/shard_map/ppermute | solution.py:104
  23.0 15.3 %collective-permute-start.9 = (bf16[272,640]{1,0:T(8,128)(2,1)S(1)}, bf16[272,640]{1,0:T(8,128)(2,1)S(1)}, u32[]{:S(2)}, u32[]{:S(2)}) collective-permute-start(bf16[272,640]{1,0:T(8,128)(2,1)S(1)} %copy-done.47), channel_id=1, source_target_pairs={{0,8},{8,0},{1,9},{9,1},{2,10},{10,2},{3,11},{11,3},{4,12},{12,4},... | collective-permute-start | bytes 1044488 | tf_op jit(solution)/shard_map/ppermute | solution.py:96
  42.3 152.6 %all-gather.6.cloned.1.call-start = ((), (), s32[]{:S(2)}) async-start(), calls=%async_computation.8 | async-start | bytes 11141120 | tf_op jit(solution)/shard_map/all_gather | solution.py:138
  42.3 27.5 %collective-permute-start.28 = (bf16[256,2176]{1,0:T(8,128)(2,1)}, bf16[256,2176]{1,0:T(8,128)(2,1)S(1)}, u32[]{:S(2)}, u32[]{:S(2)}) collective-permute-start(bf16[256,2176]{1,0:T(8,128)(2,1)} %chip_rows_kernel.1.own_ref), channel_id=1, source_target_pairs={{0,72},{72,0},{8,64},{64,8},{1,73},{73,1},{9,65},{65,9},{2,74},{74... | collective-permute-start | bytes 3342344 | tf_op jit(solution)/shard_map/ppermute | solution.py:104
  45.2 25.6 %collective-permute-start.27 = (bf16[256,2176]{1,0:T(8,128)(2,1)}, bf16[256,2176]{1,0:T(8,128)(2,1)S(1)}, u32[]{:S(2)}, u32[]{:S(2)}) collective-permute-start(bf16[256,2176]{1,0:T(8,128)(2,1)} %chip_rows_kernel.1.own_ref), channel_id=1, source_target_pairs={{0,8},{8,0},{1,9},{9,1},{2,10},{10,2},{3,11},{11,3},{4,12},{12,4},... | collective-permute-start | bytes 3342344 | tf_op jit(solution)/shard_map/ppermute | solution.py:96
  45.2 45.2 %collective-permute-start.14 = (bf16[544,640]{1,0:T(8,128)(2,1)}, bf16[544,640]{1,0:T(8,128)(2,1)S(1)}, u32[]{:S(2)}, u32[]{:S(2)}) collective-permute-start(bf16[544,640]{1,0:T(8,128)(2,1)} %get-tuple-element.159.refs_8_.refs_0_), channel_id=1, source_target_pairs={{48,0},{0,16},{16,32},{32,48},{49,1},{1,17},{17,33},{33,49},{50,2}... | collective-permute-start | bytes 2088968 | tf_op jit(solution)/shard_map/ppermute | solution.py:88
  46.4 52.5 %collective-permute-start.13 = (bf16[544,640]{1,0:T(8,128)(2,1)}, bf16[544,640]{1,0:T(8,128)(2,1)S(1)}, u32[]{:S(2)}, u32[]{:S(2)}) collective-permute-start(bf16[544,640]{1,0:T(8,128)(2,1)} %get-tuple-element.159.refs_8_.refs_0_), channel_id=1, source_target_pairs={{32,0},{48,16},{0,32},{16,48},{33,1},{49,17},{1,33},{17,49},{34,2}... | collective-permute-start | bytes 2088968 | tf_op jit(solution)/shard_map/ppermute | solution.py:88
  48.9 50.0 %collective-permute-start.12 = (bf16[544,640]{1,0:T(8,128)(2,1)}, bf16[544,640]{1,0:T(8,128)(2,1)S(1)}, u32[]{:S(2)}, u32[]{:S(2)}) collective-permute-start(bf16[544,640]{1,0:T(8,128)(2,1)} %get-tuple-element.159.refs_8_.refs_0_), channel_id=1, source_target_pairs={{16,0},{32,16},{48,32},{0,48},{17,1},{33,17},{49,33},{1,49},{18,2}... | collective-permute-start | bytes 2088968 | tf_op jit(solution)/shard_map/ppermute | solution.py:88
  70.9 14.0 %collective-permute-start.30 = (bf16[128,2176]{1,0:T(8,128)(2,1)S(1)}, bf16[128,2176]{1,0:T(8,128)(2,1)S(1)}, u32[]{:S(2)}, u32[]{:S(2)}) collective-permute-start(bf16[128,2176]{1,0:T(8,128)(2,1)S(1)} %slice.21), channel_id=1, source_target_pairs={{0,72},{72,0},{8,64},{64,8},{1,73},{73,1},{9,65},{65,9},{2,74},{74... | collective-permute-start | bytes 1671176 | tf_op jit(solution)/shard_map/ppermute | solution.py:104
  123.1 14.5 %all-to-all-start = ((bf16[8,128,128]{2,1,0:T(8,128)(2,1)}), bf16[8,128,128]{2,1,0:T(8,128)(2,1)S(1)}, u32[]{:S(2)}, u32[]{:S(2)}) async-start(bf16[8,128,128]{2,1,0:T(8,128)(2,1)} %broadcast_in_dim.58), calls=%async_computation | async-start | bytes 524288 | tf_op jit(solution)/shard_map/all_to_all | solution.py:128
  127.9 159.9 %all-gather.8.cloned.1.call-start = ((), (), s32[]{:S(2)}) async-start(), calls=%async_computation.9 | async-start | bytes 11141120 | tf_op jit(solution)/shard_map/all_gather | solution.py:138
  157.3 269.1 %reduce-scatter.4.cloned.1.call-start = ((), (), s32[]{:S(2)}) async-start(), calls=%async_computation.10 | async-start | bytes 11141120 | tf_op jit(solution)/shard_map/reduce_scatter | solution.py:142
  277.7 18.1 %collective-permute-start.57 = (bf16[32,2048]{1,0:T(8,128)(2,1)S(1)}, bf16[32,2048]{1,0:T(8,128)(2,1)}, u32[]{:S(2)}, u32[]{:S(2)}) collective-permute-start(bf16[32,2048]{1,0:T(8,128)(2,1)S(1)} %dynamic-slice_bitcast_fusion.refs_0_.after_ref), channel_id=1, source_target_pairs={{0,4},{4,0},{1,5},{5,1},{2,6},{6,2},{3,7},{7,3},{8,12},{12,8},{9,1... | collective-permute-start | bytes 393224 | tf_op jit(solution)/shard_map/ppermute | solution.py:92
  280.4 15.5 %collective-permute-start.60 = (bf16[32,2048]{1,0:T(8,128)(2,1)}, bf16[32,2048]{1,0:T(8,128)(2,1)}, u32[]{:S(2)}, u32[]{:S(2)}) collective-permute-start(bf16[32,2048]{1,0:T(8,128)(2,1)} %collective-permute-done.56.refs_3_), channel_id=1, source_target_pairs={{0,4},{4,0},{1,5},{5,1},{2,6},{6,2},{3,7},{7,3},{8,12},{12,8},{9,1... | collective-permute-start | bytes 393224 | tf_op jit(solution)/shard_map/ppermute | solution.py:92
  280.5 15.3 %collective-permute-start.59 = (bf16[32,2048]{1,0:T(8,128)(2,1)}, bf16[32,2048]{1,0:T(8,128)(2,1)}, u32[]{:S(2)}, u32[]{:S(2)}) collective-permute-start(bf16[32,2048]{1,0:T(8,128)(2,1)} %collective-permute-done.55.refs_2_), channel_id=1, source_target_pairs={{0,4},{4,0},{1,5},{5,1},{2,6},{6,2},{3,7},{7,3},{8,12},{12,8},{9,1... | collective-permute-start | bytes 393224 | tf_op jit(solution)/shard_map/ppermute | solution.py:92
  281.8 14.1 %collective-permute-start.58 = (bf16[32,2048]{1,0:T(8,128)(2,1)}, bf16[32,2048]{1,0:T(8,128)(2,1)}, u32[]{:S(2)}, u32[]{:S(2)}) collective-permute-start(bf16[32,2048]{1,0:T(8,128)(2,1)} %collective-permute-done.54.refs_1_), channel_id=1, source_target_pairs={{0,4},{4,0},{1,5},{5,1},{2,6},{6,2},{3,7},{7,3},{8,12},{12,8},{9,1... | collective-permute-start | bytes 393224 | tf_op jit(solution)/shard_map/ppermute | solution.py:92
  310.4 191.2 %reduce-scatter.8.cloned.1.call-start = ((), (), s32[]{:S(2)}) async-start(), calls=%async_computation.12 | async-start | bytes 11141120 | tf_op jit(solution)/shard_map/reduce_scatter | solution.py:142
  456.8 105.3 %reduce-scatter.6.cloned.1.call-start = ((), (), s32[]{:S(2)}) async-start(), calls=%async_computation.11 | async-start | bytes 7864320 | tf_op jit(solution)/shard_map/reduce_scatter | solution.py:142
  506.3 61.5 %collective-permute-start.113 = (bf16[256,2176]{1,0:T(8,128)(2,1)}, bf16[256,2176]{1,0:T(8,128)(2,1)S(1)}, u32[]{:S(2)}, u32[]{:S(2)}) collective-permute-start(bf16[256,2176]{1,0:T(8,128)(2,1)} %get-tuple-element.289), channel_id=1, source_target_pairs={{0,8},{8,0},{1,9},{9,1},{2,10},{10,2},{3,11},{11,3},{4,12},{12,4},... | collective-permute-start | bytes 3342344 | tf_op jit(solution)/shard_map/ppermute | solution.py:96
  507.5 61.1 %collective-permute-start.114 = (bf16[256,2176]{1,0:T(8,128)(2,1)}, bf16[256,2176]{1,0:T(8,128)(2,1)S(1)}, u32[]{:S(2)}, u32[]{:S(2)}) collective-permute-start(bf16[256,2176]{1,0:T(8,128)(2,1)} %get-tuple-element.290), channel_id=1, source_target_pairs={{0,72},{72,0},{8,64},{64,8},{1,73},{73,1},{9,65},{65,9},{2,74},{74... | collective-permute-start | bytes 3342344 | tf_op jit(solution)/shard_map/ppermute | solution.py:104
  509.0 59.5 %collective-permute-start.115 = (bf16[256,2176]{1,0:T(8,128)(2,1)}, bf16[256,2176]{1,0:T(8,128)(2,1)}, u32[]{:S(2)}, u32[]{:S(2)}) collective-permute-start(bf16[256,2176]{1,0:T(8,128)(2,1)} %get-tuple-element.291), channel_id=1, source_target_pairs={{0,64},{64,0},{1,65},{65,1},{2,66},{66,2},{3,67},{67,3},{4,68},{68... | collective-permute-start | bytes 3342344 | tf_op jit(solution)/shard_map/ppermute | solution.py:100
  567.8 17.9 %collective-permute-start.108 = (bf16[256,768]{1,0:T(8,128)(2,1)}, bf16[256,768]{1,0:T(8,128)(2,1)S(1)}, u32[]{:S(2)}, u32[]{:S(2)}) collective-permute-start(bf16[256,768]{1,0:T(8,128)(2,1)} %get-tuple-element.275), channel_id=1, source_target_pairs={{0,64},{64,0},{1,65},{65,1},{2,66},{66,2},{3,67},{67,3},{4,68},{68... | collective-permute-start | bytes 1179656 | tf_op jit(solution)/shard_map/ppermute | solution.py:100
  573.1 26.7 %collective-permute-start.116 = (bf16[128,2176]{1,0:T(8,128)(2,1)S(1)}, bf16[128,2176]{1,0:T(8,128)(2,1)S(1)}, u32[]{:S(2)}, u32[]{:S(2)}) collective-permute-start(bf16[128,2176]{1,0:T(8,128)(2,1)S(1)} %get-tuple-element.293), channel_id=1, source_target_pairs={{0,4},{4,0},{1,5},{5,1},{2,6},{6,2},{3,7},{7,3},{8,12},{12,8},{9,1... | collective-permute-start | bytes 1671176 | tf_op jit(solution)/shard_map/ppermute | solution.py:92
  (208 other events, 1525.6 us)
Sparse Core Ops, SparseCore 0:
  42.4 59.3 all-gather.3
  103.5 91.3 all-gather.5
  196.5 91.3 all-gather.7
  310.5 88.5 reduce-scatter.3
  410.6 85.5 reduce-scatter.7
  498.4 63.6 reduce-scatter.5
